TPU v7x, 256 devices: a whole 4x4x8 slice. The times are simulated.
256 devices in a mesh: traj: 8 (over y, core), feat: 32 (over z, x).
Axes of the slice: x: 4, y: 4, z: 8, core: 2. Of those that a mesh axis runs over, the one named last changes fastest.
Arguments:
- frames_now: bfloat16 [4096, 131072], P('traj', 'feat'), may hold values from -6 to 6
- frames_lag: bfloat16 [4096, 131072], P('traj', 'feat'), may hold values from -6 to 6
- test_matrix: bfloat16 [131072, 256], P('feat'), may hold values from -0.015625 to 0.015625
- feature_scale: float32 [131072], P('feat'), may hold values from 0.1 to 8
Outputs:
- basis: bfloat16 [131072, 256], P('feat')
- upper: float32 [256, 256], replicated
All inputs are finite; a program needn't handle non-finite values.
Results may differ from a plain program's by a relative error of at most 0.006.
Values may be sent and summed in bfloat16 or wider, within the bound.
No kernel may reach another device: no remote copies, remote signals or barrier semaphores. Data moves between devices by JAX's collectives and lax.ppermute only.
A program may use at most 64 MiB of HBM per device.

v0:
```python
import jax
import jax.numpy as jnp
from jax import lax
from jax.experimental import pallas as pl
from jax.experimental.pallas import tpu as pltpu
from jax.sharding import Mesh
from jax.sharding import PartitionSpec as P

F32 = jnp.float32
BF16 = jnp.bfloat16
EXACT = lax.Precision.HIGHEST


def shifted(x, axis, by):
    n = lax.axis_size(axis)
    return lax.ppermute(x, axis, [((i + by) % n, i) for i in range(n)])


def swapped(x, axis, mask):
    n = lax.axis_size(axis)
    return lax.ppermute(x, axis, [(i ^ mask, i) for i in range(n)])


def piece(x, index, size):
    return lax.dynamic_slice_in_dim(x, index * size, size, axis=0)


def scatter_sum(x, axis):
    n = lax.axis_size(axis)
    me = lax.axis_index(axis)
    size = x.shape[0] // n
    total = piece(x, me, size).astype(F32)
    for by in (2, 1, 3) if n == 4 else (1,):
        total = total + shifted(piece(x, (me + by) % n, size), axis, n - by).astype(F32)
    return total


def gather(x, axis):
    n = lax.axis_size(axis)
    me = lax.axis_index(axis)
    size = x.shape[0]
    out = jnp.zeros((n * size, x.shape[1]), x.dtype)
    out = lax.dynamic_update_slice_in_dim(out, x, me * size, axis=0)
    for by in (2, 1, 3) if n == 4 else (1,):
        out = lax.dynamic_update_slice_in_dim(out, shifted(x, axis, by), ((me + by) % n) * size, axis=0)
    return out


def ring_sum(x, axis):
    own = x.astype(BF16)
    before = shifted(own, axis, -1).astype(F32)
    after = shifted(own, axis, 1).astype(F32)
    two = x + before
    three = two + after
    far = shifted(three.astype(BF16), axis, 3).astype(F32)
    near = shifted(two.astype(BF16), axis, -2).astype(F32)
    return three + (far + near)


def exact_sum(x, axis):
    if lax.axis_size(axis) == 4:
        return (x + swapped(x, axis, 1)) + (swapped(x, axis, 2) + swapped(x, axis, 3))
    x = (x + swapped(x, axis, 1)) + (swapped(x, axis, 6) + swapped(x, axis, 7))
    return x + swapped(x, axis, 2)


def factor_block(tile, lead, size):
    groups = size // 8
    rows = [tile[8 * g : 8 * g + 8, :] for g in range(groups)]
    sub = lax.broadcasted_iota(jnp.int32, (8, 128), 0)
    for q in range(groups):
        first = lead + 8 * q
        column = [
            [jnp.broadcast_to(rows[g][:, first + k : first + k + 1], (8, 128)) for g in range(q, groups)]
            for k in range(8)
        ]
        pivots = jnp.zeros((8, 128), F32)
        for j in range(8):
            pivot = jnp.broadcast_to(column[j][0][j : j + 1, :], (8, 128))
            inverse = 1.0 / pivot
            pivots = jnp.where(sub == j, pivot, pivots)
            factor = [c * inverse for c in column[j]]
            factor[0] = jnp.where(sub > j, factor[0], 0.0)
            for k in range(j + 1, 8):
                top = jnp.broadcast_to(column[k][0][j : j + 1, :], (8, 128))
                column[k] = [c - f * top for c, f in zip(column[k], factor)]
            top = jnp.broadcast_to(rows[q][j : j + 1, :], (8, 128))
            for g in range(q, groups):
                rows[g] = rows[g] - factor[g - q] * top
        rows[q] = rows[q] * lax.rsqrt(pivots)
    return jnp.concatenate(rows, axis=0)


def factor_kernel(scale, gram_ref, upper_ref, high_ref, low_ref, work):
    n = gram_ref.shape[0]
    size = 64
    row = lax.broadcasted_iota(jnp.int32, (n, n), 0)
    col = lax.broadcasted_iota(jnp.int32, (n, n), 1)
    work[:, :n] = gram_ref[...]
    work[:, n:] = jnp.where(row == col, 1.0, 0.0).astype(F32)
    block_row = lax.broadcasted_iota(jnp.int32, (size, 128), 0)
    block_col = lax.broadcasted_iota(jnp.int32, (size, 128), 1)
    for r0 in range(0, n, size):
        r1 = r0 + size
        lead = r0 % 128
        other = (lead + size) % 128
        tile = work[r0:r1, r0 - lead : r0 - lead + 128]
        mine = (block_col >= lead) & (block_col < lead + size)
        tile = jnp.where(mine, tile, jnp.where(block_col - other == block_row, 1.0, 0.0))
        tile = factor_block(tile, lead, size)
        inverse = tile[:, other : other + size]
        panel = jnp.dot(inverse, work[r0:r1, :], precision=EXACT, preferred_element_type=F32)
        work[r0:r1, :] = panel
        if r1 < n:
            work[r1:, :] = work[r1:, :] - lax.dot_general(
                panel[:, r1:n], panel, (((0,), (0,)), ((), ())), precision=EXACT, preferred_element_type=F32
            )
    upper_ref[...] = jnp.where(row <= col, work[:, :n], 0.0)
    inverse = jnp.where(row >= col, work[:, n:], 0.0) * scale
    high = inverse.astype(BF16)
    high_ref[...] = high
    low_ref[...] = (inverse - high.astype(F32)).astype(BF16)


def factorize(gram, scale):
    n = gram.shape[0]
    whole = pl.BlockSpec(memory_space=pltpu.VMEM)
    return pl.pallas_call(
        lambda *refs: factor_kernel(scale, *refs),
        out_shape=[
            jax.ShapeDtypeStruct((n, n), F32),
            jax.ShapeDtypeStruct((n, n), BF16),
            jax.ShapeDtypeStruct((n, n), BF16),
        ],
        in_specs=[whole],
        out_specs=[whole] * 3,
        scratch_shapes=[pltpu.VMEM((n, 2 * n), F32)],
        compiler_params=pltpu.CompilerParams(vmem_limit_bytes=16 * 2**20),
        cost_estimate=pl.CostEstimate(flops=12 * n * n * n, bytes_accessed=8 * n * n, transcendentals=0),
        name="factorize",
    )(gram)


def project_kernel(now_ref, lag_ref, test_ref, scale_ref, out_ref, acc):
    step = pl.program_id(0)
    frames = now_ref.shape[0]
    columns = test_ref.shape[1]

    @pl.when(step == 0)
    def _():
        acc[...] = jnp.zeros_like(acc)

    scale = jnp.transpose(jnp.broadcast_to(scale_ref[...], (128, scale_ref.shape[1])))
    test = test_ref[...].astype(F32)
    scaled = jnp.concatenate([scale * test[:, i : i + 128] for i in range(0, columns, 128)], axis=1).astype(BF16)
    acc[:frames, :] += jnp.dot(now_ref[...], scaled, preferred_element_type=F32)
    acc[frames:, :] += jnp.dot(lag_ref[...], scaled, preferred_element_type=F32)

    @pl.when(step == pl.num_programs(0) - 1)
    def _():
        out_ref[...] = jnp.transpose(acc[...]).astype(BF16)


def project(frames_now, frames_lag, test_matrix, scale):
    frames, features = frames_now.shape
    columns = test_matrix.shape[1]
    block = 512
    return pl.pallas_call(
        project_kernel,
        grid=(features // block,),
        in_specs=[
            pl.BlockSpec((frames, block), lambda i: (0, i)),
            pl.BlockSpec((frames, block), lambda i: (0, i)),
            pl.BlockSpec((block, columns), lambda i: (i, 0)),
            pl.BlockSpec((1, block), lambda i: (0, i)),
        ],
        out_specs=pl.BlockSpec((columns, 2 * frames), lambda i: (0, 0)),
        out_shape=jax.ShapeDtypeStruct((columns, 2 * frames), BF16),
        scratch_shapes=[pltpu.VMEM((2 * frames, columns), F32)],
        compiler_params=pltpu.CompilerParams(vmem_limit_bytes=60 * 2**20),
        cost_estimate=pl.CostEstimate(
            flops=4 * frames * features * columns, bytes_accessed=4 * frames * features, transcendentals=0
        ),
        name="project",
    )(frames_now, frames_lag, test_matrix, scale)


def cross_kernel(order_ref, proj_ref, now_ref, lag_ref, factor_ref, out_ref):
    del order_ref
    frames = now_ref.shape[0]
    total = jnp.dot(proj_ref[:, frames:], now_ref[...], preferred_element_type=F32)
    total = total + jnp.dot(proj_ref[:, :frames], lag_ref[...], preferred_element_type=F32)
    out_ref[0] = (total * factor_ref[...]).astype(out_ref.dtype)


def cross(order, block, proj, frames_now, frames_lag, factor, dtype):
    frames, features = frames_now.shape
    columns = proj.shape[0]
    count = order.shape[0]
    return pl.pallas_call(
        cross_kernel,
        grid_spec=pltpu.PrefetchScalarGridSpec(
            num_scalar_prefetch=1,
            grid=(count,),
            in_specs=[
                pl.BlockSpec((columns, 2 * frames), lambda i, order: (0, 0)),
                pl.BlockSpec((frames, block), lambda i, order: (0, order[i])),
                pl.BlockSpec((frames, block), lambda i, order: (0, order[i])),
                pl.BlockSpec((1, block), lambda i, order: (0, order[i])),
            ],
            out_specs=pl.BlockSpec((1, columns, block), lambda i, order: (i, 0, 0)),
        ),
        out_shape=jax.ShapeDtypeStruct((count, columns, block), dtype),
        compiler_params=pltpu.CompilerParams(vmem_limit_bytes=50 * 2**20),
        cost_estimate=pl.CostEstimate(
            flops=4 * frames * count * block * columns,
            bytes_accessed=4 * frames * count * block,
            transcendentals=0,
        ),
        name="cross",
    )(order, proj, frames_now, frames_lag, factor)


def combine_kernel(own_ref, came_ref, *out_refs):
    for k, out_ref in enumerate(out_refs):
        out_ref[...] = (own_ref[k + 1] + came_ref[k + 1].astype(F32)).astype(BF16)


def combine(own, came):
    count, columns, block = own.shape
    whole = pl.BlockSpec(memory_space=pltpu.VMEM)
    return pl.pallas_call(
        combine_kernel,
        in_specs=[whole] * 2,
        out_specs=[whole] * (count - 1),
        out_shape=[jax.ShapeDtypeStruct((columns, block), BF16)] * (count - 1),
        compiler_params=pltpu.CompilerParams(vmem_limit_bytes=16 * 2**20),
        name="combine",
    )(own, came)


def gram_kernel(core_ref, own_ref, came_ref, a_ref, b_ref, d_ref, keep_ref, send_ref, rows_ref, work):
    total = own_ref[0] + came_ref[0].astype(F32)
    total = total + (a_ref[...].astype(F32) + b_ref[...].astype(F32) + d_ref[...].astype(F32))
    half = keep_ref.shape[0]
    core = core_ref[0]
    work[...] = lax.dot_general(
        total, total, (((1,), (1,)), ((), ())), precision=EXACT, preferred_element_type=F32
    )
    keep_ref[...] = work[pl.ds(pl.multiple_of(core * half, half), half), :]
    send_ref[...] = work[pl.ds(pl.multiple_of((1 - core) * half, half), half), :]
    rows_ref[...] = jnp.transpose(total).astype(BF16)


def gram_of(core, own, came, others):
    columns, block = own.shape[1:]
    whole = pl.BlockSpec(memory_space=pltpu.VMEM)
    half = jax.ShapeDtypeStruct((columns // 2, columns), F32)
    return pl.pallas_call(
        gram_kernel,
        in_specs=[pl.BlockSpec(memory_space=pltpu.SMEM)] + [whole] * 5,
        out_specs=[whole] * 3,
        out_shape=[half, half, jax.ShapeDtypeStruct((block, columns), BF16)],
        scratch_shapes=[pltpu.VMEM((columns, columns), F32)],
        compiler_params=pltpu.CompilerParams(vmem_limit_bytes=16 * 2**20),
        name="gram",
    )(core, own, came, *others)


def basis_kernel(sketch_ref, high_ref, low_ref, out_ref):
    transposed = (((1,), (1,)), ((), ()))
    total = lax.dot_general(sketch_ref[...], high_ref[...], transposed, preferred_element_type=F32)
    total = total + lax.dot_general(sketch_ref[...], low_ref[...], transposed, preferred_element_type=F32)
    out_ref[...] = total.astype(BF16)


def basis_of(sketch, high, low):
    rows, columns = sketch.shape
    block = 512
    small = pl.BlockSpec((columns, columns), lambda i: (0, 0))
    return pl.pallas_call(
        basis_kernel,
        grid=(rows // block,),
        in_specs=[pl.BlockSpec((block, columns), lambda i: (i, 0)), small, small],
        out_specs=pl.BlockSpec((block, columns), lambda i: (i, 0)),
        out_shape=jax.ShapeDtypeStruct((rows, columns), BF16),
        compiler_params=pltpu.CompilerParams(vmem_limit_bytes=16 * 2**20),
        cost_estimate=pl.CostEstimate(
            flops=4 * rows * columns * columns, bytes_accessed=4 * rows * columns, transcendentals=0
        ),
        name="basis",
    )(sketch, high, low)


def on_device(frames_now, frames_lag, test_matrix, feature_scale):
    frames, features = frames_now.shape
    frame_total = frames * lax.axis_size(("y", "c"))
    feature_total = features * lax.axis_size(("z", "x"))
    ring = lax.axis_size("y")
    scale = feature_scale[None, :]
    factor = (0.5 / frame_total) * scale
    with jax.named_scope("project"):
        part = project(frames_now, frames_lag, test_matrix, scale)
        proj = gather(ring_sum(scatter_sum(part, "x"), "z").astype(BF16), "x")

    with jax.named_scope("sketch"):
        y = lax.axis_index("y")
        c = lax.axis_index("c")
        block = features // (2 * ring)
        turn = (y + jnp.arange(ring, dtype=jnp.int32)) % ring
        sent = cross((1 - c) * ring + turn, block, proj, frames_now, frames_lag, factor, BF16)
        came = swapped(sent, "c", 1)
        own = cross(c * ring + turn, block, proj, frames_now, frames_lag, factor, F32)
        pieces = combine(own, came)
        others = [shifted(pieces[k - 1], "y", -k) for k in (2, 1, 3)]

    with jax.named_scope("gram"):
        keep, send, mine = gram_of(c[None], own, came, others)
        slab = scatter_sum(keep + swapped(send, "c", 1), "y")
        slab, mine = lax.optimization_barrier((slab, mine))
        whole = gather(mine, "y")
        slab = exact_sum(exact_sum(slab, "x"), "z")
        half = gather(slab, "y")
        half, whole = lax.optimization_barrier((half, whole))
        gram = gather(half, "c")
        whole = gather(whole, "c")
        upper, high, low = factorize(gram, feature_total**0.5)
    return (basis_of(whole, high, low), upper)


def solution(mesh):
    split = Mesh(mesh.devices.reshape(4, 2, 8, 4), ("y", "c", "z", "x"))
    traj, feat = ("y", "c"), ("z", "x")
    in_specs = (P(traj, feat), P(traj, feat), P(feat, None), P(feat))
    out_specs = (P(feat, None), P())
    return jax.shard_map(
        on_device, mesh=split, in_specs=in_specs, out_specs=out_specs, check_vma=False
    )
```

profile of v0, /device:TPU:1, one launch (start us, length us, event | category | flops | bytes accessed | tf_op | source)
XLA Modules:
  0.0 144.5 jit_solution(16920952422196056046)
XLA Ops:
  0.7 9.2 %project.1 = bf16[256,1024]{1,0:T(8,128)(2,1)} custom-call(bf16[512,4096]{1,0:T(8,128)(2,1)} %now_ref.5, bf16[512,4096]{1,0:T(8,128)(2,1)} %lag_ref.5, bf16[4096,256]{1,0:T(8,128)(2,1)} %test_ref.1, f32[1,4096]{1,0:T(1,128)} %bitcast.5), custom_call_target="tpu_custom_call" | custom-call | flops 2147483648 | bytes 8388608 | tf_op jit(solution)/shard_map/project/project/pallas_call | solution.py:168
  10.9 3.7 %collective-permute-start = (bf16[64,1024]{1,0:T(8,128)(2,1)S(1)}, bf16[64,1024]{1,0:T(8,128)(2,1)S(1)}, u32[]{:S(2)}, u32[]{:S(2)}) collective-permute-start(bf16[64,1024]{1,0:T(8,128)(2,1)S(1)} %get-tuple-element.34), channel_id=1, source_target_pairs={{2,0},{3,1},{0,2},{1,3},{6,4},{7,5},{4,6},{5,7},{10,8},{11,9},{8,1... | collective-permute-start | bytes 393224 | tf_op jit(solution)/shard_map/project/ppermute | solution.py:16
  14.9 2.4 %collective-permute-start.2 = (bf16[64,1024]{1,0:T(8,128)(2,1)S(1)}, bf16[64,1024]{1,0:T(8,128)(2,1)S(1)}, u32[]{:S(2)}, u32[]{:S(2)}) collective-permute-start(bf16[64,1024]{1,0:T(8,128)(2,1)S(1)} %get-tuple-element.35), channel_id=1, source_target_pairs={{1,0},{2,1},{3,2},{0,3},{5,4},{6,5},{7,6},{4,7},{9,8},{10,9},{11,1... | collective-permute-start | bytes 393224 | tf_op jit(solution)/shard_map/project/ppermute | solution.py:16
  17.3 4.5 %collective-permute-done.1 = bf16[64,1024]{1,0:T(8,128)(2,1)S(1)} collective-permute-done((bf16[64,1024]{1,0:T(8,128)(2,1)S(1)}, bf16[64,1024]{1,0:T(8,128)(2,1)S(1)}, u32[]{:S(2)}, u32[]{:S(2)}) %collective-permute-start.1) | collective-permute-done | bytes 131104 | tf_op jit(solution)/shard_map/project/ppermute | solution.py:16
  23.9 4.0 %collective-permute-start.4 = (bf16[64,1024]{1,0:T(8,128)(2,1)S(1)}, bf16[64,1024]{1,0:T(8,128)(2,1)S(1)}, u32[]{:S(2)}, u32[]{:S(2)}) collective-permute-start(bf16[64,1024]{1,0:T(8,128)(2,1)S(1)} %get-tuple-element.32), channel_id=1, source_target_pairs={{4,0},{8,4},{12,8},{16,12},{20,16},{24,20},{28,24},{0,28},{5,1},{9... | collective-permute-start | bytes 393224 | tf_op jit(solution)/shard_map/project/ppermute | solution.py:16
  27.9 2.3 %collective-permute-done.3 = bf16[64,1024]{1,0:T(8,128)(2,1)S(1)} collective-permute-done((bf16[64,1024]{1,0:T(8,128)(2,1)S(1)}, bf16[64,1024]{1,0:T(8,128)(2,1)S(1)}, u32[]{:S(2)}, u32[]{:S(2)}) %collective-permute-start.3) | collective-permute-done | bytes 131104 | tf_op jit(solution)/shard_map/project/ppermute | solution.py:16
  30.3 3.5 %collective-permute-start.5 = (bf16[64,1024]{1,0:T(8,128)(2,1)S(1)}, bf16[64,1024]{1,0:T(8,128)(2,1)S(1)}, u32[]{:S(2)}, u32[]{:S(2)}) collective-permute-start(bf16[64,1024]{1,0:T(8,128)(2,1)S(1)} %get-tuple-element.37), channel_id=1, source_target_pairs={{12,0},{16,4},{20,8},{24,12},{28,16},{0,20},{4,24},{8,28},{13,1},{... | collective-permute-start | bytes 393224 | tf_op jit(solution)/shard_map/project/ppermute | solution.py:16
  35.2 7.5 %collective-permute-done.5 = bf16[64,1024]{1,0:T(8,128)(2,1)S(1)} collective-permute-done((bf16[64,1024]{1,0:T(8,128)(2,1)S(1)}, bf16[64,1024]{1,0:T(8,128)(2,1)S(1)}, u32[]{:S(2)}, u32[]{:S(2)}) %collective-permute-start.5) | collective-permute-done | bytes 131104 | tf_op jit(solution)/shard_map/project/ppermute | solution.py:16
  43.0 4.9 %collective-permute-start.8 = (bf16[64,1024]{1,0:T(8,128)(2,1)S(1)}, bf16[64,1024]{1,0:T(8,128)(2,1)S(1)}, u32[]{:S(2)}, u32[]{:S(2)}) collective-permute-start(bf16[64,1024]{1,0:T(8,128)(2,1)S(1)} %get-tuple-element.31), channel_id=1, source_target_pairs={{1,0},{2,1},{3,2},{0,3},{5,4},{6,5},{7,6},{4,7},{9,8},{10,9},{11,1... | collective-permute-start | bytes 393224 | tf_op jit(solution)/shard_map/project/ppermute | solution.py:16
  49.9 3.3 %collective-permute-done.9 = bf16[64,1024]{1,0:T(8,128)(2,1)S(1)} collective-permute-done((bf16[64,1024]{1,0:T(8,128)(2,1)S(1)}, bf16[64,1024]{1,0:T(8,128)(2,1)S(1)}, u32[]{:S(2)}, u32[]{:S(2)}) %collective-permute-start.9) | collective-permute-done | bytes 131104 | tf_op jit(solution)/shard_map/project/ppermute | solution.py:16
  53.2 4.4 %cross.3 = bf16[4,256,512]{2,1,0:T(8,128)(2,1)S(1)} custom-call(s32[4]{0:T(128)S(1)} %broadcast_add_fusion.order_ref, bf16[256,1024]{1,0:T(8,128)(2,1)S(1)} %constant_dynamic-update-slice_fusion.12.proj_ref, bf16[512,4096]{1,0:T(8,128)(2,1)} %now_ref.5, bf16[512,4096]{1,0:T(8,128)(2,1)} %lag_ref.5, f32[1,4096]{1,0:T(1,128)S(1)} %bitcast.3), custom_call_target="tpu_custom_call" | custom-call | flops 1073741824 | bytes 4194304 | tf_op jit(solution)/shard_map/sketch/cross/pallas_call | solution.py:200
  57.6 2.5 %collective-permute-start.10 = (bf16[4,256,512]{2,1,0:T(8,128)(2,1)S(1)}, bf16[4,256,512]{2,1,0:T(8,128)(2,1)S(1)}, u32[]{:S(2)}, u32[]{:S(2)}) collective-permute-start(bf16[4,256,512]{2,1,0:T(8,128)(2,1)S(1)} %cross.3), channel_id=1, source_target_pairs={{32,0},{0,32},{33,1},{1,33},{34,2},{2,34},{35,3},{3,35},{36,4},{4,... | collective-permute-start | bytes 3145736 | tf_op jit(solution)/shard_map/sketch/ppermute | solution.py:21
  60.2 4.4 %cross.2.own_ref = f32[4,256,512]{2,1,0:T(8,128)S(1)} custom-call(s32[4]{0:T(128)S(1)} %fusion.3.order_ref, bf16[256,1024]{1,0:T(8,128)(2,1)S(1)} %constant_dynamic-update-slice_fusion.12.proj_ref, bf16[512,4096]{1,0:T(8,128)(2,1)} %now_ref.5, bf16[512,4096]{1,0:T(8,128)(2,1)} %lag_ref.5, f32[1,4096]{1,0:T(1,128)S(1)} %bitcast.4), custom_call_target="tpu_custom_call" | custom-call | flops 1073741824 | bytes 4194304 | tf_op jit(solution)/shard_map/sketch/cross/pallas_call | solution.py:200
  64.8 3.0 %collective-permute-start.11 = (bf16[256,512]{1,0:T(8,128)(2,1)S(1)}, bf16[256,512]{1,0:T(8,128)(2,1)S(1)}, u32[]{:S(2)}, u32[]{:S(2)}) collective-permute-start(bf16[256,512]{1,0:T(8,128)(2,1)S(1)} %get-tuple-element.15), channel_id=1, source_target_pairs={{128,0},{192,64},{0,128},{64,192},{129,1},{193,65},{1,129},{65,193... | collective-permute-start | bytes 786440 | tf_op jit(solution)/shard_map/sketch/ppermute | solution.py:16
  68.2 2.3 %collective-permute-start.13 = (bf16[256,512]{1,0:T(8,128)(2,1)S(1)}, bf16[256,512]{1,0:T(8,128)(2,1)S(1)}, u32[]{:S(2)}, u32[]{:S(2)}) collective-permute-start(bf16[256,512]{1,0:T(8,128)(2,1)S(1)} %get-tuple-element.17), channel_id=1, source_target_pairs={{64,0},{128,64},{192,128},{0,192},{65,1},{129,65},{193,129},{1,193... | collective-permute-start | bytes 786440 | tf_op jit(solution)/shard_map/sketch/ppermute | solution.py:16
  70.4 3.9 %collective-permute-done.11.a_ref = bf16[256,512]{1,0:T(8,128)(2,1)S(1)} collective-permute-done((bf16[256,512]{1,0:T(8,128)(2,1)S(1)}, bf16[256,512]{1,0:T(8,128)(2,1)S(1)}, u32[]{:S(2)}, u32[]{:S(2)}) %collective-permute-start.11) | collective-permute-done | bytes 262176 | tf_op jit(solution)/shard_map/sketch/ppermute | solution.py:16
  74.3 5.9 %collective-permute-done.12.b_ref = bf16[256,512]{1,0:T(8,128)(2,1)S(1)} collective-permute-done((bf16[256,512]{1,0:T(8,128)(2,1)S(1)}, bf16[256,512]{1,0:T(8,128)(2,1)S(1)}, u32[]{:S(2)}, u32[]{:S(2)}) %collective-permute-start.12) | collective-permute-done | bytes 262176 | tf_op jit(solution)/shard_map/sketch/ppermute | solution.py:16
  95.2 2.9 %collective-permute-start.22 = (f32[32,256]{1,0:T(8,128)S(1)}, f32[32,256]{1,0:T(8,128)S(1)}, u32[]{:S(2)}, u32[]{:S(2)}) collective-permute-start(f32[32,256]{1,0:T(8,128)S(1)} %add_add_fusion.1), channel_id=1, source_target_pairs={{24,0},{28,4},{16,8},{20,12},{8,16},{12,20},{0,24},{4,28},{25,1},{... | collective-permute-start | bytes 98312 | tf_op jit(solution)/shard_map/gram/ppermute | solution.py:21
  102.1 2.8 %collective-permute-start.24 = (f32[32,256]{1,0:T(8,128)S(1)}, f32[32,256]{1,0:T(8,128)S(1)}, u32[]{:S(2)}, u32[]{:S(2)}) collective-permute-start(f32[32,256]{1,0:T(8,128)S(1)} %add_add_fusion), channel_id=1, source_target_pairs={{8,0},{12,4},{0,8},{4,12},{24,16},{28,20},{16,24},{20,28},{9,1},{1... | collective-permute-start | bytes 98312 | tf_op jit(solution)/shard_map/gram/ppermute | solution.py:21
  112.4 2.4 %collective-permute-done.25 = f32[32,256]{1,0:T(8,128)S(1)} collective-permute-done((f32[32,256]{1,0:T(8,128)S(1)}, f32[32,256]{1,0:T(8,128)S(1)}, u32[]{:S(2)}, u32[]{:S(2)}) %collective-permute-start.25) | collective-permute-done | bytes 32800 | tf_op jit(solution)/shard_map/gram/ppermute | solution.py:16
  116.2 3.4 %collective-permute-done.27 = f32[32,256]{1,0:T(8,128)S(1)} collective-permute-done((f32[32,256]{1,0:T(8,128)S(1)}, f32[32,256]{1,0:T(8,128)S(1)}, u32[]{:S(2)}, u32[]{:S(2)}) %collective-permute-start.27) | collective-permute-done | bytes 32800 | tf_op jit(solution)/shard_map/gram/ppermute | solution.py:16
  119.7 7.7 %collective-permute-start.31 = (bf16[2048,256]{1,0:T(8,128)(2,1)S(1)}, bf16[2048,256]{1,0:T(8,128)(2,1)S(1)}, u32[]{:S(2)}, u32[]{:S(2)}) collective-permute-start(bf16[2048,256]{1,0:T(8,128)(2,1)S(1)} %constant_dynamic-update-slice_fusion.4), channel_id=1, source_target_pairs={{32,0},{0,32},{33,1},{1,33},{34,2},{2,34},{35,3},{3,35},{36,4},{4,... | collective-permute-start | bytes 3145736 | tf_op jit(solution)/shard_map/gram/ppermute | solution.py:16
  129.9 10.0 %factorize.1 = (f32[256,256]{1,0:T(8,128)}, bf16[256,256]{1,0:T(8,128)(2,1)S(1)}, bf16[256,256]{1,0:T(8,128)(2,1)S(1)}) custom-call(f32[256,256]{1,0:T(8,128)S(1)} %constant_dynamic-update-slice_fusion.refs_0_), custom_call_target="tpu_custom_call" | custom-call | flops 201326592 | bytes 524288 | tf_op jit(solution)/shard_map/gram/factorize/pallas_call | solution.py:128
  140.0 4.5 %basis.1 = bf16[4096,256]{1,0:T(8,128)(2,1)} custom-call(bf16[4096,256]{1,0:T(8,128)(2,1)S(1)} %constant_dynamic-update-slice_fusion.2.sketch_ref, bf16[256,256]{1,0:T(8,128)(2,1)S(1)} %get-tuple-element.25.high_ref, bf16[256,256]{1,0:T(8,128)(2,1)S(1)} %get-tuple-element.26.low_ref), custom_call_target="tpu_custom_call" | custom-call | flops 1073741824 | bytes 4194304 | tf_op jit(solution)/shard_map/basis/pallas_call | solution.py:281
  (83 shorter events, 38.0 us)
Async XLA Ops:
  10.9 6.3 %collective-permute-start = (bf16[64,1024]{1,0:T(8,128)(2,1)S(1)}, bf16[64,1024]{1,0:T(8,128)(2,1)S(1)}, u32[]{:S(2)}, u32[]{:S(2)}) collective-permute-start(bf16[64,1024]{1,0:T(8,128)(2,1)S(1)} %get-tuple-element.34), channel_id=1, source_target_pairs={{2,0},{3,1},{0,2},{1,3},{6,4},{7,5},{4,6},{5,7},{10,8},{11,9},{8,1... | collective-permute-start | bytes 393224 | tf_op jit(solution)/shard_map/project/ppermute | solution.py:16
  14.6 7.2 %collective-permute-start.1 = (bf16[64,1024]{1,0:T(8,128)(2,1)S(1)}, bf16[64,1024]{1,0:T(8,128)(2,1)S(1)}, u32[]{:S(2)}, u32[]{:S(2)}) collective-permute-start(bf16[64,1024]{1,0:T(8,128)(2,1)S(1)} %get-tuple-element.36), channel_id=1, source_target_pairs={{3,0},{0,1},{1,2},{2,3},{7,4},{4,5},{5,6},{6,7},{11,8},{8,9},{9,10... | collective-permute-start | bytes 393224 | tf_op jit(solution)/shard_map/project/ppermute | solution.py:16
  14.9 6.9 %collective-permute-start.2 = (bf16[64,1024]{1,0:T(8,128)(2,1)S(1)}, bf16[64,1024]{1,0:T(8,128)(2,1)S(1)}, u32[]{:S(2)}, u32[]{:S(2)}) collective-permute-start(bf16[64,1024]{1,0:T(8,128)(2,1)S(1)} %get-tuple-element.35), channel_id=1, source_target_pairs={{1,0},{2,1},{3,2},{0,3},{5,4},{6,5},{7,6},{4,7},{9,8},{10,9},{11,1... | collective-permute-start | bytes 393224 | tf_op jit(solution)/shard_map/project/ppermute | solution.py:16
  22.8 7.4 %collective-permute-start.3 = (bf16[64,1024]{1,0:T(8,128)(2,1)S(1)}, bf16[64,1024]{1,0:T(8,128)(2,1)S(1)}, u32[]{:S(2)}, u32[]{:S(2)}) collective-permute-start(bf16[64,1024]{1,0:T(8,128)(2,1)S(1)} %get-tuple-element.32), channel_id=1, source_target_pairs={{28,0},{0,4},{4,8},{8,12},{12,16},{16,20},{20,24},{24,28},{29,1},{... | collective-permute-start | bytes 393224 | tf_op jit(solution)/shard_map/project/ppermute | solution.py:16
  23.9 6.3 %collective-permute-start.4 = (bf16[64,1024]{1,0:T(8,128)(2,1)S(1)}, bf16[64,1024]{1,0:T(8,128)(2,1)S(1)}, u32[]{:S(2)}, u32[]{:S(2)}) collective-permute-start(bf16[64,1024]{1,0:T(8,128)(2,1)S(1)} %get-tuple-element.32), channel_id=1, source_target_pairs={{4,0},{8,4},{12,8},{16,12},{20,16},{24,20},{28,24},{0,28},{5,1},{9... | collective-permute-start | bytes 393224 | tf_op jit(solution)/shard_map/project/ppermute | solution.py:16
  30.3 12.4 %collective-permute-start.5 = (bf16[64,1024]{1,0:T(8,128)(2,1)S(1)}, bf16[64,1024]{1,0:T(8,128)(2,1)S(1)}, u32[]{:S(2)}, u32[]{:S(2)}) collective-permute-start(bf16[64,1024]{1,0:T(8,128)(2,1)S(1)} %get-tuple-element.37), channel_id=1, source_target_pairs={{12,0},{16,4},{20,8},{24,12},{28,16},{0,20},{4,24},{8,28},{13,1},{... | collective-permute-start | bytes 393224 | tf_op jit(solution)/shard_map/project/ppermute | solution.py:16
  33.7 9.0 %collective-permute-start.6 = (bf16[64,1024]{1,0:T(8,128)(2,1)S(1)}, bf16[64,1024]{1,0:T(8,128)(2,1)S(1)}, u32[]{:S(2)}, u32[]{:S(2)}) collective-permute-start(bf16[64,1024]{1,0:T(8,128)(2,1)S(1)} %get-tuple-element.38), channel_id=1, source_target_pairs={{24,0},{28,4},{0,8},{4,12},{8,16},{12,20},{16,24},{20,28},{25,1},{... | collective-permute-start | bytes 393224 | tf_op jit(solution)/shard_map/project/ppermute | solution.py:16
  42.8 5.4 %collective-permute-start.7 = (bf16[64,1024]{1,0:T(8,128)(2,1)S(1)}, bf16[64,1024]{1,0:T(8,128)(2,1)S(1)}, u32[]{:S(2)}, u32[]{:S(2)}) collective-permute-start(bf16[64,1024]{1,0:T(8,128)(2,1)S(1)} %get-tuple-element.31), channel_id=1, source_target_pairs={{2,0},{3,1},{0,2},{1,3},{6,4},{7,5},{4,6},{5,7},{10,8},{11,9},{8,1... | collective-permute-start | bytes 393224 | tf_op jit(solution)/shard_map/project/ppermute | solution.py:16
  43.0 6.9 %collective-permute-start.8 = (bf16[64,1024]{1,0:T(8,128)(2,1)S(1)}, bf16[64,1024]{1,0:T(8,128)(2,1)S(1)}, u32[]{:S(2)}, u32[]{:S(2)}) collective-permute-start(bf16[64,1024]{1,0:T(8,128)(2,1)S(1)} %get-tuple-element.31), channel_id=1, source_target_pairs={{1,0},{2,1},{3,2},{0,3},{5,4},{6,5},{7,6},{4,7},{9,8},{10,9},{11,1... | collective-permute-start | bytes 393224 | tf_op jit(solution)/shard_map/project/ppermute | solution.py:16
  47.9 5.3 %collective-permute-start.9 = (bf16[64,1024]{1,0:T(8,128)(2,1)S(1)}, bf16[64,1024]{1,0:T(8,128)(2,1)S(1)}, u32[]{:S(2)}, u32[]{:S(2)}) collective-permute-start(bf16[64,1024]{1,0:T(8,128)(2,1)S(1)} %get-tuple-element.31), channel_id=1, source_target_pairs={{3,0},{0,1},{1,2},{2,3},{7,4},{4,5},{5,6},{6,7},{11,8},{8,9},{9,10... | collective-permute-start | bytes 393224 | tf_op jit(solution)/shard_map/project/ppermute | solution.py:16
  57.6 7.0 %collective-permute-start.10 = (bf16[4,256,512]{2,1,0:T(8,128)(2,1)S(1)}, bf16[4,256,512]{2,1,0:T(8,128)(2,1)S(1)}, u32[]{:S(2)}, u32[]{:S(2)}) collective-permute-start(bf16[4,256,512]{2,1,0:T(8,128)(2,1)S(1)} %cross.3), channel_id=1, source_target_pairs={{32,0},{0,32},{33,1},{1,33},{34,2},{2,34},{35,3},{3,35},{36,4},{4,... | collective-permute-start | bytes 3145736 | tf_op jit(solution)/shard_map/sketch/ppermute | solution.py:21
  64.8 9.5 %collective-permute-start.11 = (bf16[256,512]{1,0:T(8,128)(2,1)S(1)}, bf16[256,512]{1,0:T(8,128)(2,1)S(1)}, u32[]{:S(2)}, u32[]{:S(2)}) collective-permute-start(bf16[256,512]{1,0:T(8,128)(2,1)S(1)} %get-tuple-element.15), channel_id=1, source_target_pairs={{128,0},{192,64},{0,128},{64,192},{129,1},{193,65},{1,129},{65,193... | collective-permute-start | bytes 786440 | tf_op jit(solution)/shard_map/sketch/ppermute | solution.py:16
  67.8 12.5 %collective-permute-start.12 = (bf16[256,512]{1,0:T(8,128)(2,1)S(1)}, bf16[256,512]{1,0:T(8,128)(2,1)S(1)}, u32[]{:S(2)}, u32[]{:S(2)}) collective-permute-start(bf16[256,512]{1,0:T(8,128)(2,1)S(1)} %get-tuple-element.16), channel_id=1, source_target_pairs={{192,0},{0,64},{64,128},{128,192},{193,1},{1,65},{65,129},{129,193... | collective-permute-start | bytes 786440 | tf_op jit(solution)/shard_map/sketch/ppermute | solution.py:16
  68.2 12.1 %collective-permute-start.13 = (bf16[256,512]{1,0:T(8,128)(2,1)S(1)}, bf16[256,512]{1,0:T(8,128)(2,1)S(1)}, u32[]{:S(2)}, u32[]{:S(2)}) collective-permute-start(bf16[256,512]{1,0:T(8,128)(2,1)S(1)} %get-tuple-element.17), channel_id=1, source_target_pairs={{64,0},{128,64},{192,128},{0,192},{65,1},{129,65},{193,129},{1,193... | collective-permute-start | bytes 786440 | tf_op jit(solution)/shard_map/sketch/ppermute | solution.py:16
  82.9 4.5 %collective-permute-start.15 = (f32[32,256]{1,0:T(8,128)S(1)}, f32[32,256]{1,0:T(8,128)S(1)}, u32[]{:S(2)}, u32[]{:S(2)}) collective-permute-start(f32[32,256]{1,0:T(8,128)S(1)} %get-tuple-element.39), channel_id=1, source_target_pairs={{128,0},{192,64},{0,128},{64,192},{129,1},{193,65},{1,129},{65,193... | collective-permute-start | bytes 98312 | tf_op jit(solution)/shard_map/gram/ppermute | solution.py:16
  95.2 5.0 %collective-permute-start.22 = (f32[32,256]{1,0:T(8,128)S(1)}, f32[32,256]{1,0:T(8,128)S(1)}, u32[]{:S(2)}, u32[]{:S(2)}) collective-permute-start(f32[32,256]{1,0:T(8,128)S(1)} %add_add_fusion.1), channel_id=1, source_target_pairs={{24,0},{28,4},{16,8},{20,12},{8,16},{12,20},{0,24},{4,28},{25,1},{... | collective-permute-start | bytes 98312 | tf_op jit(solution)/shard_map/gram/ppermute | solution.py:21
  102.1 6.1 %collective-permute-start.24 = (f32[32,256]{1,0:T(8,128)S(1)}, f32[32,256]{1,0:T(8,128)S(1)}, u32[]{:S(2)}, u32[]{:S(2)}) collective-permute-start(f32[32,256]{1,0:T(8,128)S(1)} %add_add_fusion), channel_id=1, source_target_pairs={{8,0},{12,4},{0,8},{4,12},{24,16},{28,20},{16,24},{20,28},{9,1},{1... | collective-permute-start | bytes 98312 | tf_op jit(solution)/shard_map/gram/ppermute | solution.py:21
  104.9 14.6 %collective-permute-start.28 = (bf16[512,256]{1,0:T(8,128)(2,1)S(1)}, bf16[512,256]{1,0:T(8,128)(2,1)S(1)}, u32[]{:S(2)}, u32[]{:S(2)}) collective-permute-start(bf16[512,256]{1,0:T(8,128)(2,1)S(1)} %get-tuple-element.22), channel_id=1, source_target_pairs={{128,0},{192,64},{0,128},{64,192},{129,1},{193,65},{1,129},{65,193... | collective-permute-start | bytes 786440 | tf_op jit(solution)/shard_map/gram/ppermute | solution.py:16
  106.6 13.0 %collective-permute-start.29 = (bf16[512,256]{1,0:T(8,128)(2,1)S(1)}, bf16[512,256]{1,0:T(8,128)(2,1)S(1)}, u32[]{:S(2)}, u32[]{:S(2)}) collective-permute-start(bf16[512,256]{1,0:T(8,128)(2,1)S(1)} %get-tuple-element.22), channel_id=1, source_target_pairs={{64,0},{128,64},{192,128},{0,192},{65,1},{129,65},{193,129},{1,193... | collective-permute-start | bytes 786440 | tf_op jit(solution)/shard_map/gram/ppermute | solution.py:16
  107.6 12.0 %collective-permute-start.30 = (bf16[512,256]{1,0:T(8,128)(2,1)S(1)}, bf16[512,256]{1,0:T(8,128)(2,1)S(1)}, u32[]{:S(2)}, u32[]{:S(2)}) collective-permute-start(bf16[512,256]{1,0:T(8,128)(2,1)S(1)} %get-tuple-element.22), channel_id=1, source_target_pairs={{192,0},{0,64},{64,128},{128,192},{193,1},{1,65},{65,129},{129,193... | collective-permute-start | bytes 786440 | tf_op jit(solution)/shard_map/gram/ppermute | solution.py:16
  108.2 6.6 %collective-permute-start.25 = (f32[32,256]{1,0:T(8,128)S(1)}, f32[32,256]{1,0:T(8,128)S(1)}, u32[]{:S(2)}, u32[]{:S(2)}) collective-permute-start(f32[32,256]{1,0:T(8,128)S(1)} %get-tuple-element.29), channel_id=1, source_target_pairs={{128,0},{192,64},{0,128},{64,192},{129,1},{193,65},{1,129},{65,193... | collective-permute-start | bytes 98312 | tf_op jit(solution)/shard_map/gram/ppermute | solution.py:16
  110.2 5.9 %collective-permute-start.26 = (f32[32,256]{1,0:T(8,128)S(1)}, f32[32,256]{1,0:T(8,128)S(1)}, u32[]{:S(2)}, u32[]{:S(2)}) collective-permute-start(f32[32,256]{1,0:T(8,128)S(1)} %get-tuple-element.29), channel_id=1, source_target_pairs={{64,0},{128,64},{192,128},{0,192},{65,1},{129,65},{193,129},{1,193... | collective-permute-start | bytes 98312 | tf_op jit(solution)/shard_map/gram/ppermute | solution.py:16
  114.8 4.7 %collective-permute-start.27 = (f32[32,256]{1,0:T(8,128)S(1)}, f32[32,256]{1,0:T(8,128)S(1)}, u32[]{:S(2)}, u32[]{:S(2)}) collective-permute-start(f32[32,256]{1,0:T(8,128)S(1)} %get-tuple-element.29), channel_id=1, source_target_pairs={{192,0},{0,64},{64,128},{128,192},{193,1},{1,65},{65,129},{129,193... | collective-permute-start | bytes 98312 | tf_op jit(solution)/shard_map/gram/ppermute | solution.py:16
  119.7 20.2 %collective-permute-start.31 = (bf16[2048,256]{1,0:T(8,128)(2,1)S(1)}, bf16[2048,256]{1,0:T(8,128)(2,1)S(1)}, u32[]{:S(2)}, u32[]{:S(2)}) collective-permute-start(bf16[2048,256]{1,0:T(8,128)(2,1)S(1)} %constant_dynamic-update-slice_fusion.4), channel_id=1, source_target_pairs={{32,0},{0,32},{33,1},{1,33},{34,2},{2,34},{35,3},{3,35},{36,4},{4,... | collective-permute-start | bytes 3145736 | tf_op jit(solution)/shard_map/gram/ppermute | solution.py:16
  (10 other events, 64.4 us)
where the time goes:
time: 145 us; the launch traced here: 144 us
  starting transfers between devices  61.8 us (43%)
  waiting for transfers between devices  45.5 us (31%)
  Pallas kernels  33.4 us (23%)
  local copies, waits for them, and re-layouts  1.72 us (1%)
    ppermute x24, starting transfers between devices, shifted(): return lax.ppermute(x, axis, [((i + by) % n, i) for i in range(n)])  47.6 us
    ppermute x24, waiting for transfers between devices, shifted(): return lax.ppermute(x, axis, [((i + by) % n, i) for i in range(n)])  39.1 us
    ppermute x9, starting transfers between devices, swapped(): return lax.ppermute(x, axis, [(i ^ mask, i) for i in range(n)])  14.1 us
    pallas_call x1, Pallas kernels, factorize(): pl.pallas_call(lambda *refs: factor_kernel(scale, *refs), out_shape=[jax....  10 us
    pallas_call x1, Pallas kernels, project(): pl.pallas_call(project_kernel, grid=(features // block,), in_specs=[pl.Bl...  9.18 us
    pallas_call x2, Pallas kernels, cross(): pl.pallas_call(cross_kernel, grid_spec=pltpu.PrefetchScalarGridSpec(num_s...  8.83 us
    ppermute x9, waiting for transfers between devices, swapped(): return lax.ppermute(x, axis, [(i ^ mask, i) for i in range(n)])  6.4 us
    pallas_call x1, Pallas kernels, basis_of(): pl.pallas_call(basis_kernel, grid=(rows // block,), in_specs=[pl.BlockSpe...  4.51 us
  transfers between devices with their start and end apart: 33, of which 18 were waited for; matrix products, arithmetic and copies ran while one was open for 0% of the time, Pallas kernels for 10%

commit v1 on v0

--- a/solution.py
+++ b/solution.py
@@ -58,10 +58,7 @@
 
 
 def exact_sum(x, axis):
-    if lax.axis_size(axis) == 4:
-        return (x + swapped(x, axis, 1)) + (swapped(x, axis, 2) + swapped(x, axis, 3))
-    x = (x + swapped(x, axis, 1)) + (swapped(x, axis, 6) + swapped(x, axis, 7))
-    return x + swapped(x, axis, 2)
+    return (x + swapped(x, axis, 1)) + (swapped(x, axis, 2) + swapped(x, axis, 3))
 
 
 def factor_block(tile, lead, size):
@@ -141,84 +138,127 @@
     )(gram)
 
 
-def project_kernel(now_ref, lag_ref, test_ref, scale_ref, out_ref, acc):
-    step = pl.program_id(0)
-    frames = now_ref.shape[0]
-    columns = test_ref.shape[1]
-
-    @pl.when(step == 0)
-    def _():
-        acc[...] = jnp.zeros_like(acc)
-
-    scale = jnp.transpose(jnp.broadcast_to(scale_ref[...], (128, scale_ref.shape[1])))
-    test = test_ref[...].astype(F32)
-    scaled = jnp.concatenate([scale * test[:, i : i + 128] for i in range(0, columns, 128)], axis=1).astype(BF16)
-    acc[:frames, :] += jnp.dot(now_ref[...], scaled, preferred_element_type=F32)
-    acc[frames:, :] += jnp.dot(lag_ref[...], scaled, preferred_element_type=F32)
-
-    @pl.when(step == pl.num_programs(0) - 1)
-    def _():
-        out_ref[...] = jnp.transpose(acc[...]).astype(BF16)
-
-
-def project(frames_now, frames_lag, test_matrix, scale):
+def in_hbm(x):
+    return pltpu.with_memory_space_constraint(x, pltpu.HBM)
+
+
+def project_kernel(parts, me_ref, now_hbm, lag_hbm, test_hbm, scale_hbm, *refs):
+    *piece_refs, frames_both, test, scale_ref, total, sems = refs
+    frames, features = now_hbm.shape
+    columns = test.shape[1]
+    width = features // parts
+    copies = []
+    scales = pltpu.make_async_copy(scale_hbm, scale_ref, sems.at[3 * parts])
+    scales.start()
+    for i in range(parts):
+        at = pl.ds(i * width, width)
+        copies.append(
+            [
+                pltpu.make_async_copy(test_hbm.at[at], test.at[at], sems.at[3 * i]),
+                pltpu.make_async_copy(now_hbm.at[:, at], frames_both.at[pl.ds(0, frames), at], sems.at[3 * i + 1]),
+                pltpu.make_async_copy(lag_hbm.at[:, at], frames_both.at[pl.ds(frames, frames), at], sems.at[3 * i + 2]),
+            ]
+        )
+        for copy in copies[-1]:
+            copy.start()
+    scales.wait()
+    for i in range(parts):
+        copies[i][0].wait()
+        scaled = [
+            (jnp.transpose(test[r : r + 128, :]).astype(F32) * scale_ref[:, r : r + 128]).astype(BF16)
+            for r in range(i * width, (i + 1) * width, 128)
+        ]
+        scaled = jnp.concatenate(scaled, axis=1)
+        copies[i][1].wait()
+        copies[i][2].wait()
+        term = lax.dot_general(
+            scaled,
+            frames_both[:, i * width : (i + 1) * width],
+            (((1,), (1,)), ((), ())),
+            preferred_element_type=F32,
+        )
+        total[...] = term if i == 0 else total[...] + term
+    count = len(piece_refs)
+    size = columns // count
+    for k, piece_ref in enumerate(piece_refs):
+        at = pl.multiple_of(lax.rem(me_ref[0] + k, count) * size, size)
+        piece_ref[...] = total[pl.ds(at, size), :].astype(piece_ref.dtype)
+
+
+def project(me, count, frames_now, frames_lag, test_matrix, scale):
     frames, features = frames_now.shape
     columns = test_matrix.shape[1]
-    block = 512
-    return pl.pallas_call(
-        project_kernel,
-        grid=(features // block,),
-        in_specs=[
-            pl.BlockSpec((frames, block), lambda i: (0, i)),
-            pl.BlockSpec((frames, block), lambda i: (0, i)),
-            pl.BlockSpec((block, columns), lambda i: (i, 0)),
-            pl.BlockSpec((1, block), lambda i: (0, i)),
+    parts = 4
+    size = columns // count
+    vmem = pl.BlockSpec(memory_space=pltpu.VMEM)
+    hbm = pl.BlockSpec(memory_space=pl.ANY)
+    return pl.pallas_call(
+        lambda *refs: project_kernel(parts, *refs),
+        in_specs=[pl.BlockSpec(memory_space=pltpu.SMEM), hbm, hbm, hbm, hbm],
+        out_specs=[vmem] * count,
+        out_shape=[jax.ShapeDtypeStruct((size, 2 * frames), F32)]
+        + [jax.ShapeDtypeStruct((size, 2 * frames), BF16)] * (count - 1),
+        scratch_shapes=[
+            pltpu.VMEM((2 * frames, features), BF16),
+            pltpu.VMEM((features, columns), BF16),
+            pltpu.VMEM((1, features), F32),
+            pltpu.VMEM((columns, 2 * frames), F32),
+            pltpu.SemaphoreType.DMA((3 * parts + 1,)),
         ],
-        out_specs=pl.BlockSpec((columns, 2 * frames), lambda i: (0, 0)),
-        out_shape=jax.ShapeDtypeStruct((columns, 2 * frames), BF16),
-        scratch_shapes=[pltpu.VMEM((2 * frames, columns), F32)],
-        compiler_params=pltpu.CompilerParams(vmem_limit_bytes=60 * 2**20),
+        compiler_params=pltpu.CompilerParams(vmem_limit_bytes=32 * 2**20),
         cost_estimate=pl.CostEstimate(
             flops=4 * frames * features * columns, bytes_accessed=4 * frames * features, transcendentals=0
         ),
         name="project",
-    )(frames_now, frames_lag, test_matrix, scale)
-
-
-def cross_kernel(order_ref, proj_ref, now_ref, lag_ref, factor_ref, out_ref):
-    del order_ref
-    frames = now_ref.shape[0]
-    total = jnp.dot(proj_ref[:, frames:], now_ref[...], preferred_element_type=F32)
-    total = total + jnp.dot(proj_ref[:, :frames], lag_ref[...], preferred_element_type=F32)
-    out_ref[0] = (total * factor_ref[...]).astype(out_ref.dtype)
-
-
-def cross(order, block, proj, frames_now, frames_lag, factor, dtype):
+    )(me[None], in_hbm(frames_now), in_hbm(frames_lag), in_hbm(test_matrix), in_hbm(scale))
+
+
+def cross_kernel(where_ref, proj_ref, now_hbm, lag_hbm, factor_ref, out_ref, work, sems):
+    frames = now_hbm.shape[0]
+    count, _, block = out_ref.shape
+    copies = []
+    for k in range(count):
+        first = where_ref[0] * count + lax.rem(where_ref[1] + k, count)
+        at = pl.ds(pl.multiple_of(first * block, block), block)
+        copies.append(
+            [
+                pltpu.make_async_copy(now_hbm.at[:, at], work.at[k, pl.ds(0, frames)], sems.at[2 * k]),
+                pltpu.make_async_copy(lag_hbm.at[:, at], work.at[k, pl.ds(frames, frames)], sems.at[2 * k + 1]),
+            ]
+        )
+        for copy in copies[-1]:
+            copy.start()
+    proj = jnp.concatenate([proj_ref[:, frames:], proj_ref[:, :frames]], axis=1)
+    for k in range(count):
+        for copy in copies[k]:
+            copy.wait()
+        first = where_ref[0] * count + lax.rem(where_ref[1] + k, count)
+        total = jnp.dot(proj, work[k], preferred_element_type=F32)
+        factor = factor_ref[:, pl.ds(pl.multiple_of(first * block, block), block)]
+        out_ref[k] = (total * factor).astype(out_ref.dtype)
+
+
+def cross(half, first, count, proj, frames_now, frames_lag, factor, dtype):
     frames, features = frames_now.shape
     columns = proj.shape[0]
-    count = order.shape[0]
+    block = features // (2 * count)
+    vmem = pl.BlockSpec(memory_space=pltpu.VMEM)
+    hbm = pl.BlockSpec(memory_space=pl.ANY)
     return pl.pallas_call(
         cross_kernel,
-        grid_spec=pltpu.PrefetchScalarGridSpec(
-            num_scalar_prefetch=1,
-            grid=(count,),
-            in_specs=[
-                pl.BlockSpec((columns, 2 * frames), lambda i, order: (0, 0)),
-                pl.BlockSpec((frames, block), lambda i, order: (0, order[i])),
-                pl.BlockSpec((frames, block), lambda i, order: (0, order[i])),
-                pl.BlockSpec((1, block), lambda i, order: (0, order[i])),
-            ],
-            out_specs=pl.BlockSpec((1, columns, block), lambda i, order: (i, 0, 0)),
-        ),
+        in_specs=[pl.BlockSpec(memory_space=pltpu.SMEM), vmem, hbm, hbm, vmem],
+        out_specs=vmem,
         out_shape=jax.ShapeDtypeStruct((count, columns, block), dtype),
-        compiler_params=pltpu.CompilerParams(vmem_limit_bytes=50 * 2**20),
+        scratch_shapes=[
+            pltpu.VMEM((count, 2 * frames, block), BF16),
+            pltpu.SemaphoreType.DMA((2 * count,)),
+        ],
+        compiler_params=pltpu.CompilerParams(vmem_limit_bytes=24 * 2**20),
         cost_estimate=pl.CostEstimate(
-            flops=4 * frames * count * block * columns,
-            bytes_accessed=4 * frames * count * block,
-            transcendentals=0,
+            flops=2 * frames * features * columns, bytes_accessed=2 * frames * features, transcendentals=0
         ),
         name="cross",
-    )(order, proj, frames_now, frames_lag, factor)
+    )(jnp.stack([half, first]), proj, in_hbm(frames_now), in_hbm(frames_lag), factor)
 
 
 def combine_kernel(own_ref, came_ref, *out_refs):
@@ -267,23 +307,32 @@
     )(core, own, came, *others)
 
 
-def basis_kernel(sketch_ref, high_ref, low_ref, out_ref):
+def basis_kernel(parts, sketch_ref, high_ref, low_ref, out_hbm, work, sems):
     transposed = (((1,), (1,)), ((), ()))
-    total = lax.dot_general(sketch_ref[...], high_ref[...], transposed, preferred_element_type=F32)
-    total = total + lax.dot_general(sketch_ref[...], low_ref[...], transposed, preferred_element_type=F32)
-    out_ref[...] = total.astype(BF16)
+    size = work.shape[0] // parts
+    copies = []
+    for i in range(parts):
+        at = slice(i * size, (i + 1) * size)
+        total = lax.dot_general(sketch_ref[at, :], high_ref[...], transposed, preferred_element_type=F32)
+        total = total + lax.dot_general(sketch_ref[at, :], low_ref[...], transposed, preferred_element_type=F32)
+        work[at, :] = total.astype(BF16)
+        rows = pl.ds(i * size, size)
+        copies.append(pltpu.make_async_copy(work.at[rows], out_hbm.at[rows], sems.at[i]))
+        copies[-1].start()
+    for copy in copies:
+        copy.wait()
 
 
 def basis_of(sketch, high, low):
     rows, columns = sketch.shape
-    block = 512
-    small = pl.BlockSpec((columns, columns), lambda i: (0, 0))
-    return pl.pallas_call(
-        basis_kernel,
-        grid=(rows // block,),
-        in_specs=[pl.BlockSpec((block, columns), lambda i: (i, 0)), small, small],
-        out_specs=pl.BlockSpec((block, columns), lambda i: (i, 0)),
+    parts = 8
+    vmem = pl.BlockSpec(memory_space=pltpu.VMEM)
+    return pl.pallas_call(
+        lambda *refs: basis_kernel(parts, *refs),
+        in_specs=[vmem] * 3,
+        out_specs=pl.BlockSpec(memory_space=pl.ANY),
         out_shape=jax.ShapeDtypeStruct((rows, columns), BF16),
+        scratch_shapes=[pltpu.VMEM((rows, columns), BF16), pltpu.SemaphoreType.DMA((parts,))],
         compiler_params=pltpu.CompilerParams(vmem_limit_bytes=16 * 2**20),
         cost_estimate=pl.CostEstimate(
             flops=4 * rows * columns * columns, bytes_accessed=4 * rows * columns, transcendentals=0
@@ -300,17 +349,18 @@
     scale = feature_scale[None, :]
     factor = (0.5 / frame_total) * scale
     with jax.named_scope("project"):
-        part = project(frames_now, frames_lag, test_matrix, scale)
-        proj = gather(ring_sum(scatter_sum(part, "x"), "z").astype(BF16), "x")
+        own, *pieces = project(
+            lax.axis_index("x"), lax.axis_size("x"), frames_now, frames_lag, test_matrix, scale
+        )
+        for k in (2, 1, 3):
+            own = own + shifted(pieces[k - 1], "x", -k).astype(F32)
+        proj = gather(ring_sum(own, "z").astype(BF16), "x")
 
     with jax.named_scope("sketch"):
         y = lax.axis_index("y")
         c = lax.axis_index("c")
-        block = features // (2 * ring)
-        turn = (y + jnp.arange(ring, dtype=jnp.int32)) % ring
-        sent = cross((1 - c) * ring + turn, block, proj, frames_now, frames_lag, factor, BF16)
-        came = swapped(sent, "c", 1)
-        own = cross(c * ring + turn, block, proj, frames_now, frames_lag, factor, F32)
+        came = swapped(cross(1 - c, y, ring, proj, frames_now, frames_lag, factor, BF16), "c", 1)
+        own = cross(c, y, ring, proj, frames_now, frames_lag, factor, F32)
         pieces = combine(own, came)
         others = [shifted(pieces[k - 1], "y", -k) for k in (2, 1, 3)]
 
@@ -319,10 +369,12 @@
         slab = scatter_sum(keep + swapped(send, "c", 1), "y")
         slab, mine = lax.optimization_barrier((slab, mine))
         whole = gather(mine, "y")
-        slab = exact_sum(exact_sum(slab, "x"), "z")
-        half = gather(slab, "y")
-        half, whole = lax.optimization_barrier((half, whole))
-        gram = gather(half, "c")
+        slab = exact_sum(slab, "x")
+        slab = (slab + swapped(slab, "z", 1)) + (swapped(slab, "z", 6) + swapped(slab, "z", 7))
+        slab, whole = lax.optimization_barrier((slab, whole))
+        slab = slab + swapped(slab, "z", 2)
+        gram = gather(gather(slab, "y"), "c")
+        gram, whole = lax.optimization_barrier((gram, whole))
         whole = gather(whole, "c")
         upper, high, low = factorize(gram, feature_total**0.5)
     return (basis_of(whole, high, low), upper)

time: 145 us -> 132 us (0.910)
  Pallas kernels: 33.4 us -> 25.4 us
  waiting for transfers between devices: 45.5 us -> 43.9 us
  starting transfers between devices: 61.8 us -> 60.2 us
    pallas_call x4, Pallas kernels: 22.5 us -> 14.6 us  [the longest x2 7.17 us: cross(): pl.pallas_call(cross_kernel, in_specs=[pl.BlockSpec(memory_space=pltpu.SM...]
    ppermute x24, starting transfers between devices: 47.6 us -> 45.3 us  [shifted(): return lax.ppermute(x, axis, [((i + by) % n, i) for i in range(n)])]
  transfers between devices with their start and end apart: 33 -> 33, of which waited for: 18 -> 19; matrix products, arithmetic and copies ran while one was open for 0% -> 0% of each run, Pallas kernels for 10% -> 10%
where the time goes in v1:
time: 132 us
  starting transfers between devices  60.2 us (46%)
  waiting for transfers between devices  43.9 us (33%)
  Pallas kernels  25.4 us (19%)
    ppermute x24, starting transfers between devices, shifted(): return lax.ppermute(x, axis, [((i + by) % n, i) for i in range(n)])  45.3 us
    ppermute x24, waiting for transfers between devices, shifted(): return lax.ppermute(x, axis, [((i + by) % n, i) for i in range(n)])  38.2 us
    ppermute x9, starting transfers between devices, swapped(): return lax.ppermute(x, axis, [(i ^ mask, i) for i in range(n)])  15 us
    pallas_call x1, Pallas kernels, factorize(): pl.pallas_call(lambda *refs: factor_kernel(scale, *refs), out_shape=[jax....  10 us
    pallas_call x2, Pallas kernels, cross(): pl.pallas_call(cross_kernel, in_specs=[pl.BlockSpec(memory_space=pltpu.SM...  7.17 us
    ppermute x9, waiting for transfers between devices, swapped(): return lax.ppermute(x, axis, [(i ^ mask, i) for i in range(n)])  5.7 us
    pallas_call x1, Pallas kernels, project(): pl.pallas_call(lambda *refs: project_kernel(parts, *refs), in_specs=[pl.B...  5.16 us
  transfers between devices with their start and end apart: 33, of which 19 were waited for; matrix products, arithmetic and copies ran while one was open for 0% of the time, Pallas kernels for 10%

profile of v1, /device:TPU:1, one launch (start us, length us, event | category | flops | bytes accessed | tf_op | source)
XLA Modules:
  0.0 131.8 jit_solution(6947260946164848340)
XLA Ops:
  0.6 5.2 %project.1 = (f32[64,1024]{1,0:T(8,128)S(1)}, bf16[64,1024]{1,0:T(8,128)(2,1)S(1)}, bf16[64,1024]{1,0:T(8,128)(2,1)S(1)}, bf16[64,1024]{1,0:T(8,128)(2,1)S(1)}) custom-call(s32[1]{0:T(128)} %bitcast.2.refs_0_, bf16[512,4096]{1,0:T(8,128)(2,1)} %now_hbm.3, bf16[512,4096]{1,0:T(8,128)(2,1)} %lag_hbm.3, bf16[4096,256]{1,0:T(8,128)(2,1)} %refs_3_.1, ...), custom_call_target="tpu_custom_call" | custom-call | flops 2147483648 | bytes 8388608 | tf_op jit(solution)/shard_map/project/project/pallas_call | solution.py:195
  5.8 3.7 %collective-permute-start = (bf16[64,1024]{1,0:T(8,128)(2,1)S(1)}, bf16[64,1024]{1,0:T(8,128)(2,1)S(1)}, u32[]{:S(2)}, u32[]{:S(2)}) collective-permute-start(bf16[64,1024]{1,0:T(8,128)(2,1)S(1)} %get-tuple-element.22), channel_id=1, source_target_pairs={{2,0},{3,1},{0,2},{1,3},{6,4},{7,5},{4,6},{5,7},{10,8},{11,9},{8,1... | collective-permute-start | bytes 393224 | tf_op jit(solution)/shard_map/project/ppermute | solution.py:16
  9.8 2.4 %collective-permute-start.2 = (bf16[64,1024]{1,0:T(8,128)(2,1)S(1)}, bf16[64,1024]{1,0:T(8,128)(2,1)S(1)}, u32[]{:S(2)}, u32[]{:S(2)}) collective-permute-start(bf16[64,1024]{1,0:T(8,128)(2,1)S(1)} %get-tuple-element.24), channel_id=1, source_target_pairs={{1,0},{2,1},{3,2},{0,3},{5,4},{6,5},{7,6},{4,7},{9,8},{10,9},{11,1... | collective-permute-start | bytes 393224 | tf_op jit(solution)/shard_map/project/ppermute | solution.py:16
  12.2 4.5 %collective-permute-done.1 = bf16[64,1024]{1,0:T(8,128)(2,1)S(1)} collective-permute-done((bf16[64,1024]{1,0:T(8,128)(2,1)S(1)}, bf16[64,1024]{1,0:T(8,128)(2,1)S(1)}, u32[]{:S(2)}, u32[]{:S(2)}) %collective-permute-start.1) | collective-permute-done | bytes 131104 | tf_op jit(solution)/shard_map/project/ppermute | solution.py:16
  17.9 4.0 %collective-permute-start.4 = (bf16[64,1024]{1,0:T(8,128)(2,1)S(1)}, bf16[64,1024]{1,0:T(8,128)(2,1)S(1)}, u32[]{:S(2)}, u32[]{:S(2)}) collective-permute-start(bf16[64,1024]{1,0:T(8,128)(2,1)S(1)} %get-tuple-element.44), channel_id=1, source_target_pairs={{4,0},{8,4},{12,8},{16,12},{20,16},{24,20},{28,24},{0,28},{5,1},{9... | collective-permute-start | bytes 393224 | tf_op jit(solution)/shard_map/project/ppermute | solution.py:16
  21.9 2.6 %collective-permute-done.3 = bf16[64,1024]{1,0:T(8,128)(2,1)S(1)} collective-permute-done((bf16[64,1024]{1,0:T(8,128)(2,1)S(1)}, bf16[64,1024]{1,0:T(8,128)(2,1)S(1)}, u32[]{:S(2)}, u32[]{:S(2)}) %collective-permute-start.3) | collective-permute-done | bytes 131104 | tf_op jit(solution)/shard_map/project/ppermute | solution.py:16
  24.6 3.1 %collective-permute-start.5 = (bf16[64,1024]{1,0:T(8,128)(2,1)S(1)}, bf16[64,1024]{1,0:T(8,128)(2,1)S(1)}, u32[]{:S(2)}, u32[]{:S(2)}) collective-permute-start(bf16[64,1024]{1,0:T(8,128)(2,1)S(1)} %get-tuple-element.46), channel_id=1, source_target_pairs={{12,0},{16,4},{20,8},{24,12},{28,16},{0,20},{4,24},{8,28},{13,1},{... | collective-permute-start | bytes 393224 | tf_op jit(solution)/shard_map/project/ppermute | solution.py:16
  29.2 7.5 %collective-permute-done.5 = bf16[64,1024]{1,0:T(8,128)(2,1)S(1)} collective-permute-done((bf16[64,1024]{1,0:T(8,128)(2,1)S(1)}, bf16[64,1024]{1,0:T(8,128)(2,1)S(1)}, u32[]{:S(2)}, u32[]{:S(2)}) %collective-permute-start.5) | collective-permute-done | bytes 131104 | tf_op jit(solution)/shard_map/project/ppermute | solution.py:16
  37.0 4.9 %collective-permute-start.8 = (bf16[64,1024]{1,0:T(8,128)(2,1)S(1)}, bf16[64,1024]{1,0:T(8,128)(2,1)S(1)}, u32[]{:S(2)}, u32[]{:S(2)}) collective-permute-start(bf16[64,1024]{1,0:T(8,128)(2,1)S(1)} %get-tuple-element.43), channel_id=1, source_target_pairs={{1,0},{2,1},{3,2},{0,3},{5,4},{6,5},{7,6},{4,7},{9,8},{10,9},{11,1... | collective-permute-start | bytes 393224 | tf_op jit(solution)/shard_map/project/ppermute | solution.py:16
  43.9 3.3 %collective-permute-done.9 = bf16[64,1024]{1,0:T(8,128)(2,1)S(1)} collective-permute-done((bf16[64,1024]{1,0:T(8,128)(2,1)S(1)}, bf16[64,1024]{1,0:T(8,128)(2,1)S(1)}, u32[]{:S(2)}, u32[]{:S(2)}) %collective-permute-start.9) | collective-permute-done | bytes 131104 | tf_op jit(solution)/shard_map/project/ppermute | solution.py:16
  47.2 3.6 %cross.3 = bf16[4,256,512]{2,1,0:T(8,128)(2,1)S(1)} custom-call(s32[2]{0:T(128)S(1)} %pad_add_fusion.1.where_ref, bf16[256,1024]{1,0:T(8,128)(2,1)S(1)} %constant_dynamic-update-slice_fusion.12.proj_ref, bf16[512,4096]{1,0:T(8,128)(2,1)} %now_hbm.3, bf16[512,4096]{1,0:T(8,128)(2,1)} %lag_hbm.3, f32[1,4096]{1,0:T(1,128)S(1)} %bitcast.6), custom_call_target="tpu_custom_call" | custom-call | flops 1073741824 | bytes 4194304 | tf_op jit(solution)/shard_map/sketch/cross/pallas_call | solution.py:247
  50.8 2.7 %collective-permute-start.10 = (bf16[4,256,512]{2,1,0:T(8,128)(2,1)S(1)}, bf16[4,256,512]{2,1,0:T(8,128)(2,1)S(1)}, u32[]{:S(2)}, u32[]{:S(2)}) collective-permute-start(bf16[4,256,512]{2,1,0:T(8,128)(2,1)S(1)} %cross.3), channel_id=1, source_target_pairs={{32,0},{0,32},{33,1},{1,33},{34,2},{2,34},{35,3},{3,35},{36,4},{4,... | collective-permute-start | bytes 3145736 | tf_op jit(solution)/shard_map/sketch/ppermute | solution.py:21
  53.6 3.6 %cross.2.own_ref = f32[4,256,512]{2,1,0:T(8,128)S(1)} custom-call(s32[2]{0:T(128)S(1)} %pad_add_fusion.where_ref, bf16[256,1024]{1,0:T(8,128)(2,1)S(1)} %constant_dynamic-update-slice_fusion.12.proj_ref, bf16[512,4096]{1,0:T(8,128)(2,1)} %now_hbm.3, bf16[512,4096]{1,0:T(8,128)(2,1)} %lag_hbm.3, f32[1,4096]{1,0:T(1,128)S(1)} %bitcast.7), custom_call_target="tpu_custom_call" | custom-call | flops 1073741824 | bytes 4194304 | tf_op jit(solution)/shard_map/sketch/cross/pallas_call | solution.py:247
  57.3 3.0 %collective-permute-start.11 = (bf16[256,512]{1,0:T(8,128)(2,1)S(1)}, bf16[256,512]{1,0:T(8,128)(2,1)S(1)}, u32[]{:S(2)}, u32[]{:S(2)}) collective-permute-start(bf16[256,512]{1,0:T(8,128)(2,1)S(1)} %get-tuple-element.25), channel_id=1, source_target_pairs={{128,0},{192,64},{0,128},{64,192},{129,1},{193,65},{1,129},{65,193... | collective-permute-start | bytes 786440 | tf_op jit(solution)/shard_map/sketch/ppermute | solution.py:16
  60.7 2.3 %collective-permute-start.13 = (bf16[256,512]{1,0:T(8,128)(2,1)S(1)}, bf16[256,512]{1,0:T(8,128)(2,1)S(1)}, u32[]{:S(2)}, u32[]{:S(2)}) collective-permute-start(bf16[256,512]{1,0:T(8,128)(2,1)S(1)} %get-tuple-element.27), channel_id=1, source_target_pairs={{64,0},{128,64},{192,128},{0,192},{65,1},{129,65},{193,129},{1,193... | collective-permute-start | bytes 786440 | tf_op jit(solution)/shard_map/sketch/ppermute | solution.py:16
  63.0 3.9 %collective-permute-done.11.a_ref = bf16[256,512]{1,0:T(8,128)(2,1)S(1)} collective-permute-done((bf16[256,512]{1,0:T(8,128)(2,1)S(1)}, bf16[256,512]{1,0:T(8,128)(2,1)S(1)}, u32[]{:S(2)}, u32[]{:S(2)}) %collective-permute-start.11) | collective-permute-done | bytes 262176 | tf_op jit(solution)/shard_map/sketch/ppermute | solution.py:16
  66.9 5.9 %collective-permute-done.12.b_ref = bf16[256,512]{1,0:T(8,128)(2,1)S(1)} collective-permute-done((bf16[256,512]{1,0:T(8,128)(2,1)S(1)}, bf16[256,512]{1,0:T(8,128)(2,1)S(1)}, u32[]{:S(2)}, u32[]{:S(2)}) %collective-permute-start.12) | collective-permute-done | bytes 262176 | tf_op jit(solution)/shard_map/sketch/ppermute | solution.py:16
  81.4 2.2 %collective-permute-start.19 = (f32[32,256]{1,0:T(8,128)S(1)}, f32[32,256]{1,0:T(8,128)S(1)}, u32[]{:S(2)}, u32[]{:S(2)}) collective-permute-start(f32[32,256]{1,0:T(8,128)S(1)} %add_add_fusion.2), channel_id=1, source_target_pairs={{2,0},{3,1},{0,2},{1,3},{6,4},{7,5},{4,6},{5,7},{10,8},{11,9},{8,1... | collective-permute-start | bytes 98312 | tf_op jit(solution)/shard_map/gram/ppermute | solution.py:21
  88.1 4.0 %collective-permute-start.22 = (f32[32,256]{1,0:T(8,128)S(1)}, f32[32,256]{1,0:T(8,128)S(1)}, u32[]{:S(2)}, u32[]{:S(2)}) collective-permute-start(f32[32,256]{1,0:T(8,128)S(1)} %add_add_fusion.1), channel_id=1, source_target_pairs={{24,0},{28,4},{16,8},{20,12},{8,16},{12,20},{0,24},{4,28},{25,1},{... | collective-permute-start | bytes 98312 | tf_op jit(solution)/shard_map/gram/ppermute | solution.py:21
  96.1 3.0 %collective-permute-done.25 = bf16[512,256]{1,0:T(8,128)(2,1)S(1)} collective-permute-done((bf16[512,256]{1,0:T(8,128)(2,1)S(1)}, bf16[512,256]{1,0:T(8,128)(2,1)S(1)}, u32[]{:S(2)}, u32[]{:S(2)}) %collective-permute-start.25) | collective-permute-done | bytes 262176 | tf_op jit(solution)/shard_map/gram/ppermute | solution.py:16
  99.1 3.3 %collective-permute-start.27 = (f32[32,256]{1,0:T(8,128)S(1)}, f32[32,256]{1,0:T(8,128)S(1)}, u32[]{:S(2)}, u32[]{:S(2)}) collective-permute-start(f32[32,256]{1,0:T(8,128)S(1)} %add_add_fusion), channel_id=1, source_target_pairs={{8,0},{12,4},{0,8},{4,12},{24,16},{28,20},{16,24},{20,28},{9,1},{1... | collective-permute-start | bytes 98312 | tf_op jit(solution)/shard_map/gram/ppermute | solution.py:21
  111.1 6.5 %collective-permute-start.31 = (f32[128,256]{1,0:T(8,128)S(1)}, f32[128,256]{1,0:T(8,128)S(1)}, u32[]{:S(2)}, u32[]{:S(2)}) collective-permute-start(f32[128,256]{1,0:T(8,128)S(1)} %constant_dynamic-update-slice_fusion.4), channel_id=1, source_target_pairs={{32,0},{0,32},{33,1},{1,33},{34,2},{2,34},{35,3},{3,35},{36,4},{4,... | collective-permute-start | bytes 393224 | tf_op jit(solution)/shard_map/gram/ppermute | solution.py:16
  119.1 10.0 %factorize.1 = (f32[256,256]{1,0:T(8,128)}, bf16[256,256]{1,0:T(8,128)(2,1)S(1)}, bf16[256,256]{1,0:T(8,128)(2,1)S(1)}) custom-call(f32[256,256]{1,0:T(8,128)S(1)} %constant_dynamic-update-slice_fusion.2.refs_0_), custom_call_target="tpu_custom_call" | custom-call | flops 201326592 | bytes 524288 | tf_op jit(solution)/shard_map/gram/factorize/pallas_call | solution.py:125
  129.4 2.2 %basis.1 = bf16[4096,256]{1,0:T(8,128)(2,1)} custom-call(bf16[4096,256]{1,0:T(8,128)(2,1)S(1)} %constant_dynamic-update-slice_fusion.refs_0_, bf16[256,256]{1,0:T(8,128)(2,1)S(1)} %get-tuple-element.37.refs_1_, bf16[256,256]{1,0:T(8,128)(2,1)S(1)} %get-tuple-element.38.refs_2_), custom_call_target="tpu_custom_call" | custom-call | flops 1073741824 | bytes 4194304 | tf_op jit(solution)/shard_map/basis/pallas_call | solution.py:330
  (82 shorter events, 33.3 us)
Async XLA Ops:
  5.8 6.3 %collective-permute-start = (bf16[64,1024]{1,0:T(8,128)(2,1)S(1)}, bf16[64,1024]{1,0:T(8,128)(2,1)S(1)}, u32[]{:S(2)}, u32[]{:S(2)}) collective-permute-start(bf16[64,1024]{1,0:T(8,128)(2,1)S(1)} %get-tuple-element.22), channel_id=1, source_target_pairs={{2,0},{3,1},{0,2},{1,3},{6,4},{7,5},{4,6},{5,7},{10,8},{11,9},{8,1... | collective-permute-start | bytes 393224 | tf_op jit(solution)/shard_map/project/ppermute | solution.py:16
  9.5 7.2 %collective-permute-start.1 = (bf16[64,1024]{1,0:T(8,128)(2,1)S(1)}, bf16[64,1024]{1,0:T(8,128)(2,1)S(1)}, u32[]{:S(2)}, u32[]{:S(2)}) collective-permute-start(bf16[64,1024]{1,0:T(8,128)(2,1)S(1)} %get-tuple-element.23), channel_id=1, source_target_pairs={{3,0},{0,1},{1,2},{2,3},{7,4},{4,5},{5,6},{6,7},{11,8},{8,9},{9,10... | collective-permute-start | bytes 393224 | tf_op jit(solution)/shard_map/project/ppermute | solution.py:16
  9.8 6.9 %collective-permute-start.2 = (bf16[64,1024]{1,0:T(8,128)(2,1)S(1)}, bf16[64,1024]{1,0:T(8,128)(2,1)S(1)}, u32[]{:S(2)}, u32[]{:S(2)}) collective-permute-start(bf16[64,1024]{1,0:T(8,128)(2,1)S(1)} %get-tuple-element.24), channel_id=1, source_target_pairs={{1,0},{2,1},{3,2},{0,3},{5,4},{6,5},{7,6},{4,7},{9,8},{10,9},{11,1... | collective-permute-start | bytes 393224 | tf_op jit(solution)/shard_map/project/ppermute | solution.py:16
  16.7 7.8 %collective-permute-start.3 = (bf16[64,1024]{1,0:T(8,128)(2,1)S(1)}, bf16[64,1024]{1,0:T(8,128)(2,1)S(1)}, u32[]{:S(2)}, u32[]{:S(2)}) collective-permute-start(bf16[64,1024]{1,0:T(8,128)(2,1)S(1)} %get-tuple-element.44), channel_id=1, source_target_pairs={{28,0},{0,4},{4,8},{8,12},{12,16},{16,20},{20,24},{24,28},{29,1},{... | collective-permute-start | bytes 393224 | tf_op jit(solution)/shard_map/project/ppermute | solution.py:16
  17.9 6.6 %collective-permute-start.4 = (bf16[64,1024]{1,0:T(8,128)(2,1)S(1)}, bf16[64,1024]{1,0:T(8,128)(2,1)S(1)}, u32[]{:S(2)}, u32[]{:S(2)}) collective-permute-start(bf16[64,1024]{1,0:T(8,128)(2,1)S(1)} %get-tuple-element.44), channel_id=1, source_target_pairs={{4,0},{8,4},{12,8},{16,12},{20,16},{24,20},{28,24},{0,28},{5,1},{9... | collective-permute-start | bytes 393224 | tf_op jit(solution)/shard_map/project/ppermute | solution.py:16
  24.6 12.1 %collective-permute-start.5 = (bf16[64,1024]{1,0:T(8,128)(2,1)S(1)}, bf16[64,1024]{1,0:T(8,128)(2,1)S(1)}, u32[]{:S(2)}, u32[]{:S(2)}) collective-permute-start(bf16[64,1024]{1,0:T(8,128)(2,1)S(1)} %get-tuple-element.46), channel_id=1, source_target_pairs={{12,0},{16,4},{20,8},{24,12},{28,16},{0,20},{4,24},{8,28},{13,1},{... | collective-permute-start | bytes 393224 | tf_op jit(solution)/shard_map/project/ppermute | solution.py:16
  27.7 9.0 %collective-permute-start.6 = (bf16[64,1024]{1,0:T(8,128)(2,1)S(1)}, bf16[64,1024]{1,0:T(8,128)(2,1)S(1)}, u32[]{:S(2)}, u32[]{:S(2)}) collective-permute-start(bf16[64,1024]{1,0:T(8,128)(2,1)S(1)} %get-tuple-element.47), channel_id=1, source_target_pairs={{24,0},{28,4},{0,8},{4,12},{8,16},{12,20},{16,24},{20,28},{25,1},{... | collective-permute-start | bytes 393224 | tf_op jit(solution)/shard_map/project/ppermute | solution.py:16
  36.9 5.4 %collective-permute-start.7 = (bf16[64,1024]{1,0:T(8,128)(2,1)S(1)}, bf16[64,1024]{1,0:T(8,128)(2,1)S(1)}, u32[]{:S(2)}, u32[]{:S(2)}) collective-permute-start(bf16[64,1024]{1,0:T(8,128)(2,1)S(1)} %get-tuple-element.43), channel_id=1, source_target_pairs={{2,0},{3,1},{0,2},{1,3},{6,4},{7,5},{4,6},{5,7},{10,8},{11,9},{8,1... | collective-permute-start | bytes 393224 | tf_op jit(solution)/shard_map/project/ppermute | solution.py:16
  37.0 6.9 %collective-permute-start.8 = (bf16[64,1024]{1,0:T(8,128)(2,1)S(1)}, bf16[64,1024]{1,0:T(8,128)(2,1)S(1)}, u32[]{:S(2)}, u32[]{:S(2)}) collective-permute-start(bf16[64,1024]{1,0:T(8,128)(2,1)S(1)} %get-tuple-element.43), channel_id=1, source_target_pairs={{1,0},{2,1},{3,2},{0,3},{5,4},{6,5},{7,6},{4,7},{9,8},{10,9},{11,1... | collective-permute-start | bytes 393224 | tf_op jit(solution)/shard_map/project/ppermute | solution.py:16
  42.0 5.1 %collective-permute-start.9 = (bf16[64,1024]{1,0:T(8,128)(2,1)S(1)}, bf16[64,1024]{1,0:T(8,128)(2,1)S(1)}, u32[]{:S(2)}, u32[]{:S(2)}) collective-permute-start(bf16[64,1024]{1,0:T(8,128)(2,1)S(1)} %get-tuple-element.43), channel_id=1, source_target_pairs={{3,0},{0,1},{1,2},{2,3},{7,4},{4,5},{5,6},{6,7},{11,8},{8,9},{9,10... | collective-permute-start | bytes 393224 | tf_op jit(solution)/shard_map/project/ppermute | solution.py:16
  50.8 6.4 %collective-permute-start.10 = (bf16[4,256,512]{2,1,0:T(8,128)(2,1)S(1)}, bf16[4,256,512]{2,1,0:T(8,128)(2,1)S(1)}, u32[]{:S(2)}, u32[]{:S(2)}) collective-permute-start(bf16[4,256,512]{2,1,0:T(8,128)(2,1)S(1)} %cross.3), channel_id=1, source_target_pairs={{32,0},{0,32},{33,1},{1,33},{34,2},{2,34},{35,3},{3,35},{36,4},{4,... | collective-permute-start | bytes 3145736 | tf_op jit(solution)/shard_map/sketch/ppermute | solution.py:21
  57.3 9.6 %collective-permute-start.11 = (bf16[256,512]{1,0:T(8,128)(2,1)S(1)}, bf16[256,512]{1,0:T(8,128)(2,1)S(1)}, u32[]{:S(2)}, u32[]{:S(2)}) collective-permute-start(bf16[256,512]{1,0:T(8,128)(2,1)S(1)} %get-tuple-element.25), channel_id=1, source_target_pairs={{128,0},{192,64},{0,128},{64,192},{129,1},{193,65},{1,129},{65,193... | collective-permute-start | bytes 786440 | tf_op jit(solution)/shard_map/sketch/ppermute | solution.py:16
  60.3 12.4 %collective-permute-start.12 = (bf16[256,512]{1,0:T(8,128)(2,1)S(1)}, bf16[256,512]{1,0:T(8,128)(2,1)S(1)}, u32[]{:S(2)}, u32[]{:S(2)}) collective-permute-start(bf16[256,512]{1,0:T(8,128)(2,1)S(1)} %get-tuple-element.26), channel_id=1, source_target_pairs={{192,0},{0,64},{64,128},{128,192},{193,1},{1,65},{65,129},{129,193... | collective-permute-start | bytes 786440 | tf_op jit(solution)/shard_map/sketch/ppermute | solution.py:16
  60.7 12.1 %collective-permute-start.13 = (bf16[256,512]{1,0:T(8,128)(2,1)S(1)}, bf16[256,512]{1,0:T(8,128)(2,1)S(1)}, u32[]{:S(2)}, u32[]{:S(2)}) collective-permute-start(bf16[256,512]{1,0:T(8,128)(2,1)S(1)} %get-tuple-element.27), channel_id=1, source_target_pairs={{64,0},{128,64},{192,128},{0,192},{65,1},{129,65},{193,129},{1,193... | collective-permute-start | bytes 786440 | tf_op jit(solution)/shard_map/sketch/ppermute | solution.py:16
  75.5 4.5 %collective-permute-start.15 = (f32[32,256]{1,0:T(8,128)S(1)}, f32[32,256]{1,0:T(8,128)S(1)}, u32[]{:S(2)}, u32[]{:S(2)}) collective-permute-start(f32[32,256]{1,0:T(8,128)S(1)} %get-tuple-element.48), channel_id=1, source_target_pairs={{128,0},{192,64},{0,128},{64,192},{129,1},{193,65},{1,129},{65,193... | collective-permute-start | bytes 98312 | tf_op jit(solution)/shard_map/gram/ppermute | solution.py:16
  81.3 6.6 %collective-permute-start.18 = (f32[32,256]{1,0:T(8,128)S(1)}, f32[32,256]{1,0:T(8,128)S(1)}, u32[]{:S(2)}, u32[]{:S(2)}) collective-permute-start(f32[32,256]{1,0:T(8,128)S(1)} %add_add_fusion.2), channel_id=1, source_target_pairs={{1,0},{0,1},{3,2},{2,3},{5,4},{4,5},{7,6},{6,7},{9,8},{8,9},{11,10... | collective-permute-start | bytes 98312 | tf_op jit(solution)/shard_map/gram/ppermute | solution.py:21
  81.4 6.5 %collective-permute-start.19 = (f32[32,256]{1,0:T(8,128)S(1)}, f32[32,256]{1,0:T(8,128)S(1)}, u32[]{:S(2)}, u32[]{:S(2)}) collective-permute-start(f32[32,256]{1,0:T(8,128)S(1)} %add_add_fusion.2), channel_id=1, source_target_pairs={{2,0},{3,1},{0,2},{1,3},{6,4},{7,5},{4,6},{5,7},{10,8},{11,9},{8,1... | collective-permute-start | bytes 98312 | tf_op jit(solution)/shard_map/gram/ppermute | solution.py:21
  85.3 10.8 %collective-permute-start.24 = (bf16[512,256]{1,0:T(8,128)(2,1)S(1)}, bf16[512,256]{1,0:T(8,128)(2,1)S(1)}, u32[]{:S(2)}, u32[]{:S(2)}) collective-permute-start(bf16[512,256]{1,0:T(8,128)(2,1)S(1)} %get-tuple-element.32), channel_id=1, source_target_pairs={{128,0},{192,64},{0,128},{64,192},{129,1},{193,65},{1,129},{65,193... | collective-permute-start | bytes 786440 | tf_op jit(solution)/shard_map/gram/ppermute | solution.py:16
  87.0 12.0 %collective-permute-start.25 = (bf16[512,256]{1,0:T(8,128)(2,1)S(1)}, bf16[512,256]{1,0:T(8,128)(2,1)S(1)}, u32[]{:S(2)}, u32[]{:S(2)}) collective-permute-start(bf16[512,256]{1,0:T(8,128)(2,1)S(1)} %get-tuple-element.32), channel_id=1, source_target_pairs={{64,0},{128,64},{192,128},{0,192},{65,1},{129,65},{193,129},{1,193... | collective-permute-start | bytes 786440 | tf_op jit(solution)/shard_map/gram/ppermute | solution.py:16
  88.1 5.9 %collective-permute-start.22 = (f32[32,256]{1,0:T(8,128)S(1)}, f32[32,256]{1,0:T(8,128)S(1)}, u32[]{:S(2)}, u32[]{:S(2)}) collective-permute-start(f32[32,256]{1,0:T(8,128)S(1)} %add_add_fusion.1), channel_id=1, source_target_pairs={{24,0},{28,4},{16,8},{20,12},{8,16},{12,20},{0,24},{4,28},{25,1},{... | collective-permute-start | bytes 98312 | tf_op jit(solution)/shard_map/gram/ppermute | solution.py:21
  92.2 6.9 %collective-permute-start.26 = (bf16[512,256]{1,0:T(8,128)(2,1)S(1)}, bf16[512,256]{1,0:T(8,128)(2,1)S(1)}, u32[]{:S(2)}, u32[]{:S(2)}) collective-permute-start(bf16[512,256]{1,0:T(8,128)(2,1)S(1)} %get-tuple-element.32), channel_id=1, source_target_pairs={{192,0},{0,64},{64,128},{128,192},{193,1},{1,65},{65,129},{129,193... | collective-permute-start | bytes 786440 | tf_op jit(solution)/shard_map/gram/ppermute | solution.py:16
  99.1 4.8 %collective-permute-start.27 = (f32[32,256]{1,0:T(8,128)S(1)}, f32[32,256]{1,0:T(8,128)S(1)}, u32[]{:S(2)}, u32[]{:S(2)}) collective-permute-start(f32[32,256]{1,0:T(8,128)S(1)} %add_add_fusion), channel_id=1, source_target_pairs={{8,0},{12,4},{0,8},{4,12},{24,16},{28,20},{16,24},{20,28},{9,1},{1... | collective-permute-start | bytes 98312 | tf_op jit(solution)/shard_map/gram/ppermute | solution.py:21
  111.1 7.5 %collective-permute-start.31 = (f32[128,256]{1,0:T(8,128)S(1)}, f32[128,256]{1,0:T(8,128)S(1)}, u32[]{:S(2)}, u32[]{:S(2)}) collective-permute-start(f32[128,256]{1,0:T(8,128)S(1)} %constant_dynamic-update-slice_fusion.4), channel_id=1, source_target_pairs={{32,0},{0,32},{33,1},{1,33},{34,2},{2,34},{35,3},{3,35},{36,4},{4,... | collective-permute-start | bytes 393224 | tf_op jit(solution)/shard_map/gram/ppermute | solution.py:16
  118.6 10.7 %collective-permute-start.32 = (bf16[2048,256]{1,0:T(8,128)(2,1)S(1)}, bf16[2048,256]{1,0:T(8,128)(2,1)S(1)}, u32[]{:S(2)}, u32[]{:S(2)}) collective-permute-start(bf16[2048,256]{1,0:T(8,128)(2,1)S(1)} %constant_dynamic-update-slice_fusion.8), channel_id=1, source_target_pairs={{32,0},{0,32},{33,1},{1,33},{34,2},{2,34},{35,3},{3,35},{36,4},{4,... | collective-permute-start | bytes 3145736 | tf_op jit(solution)/shard_map/gram/ppermute | solution.py:16
  (10 other events, 65.0 us)

commit v2 on v1

--- a/solution.py
+++ b/solution.py
@@ -213,74 +213,84 @@
     )(me[None], in_hbm(frames_now), in_hbm(frames_lag), in_hbm(test_matrix), in_hbm(scale))
 
 
-def cross_kernel(where_ref, proj_ref, now_hbm, lag_hbm, factor_ref, out_ref, work, sems):
+def cross_kernel(jobs, where_ref, proj_ref, now_hbm, lag_hbm, factor_ref, *refs):
+    *out_refs, work, sems = refs
     frames = now_hbm.shape[0]
-    count, _, block = out_ref.shape
+    block = out_refs[0].shape[2]
+    count = now_hbm.shape[1] // (2 * block)
+    places = []
     copies = []
-    for k in range(count):
-        first = where_ref[0] * count + lax.rem(where_ref[1] + k, count)
+    for n, (_, _, other, slot) in enumerate(jobs):
+        half = 1 - where_ref[0] if other else where_ref[0]
+        first = half * count + lax.rem(where_ref[1] + slot, count)
         at = pl.ds(pl.multiple_of(first * block, block), block)
+        places.append(at)
         copies.append(
             [
-                pltpu.make_async_copy(now_hbm.at[:, at], work.at[k, pl.ds(0, frames)], sems.at[2 * k]),
-                pltpu.make_async_copy(lag_hbm.at[:, at], work.at[k, pl.ds(frames, frames)], sems.at[2 * k + 1]),
+                pltpu.make_async_copy(now_hbm.at[:, at], work.at[n, pl.ds(0, frames)], sems.at[2 * n]),
+                pltpu.make_async_copy(lag_hbm.at[:, at], work.at[n, pl.ds(frames, frames)], sems.at[2 * n + 1]),
             ]
         )
         for copy in copies[-1]:
             copy.start()
     proj = jnp.concatenate([proj_ref[:, frames:], proj_ref[:, :frames]], axis=1)
-    for k in range(count):
-        for copy in copies[k]:
+    for n, (out, row, _, _) in enumerate(jobs):
+        for copy in copies[n]:
             copy.wait()
-        first = where_ref[0] * count + lax.rem(where_ref[1] + k, count)
-        total = jnp.dot(proj, work[k], preferred_element_type=F32)
-        factor = factor_ref[:, pl.ds(pl.multiple_of(first * block, block), block)]
-        out_ref[k] = (total * factor).astype(out_ref.dtype)
-
-
-def cross(half, first, count, proj, frames_now, frames_lag, factor, dtype):
+        total = jnp.dot(proj, work[n], preferred_element_type=F32)
+        out_refs[out][row] = (total * factor_ref[:, places[n]]).astype(out_refs[out].dtype)
+
+
+def cross(core, ring_place, ring, slots_other, slots_own, proj, frames_now, frames_lag, factor):
     frames, features = frames_now.shape
     columns = proj.shape[0]
-    block = features // (2 * count)
+    block = features // (2 * ring)
+    jobs, out_shape = [], []
+    for slots, other, dtype in ((slots_other, True, BF16), (slots_own, False, F32)):
+        if slots:
+            jobs += [(len(out_shape), row, other, slot) for row, slot in enumerate(slots)]
+            out_shape.append(jax.ShapeDtypeStruct((len(slots), columns, block), dtype))
     vmem = pl.BlockSpec(memory_space=pltpu.VMEM)
     hbm = pl.BlockSpec(memory_space=pl.ANY)
     return pl.pallas_call(
-        cross_kernel,
+        lambda *refs: cross_kernel(jobs, *refs),
         in_specs=[pl.BlockSpec(memory_space=pltpu.SMEM), vmem, hbm, hbm, vmem],
-        out_specs=vmem,
-        out_shape=jax.ShapeDtypeStruct((count, columns, block), dtype),
+        out_specs=[vmem] * len(out_shape),
+        out_shape=out_shape,
         scratch_shapes=[
-            pltpu.VMEM((count, 2 * frames, block), BF16),
-            pltpu.SemaphoreType.DMA((2 * count,)),
+            pltpu.VMEM((len(jobs), 2 * frames, block), BF16),
+            pltpu.SemaphoreType.DMA((2 * len(jobs),)),
         ],
         compiler_params=pltpu.CompilerParams(vmem_limit_bytes=24 * 2**20),
         cost_estimate=pl.CostEstimate(
-            flops=2 * frames * features * columns, bytes_accessed=2 * frames * features, transcendentals=0
+            flops=4 * frames * len(jobs) * block * columns,
+            bytes_accessed=4 * frames * len(jobs) * block,
+            transcendentals=0,
         ),
         name="cross",
-    )(jnp.stack([half, first]), proj, in_hbm(frames_now), in_hbm(frames_lag), factor)
+    )(jnp.stack([core, ring_place]), proj, in_hbm(frames_now), in_hbm(frames_lag), factor)
 
 
 def combine_kernel(own_ref, came_ref, *out_refs):
     for k, out_ref in enumerate(out_refs):
-        out_ref[...] = (own_ref[k + 1] + came_ref[k + 1].astype(F32)).astype(BF16)
-
-
-def combine(own, came):
-    count, columns, block = own.shape
+        out_ref[...] = (own_ref[k] + came_ref[k].astype(F32)).astype(BF16)
+
+
+def combine(own, came, count):
+    _, columns, block = own.shape
     whole = pl.BlockSpec(memory_space=pltpu.VMEM)
     return pl.pallas_call(
         combine_kernel,
         in_specs=[whole] * 2,
-        out_specs=[whole] * (count - 1),
-        out_shape=[jax.ShapeDtypeStruct((columns, block), BF16)] * (count - 1),
+        out_specs=[whole] * count,
+        out_shape=[jax.ShapeDtypeStruct((columns, block), BF16)] * count,
         compiler_params=pltpu.CompilerParams(vmem_limit_bytes=16 * 2**20),
         name="combine",
     )(own, came)
 
 
 def gram_kernel(core_ref, own_ref, came_ref, a_ref, b_ref, d_ref, keep_ref, send_ref, rows_ref, work):
-    total = own_ref[0] + came_ref[0].astype(F32)
+    total = own_ref[own_ref.shape[0] - 1] + came_ref[own_ref.shape[0] - 1].astype(F32)
     total = total + (a_ref[...].astype(F32) + b_ref[...].astype(F32) + d_ref[...].astype(F32))
     half = keep_ref.shape[0]
     core = core_ref[0]
@@ -359,10 +369,18 @@
     with jax.named_scope("sketch"):
         y = lax.axis_index("y")
         c = lax.axis_index("c")
-        came = swapped(cross(1 - c, y, ring, proj, frames_now, frames_lag, factor, BF16), "c", 1)
-        own = cross(c, y, ring, proj, frames_now, frames_lag, factor, F32)
-        pieces = combine(own, came)
-        others = [shifted(pieces[k - 1], "y", -k) for k in (2, 1, 3)]
+        terms = (frames_now, frames_lag, factor)
+        send, own = cross(c, y, ring, (2,), (2,), proj, *terms)
+        send, proj = lax.optimization_barrier((send, proj))
+        came = swapped(send, "c", 1)
+        (send,) = cross(c, y, ring, (1, 3, 0), (), proj, *terms)
+        (piece,) = combine(own, came, 1)
+        others = [shifted(piece, "y", -2)]
+        came = swapped(send, "c", 1)
+        proj, piece = lax.optimization_barrier((proj, piece))
+        (own,) = cross(c, y, ring, (), (1, 3, 0), proj, *terms)
+        pieces = combine(own, came, 2)
+        others += [shifted(pieces[0], "y", -1), shifted(pieces[1], "y", -3)]
 
     with jax.named_scope("gram"):
         keep, send, mine = gram_of(c[None], own, came, others)

time: 132 us -> 133 us (level)
  Pallas kernels: 25.4 us -> 27.2 us
  waiting for transfers between devices: 43.9 us -> 42.2 us
    ppermute x24, waiting for transfers between devices: 38.2 us -> 34.5 us  [shifted(): return lax.ppermute(x, axis, [((i + by) % n, i) for i in range(n)])]
    ppermute x9 -> x10, waiting for transfers between devices: 5.7 us -> 7.7 us  [swapped(): return lax.ppermute(x, axis, [(i ^ mask, i) for i in range(n)])]
    pallas_call x2 -> x3, Pallas kernels: 7.17 us -> 8.93 us  [cross(): pl.pallas_call(lambda *refs: cross_kernel(jobs, *refs), in_specs=[pl.Bloc...]
    ppermute x9 -> x10, starting transfers between devices: 15 us -> 15.5 us  [swapped(): return lax.ppermute(x, axis, [(i ^ mask, i) for i in range(n)])]
  transfers between devices with their start and end apart: 33 -> 34, of which waited for: 19 -> 20; matrix products, arithmetic and copies ran while one was open for 0% -> 0% of each run, Pallas kernels for 10% -> 10%
where the time goes in v2:
time: 133 us
  starting transfers between devices  61.5 us (46%)
  waiting for transfers between devices  42.2 us (32%)
  Pallas kernels  27.2 us (20%)
    ppermute x24, starting transfers between devices, shifted(): return lax.ppermute(x, axis, [((i + by) % n, i) for i in range(n)])  46 us
    ppermute x24, waiting for transfers between devices, shifted(): return lax.ppermute(x, axis, [((i + by) % n, i) for i in range(n)])  34.5 us
    ppermute x10, starting transfers between devices, swapped(): return lax.ppermute(x, axis, [(i ^ mask, i) for i in range(n)])  15.5 us
    pallas_call x1, Pallas kernels, factorize(): pl.pallas_call(lambda *refs: factor_kernel(scale, *refs), out_shape=[jax....  10 us
    pallas_call x3, Pallas kernels, cross(): pl.pallas_call(lambda *refs: cross_kernel(jobs, *refs), in_specs=[pl.Bloc...  8.93 us
    ppermute x10, waiting for transfers between devices, swapped(): return lax.ppermute(x, axis, [(i ^ mask, i) for i in range(n)])  7.7 us
    pallas_call x1, Pallas kernels, project(): pl.pallas_call(lambda *refs: project_kernel(parts, *refs), in_specs=[pl.B...  5.16 us
  transfers between devices with their start and end apart: 34, of which 20 were waited for; matrix products, arithmetic and copies ran while one was open for 0% of the time, Pallas kernels for 10%

profile of v2, /device:TPU:1, one launch (start us, length us, event | category | flops | bytes accessed | tf_op | source)
XLA Modules:
  0.0 133.0 jit_solution(17586109365042186265)
XLA Ops:
  0.6 5.2 %project.1 = (f32[64,1024]{1,0:T(8,128)S(1)}, bf16[64,1024]{1,0:T(8,128)(2,1)S(1)}, bf16[64,1024]{1,0:T(8,128)(2,1)S(1)}, bf16[64,1024]{1,0:T(8,128)(2,1)S(1)}) custom-call(s32[1]{0:T(128)} %bitcast.2.refs_0_, bf16[512,4096]{1,0:T(8,128)(2,1)} %refs_2_.7, bf16[512,4096]{1,0:T(8,128)(2,1)} %refs_3_.7, bf16[4096,256]{1,0:T(8,128)(2,1)} %refs_3_.4, ...), custom_call_target="tpu_custom_call" | custom-call | flops 2147483648 | bytes 8388608 | tf_op jit(solution)/shard_map/project/project/pallas_call | solution.py:195
  5.8 3.7 %collective-permute-start = (bf16[64,1024]{1,0:T(8,128)(2,1)S(1)}, bf16[64,1024]{1,0:T(8,128)(2,1)S(1)}, u32[]{:S(2)}, u32[]{:S(2)}) collective-permute-start(bf16[64,1024]{1,0:T(8,128)(2,1)S(1)} %get-tuple-element.26), channel_id=1, source_target_pairs={{2,0},{3,1},{0,2},{1,3},{6,4},{7,5},{4,6},{5,7},{10,8},{11,9},{8,1... | collective-permute-start | bytes 393224 | tf_op jit(solution)/shard_map/project/ppermute | solution.py:16
  9.8 2.4 %collective-permute-start.2 = (bf16[64,1024]{1,0:T(8,128)(2,1)S(1)}, bf16[64,1024]{1,0:T(8,128)(2,1)S(1)}, u32[]{:S(2)}, u32[]{:S(2)}) collective-permute-start(bf16[64,1024]{1,0:T(8,128)(2,1)S(1)} %get-tuple-element.28), channel_id=1, source_target_pairs={{1,0},{2,1},{3,2},{0,3},{5,4},{6,5},{7,6},{4,7},{9,8},{10,9},{11,1... | collective-permute-start | bytes 393224 | tf_op jit(solution)/shard_map/project/ppermute | solution.py:16
  12.2 4.5 %collective-permute-done.1 = bf16[64,1024]{1,0:T(8,128)(2,1)S(1)} collective-permute-done((bf16[64,1024]{1,0:T(8,128)(2,1)S(1)}, bf16[64,1024]{1,0:T(8,128)(2,1)S(1)}, u32[]{:S(2)}, u32[]{:S(2)}) %collective-permute-start.1) | collective-permute-done | bytes 131104 | tf_op jit(solution)/shard_map/project/ppermute | solution.py:16
  17.9 4.0 %collective-permute-start.4 = (bf16[64,1024]{1,0:T(8,128)(2,1)S(1)}, bf16[64,1024]{1,0:T(8,128)(2,1)S(1)}, u32[]{:S(2)}, u32[]{:S(2)}) collective-permute-start(bf16[64,1024]{1,0:T(8,128)(2,1)S(1)} %get-tuple-element.52), channel_id=1, source_target_pairs={{4,0},{8,4},{12,8},{16,12},{20,16},{24,20},{28,24},{0,28},{5,1},{9... | collective-permute-start | bytes 393224 | tf_op jit(solution)/shard_map/project/ppermute | solution.py:16
  21.9 2.6 %collective-permute-done.3 = bf16[64,1024]{1,0:T(8,128)(2,1)S(1)} collective-permute-done((bf16[64,1024]{1,0:T(8,128)(2,1)S(1)}, bf16[64,1024]{1,0:T(8,128)(2,1)S(1)}, u32[]{:S(2)}, u32[]{:S(2)}) %collective-permute-start.3) | collective-permute-done | bytes 131104 | tf_op jit(solution)/shard_map/project/ppermute | solution.py:16
  24.6 3.1 %collective-permute-start.5 = (bf16[64,1024]{1,0:T(8,128)(2,1)S(1)}, bf16[64,1024]{1,0:T(8,128)(2,1)S(1)}, u32[]{:S(2)}, u32[]{:S(2)}) collective-permute-start(bf16[64,1024]{1,0:T(8,128)(2,1)S(1)} %get-tuple-element.54), channel_id=1, source_target_pairs={{12,0},{16,4},{20,8},{24,12},{28,16},{0,20},{4,24},{8,28},{13,1},{... | collective-permute-start | bytes 393224 | tf_op jit(solution)/shard_map/project/ppermute | solution.py:16
  29.2 7.5 %collective-permute-done.5 = bf16[64,1024]{1,0:T(8,128)(2,1)S(1)} collective-permute-done((bf16[64,1024]{1,0:T(8,128)(2,1)S(1)}, bf16[64,1024]{1,0:T(8,128)(2,1)S(1)}, u32[]{:S(2)}, u32[]{:S(2)}) %collective-permute-start.5) | collective-permute-done | bytes 131104 | tf_op jit(solution)/shard_map/project/ppermute | solution.py:16
  37.0 4.9 %collective-permute-start.8 = (bf16[64,1024]{1,0:T(8,128)(2,1)S(1)}, bf16[64,1024]{1,0:T(8,128)(2,1)S(1)}, u32[]{:S(2)}, u32[]{:S(2)}) collective-permute-start(bf16[64,1024]{1,0:T(8,128)(2,1)S(1)} %get-tuple-element.51), channel_id=1, source_target_pairs={{1,0},{2,1},{3,2},{0,3},{5,4},{6,5},{7,6},{4,7},{9,8},{10,9},{11,1... | collective-permute-start | bytes 393224 | tf_op jit(solution)/shard_map/project/ppermute | solution.py:16
  43.9 3.3 %collective-permute-done.9 = bf16[64,1024]{1,0:T(8,128)(2,1)S(1)} collective-permute-done((bf16[64,1024]{1,0:T(8,128)(2,1)S(1)}, bf16[64,1024]{1,0:T(8,128)(2,1)S(1)}, u32[]{:S(2)}, u32[]{:S(2)}) %collective-permute-start.9) | collective-permute-done | bytes 131104 | tf_op jit(solution)/shard_map/project/ppermute | solution.py:16
  47.2 2.7 %cross.3 = (bf16[1,256,512]{2,1,0:T(8,128)(2,1)S(1)}, f32[1,256,512]{2,1,0:T(8,128)S(1)}) custom-call(s32[2]{0:T(128)S(1)} %pad_add_fusion.refs_0_, bf16[256,1024]{1,0:T(8,128)(2,1)S(1)} %constant_dynamic-update-slice_fusion.12.refs_1_, bf16[512,4096]{1,0:T(8,128)(2,1)} %refs_2_.7, bf16[512,4096]{1,0:T(8,128)(2,1)} %refs_3_.7, f32[1,4096]{1,0:T(1,128)S(1)} %bitcast.5), custom_call_target="tpu_custom_call" | custom-call | flops 536870912 | bytes 2097152 | tf_op jit(solution)/shard_map/sketch/cross/pallas_call | solution.py:255
  49.8 3.1 %cross.5 = bf16[3,256,512]{2,1,0:T(8,128)(2,1)S(1)} custom-call(s32[2]{0:T(128)S(1)} %pad_add_fusion.refs_0_, bf16[256,1024]{1,0:T(8,128)(2,1)S(1)} %constant_dynamic-update-slice_fusion.12.refs_1_, bf16[512,4096]{1,0:T(8,128)(2,1)} %refs_2_.7, bf16[512,4096]{1,0:T(8,128)(2,1)} %refs_3_.7, f32[1,4096]{1,0:T(1,128)S(1)} %bitcast.6), custom_call_target="tpu_custom_call" | custom-call | flops 805306368 | bytes 3145728 | tf_op jit(solution)/shard_map/sketch/cross/pallas_call | solution.py:255
  53.0 2.6 %collective-permute-start.11 = (bf16[3,256,512]{2,1,0:T(8,128)(2,1)S(1)}, bf16[3,256,512]{2,1,0:T(8,128)(2,1)S(1)}, u32[]{:S(2)}, u32[]{:S(2)}) collective-permute-start(bf16[3,256,512]{2,1,0:T(8,128)(2,1)S(1)} %cross.5), channel_id=1, source_target_pairs={{32,0},{0,32},{33,1},{1,33},{34,2},{2,34},{35,3},{3,35},{36,4},{4,... | collective-permute-start | bytes 2359304 | tf_op jit(solution)/shard_map/sketch/ppermute | solution.py:21
  57.9 3.0 %collective-permute-start.12 = (bf16[256,512]{1,0:T(8,128)(2,1)S(1)}, bf16[256,512]{1,0:T(8,128)(2,1)S(1)}, u32[]{:S(2)}, u32[]{:S(2)}) collective-permute-start(bf16[256,512]{1,0:T(8,128)(2,1)S(1)} %combine.2), channel_id=1, source_target_pairs={{128,0},{192,64},{0,128},{64,192},{129,1},{193,65},{1,129},{65,193... | collective-permute-start | bytes 786440 | tf_op jit(solution)/shard_map/sketch/ppermute | solution.py:16
  60.9 3.1 %cross.4.own_ref = f32[3,256,512]{2,1,0:T(8,128)S(1)} custom-call(s32[2]{0:T(128)S(1)} %pad_add_fusion.refs_0_, bf16[256,1024]{1,0:T(8,128)(2,1)S(1)} %constant_dynamic-update-slice_fusion.12.refs_1_, bf16[512,4096]{1,0:T(8,128)(2,1)} %refs_2_.7, bf16[512,4096]{1,0:T(8,128)(2,1)} %refs_3_.7, f32[1,4096]{1,0:T(1,128)S(1)} %bitcast.7), custom_call_target="tpu_custom_call" | custom-call | flops 805306368 | bytes 3145728 | tf_op jit(solution)/shard_map/sketch/cross/pallas_call | solution.py:255
  64.6 2.3 %collective-permute-start.14 = (bf16[256,512]{1,0:T(8,128)(2,1)S(1)}, bf16[256,512]{1,0:T(8,128)(2,1)S(1)}, u32[]{:S(2)}, u32[]{:S(2)}) collective-permute-start(bf16[256,512]{1,0:T(8,128)(2,1)S(1)} %get-tuple-element.35), channel_id=1, source_target_pairs={{64,0},{128,64},{192,128},{0,192},{65,1},{129,65},{193,129},{1,193... | collective-permute-start | bytes 786440 | tf_op jit(solution)/shard_map/sketch/ppermute | solution.py:16
  67.0 5.6 %collective-permute-done.13.b_ref = bf16[256,512]{1,0:T(8,128)(2,1)S(1)} collective-permute-done((bf16[256,512]{1,0:T(8,128)(2,1)S(1)}, bf16[256,512]{1,0:T(8,128)(2,1)S(1)}, u32[]{:S(2)}, u32[]{:S(2)}) %collective-permute-start.13) | collective-permute-done | bytes 262176 | tf_op jit(solution)/shard_map/sketch/ppermute | solution.py:16
  76.0 2.7 %collective-permute-start.16 = (f32[32,256]{1,0:T(8,128)S(1)}, f32[32,256]{1,0:T(8,128)S(1)}, u32[]{:S(2)}, u32[]{:S(2)}) collective-permute-start(f32[32,256]{1,0:T(8,128)S(1)} %get-tuple-element.56), channel_id=1, source_target_pairs={{128,0},{192,64},{0,128},{64,192},{129,1},{193,65},{1,129},{65,193... | collective-permute-start | bytes 98312 | tf_op jit(solution)/shard_map/gram/ppermute | solution.py:16
  82.8 2.2 %collective-permute-start.20 = (f32[32,256]{1,0:T(8,128)S(1)}, f32[32,256]{1,0:T(8,128)S(1)}, u32[]{:S(2)}, u32[]{:S(2)}) collective-permute-start(f32[32,256]{1,0:T(8,128)S(1)} %add_add_fusion.2), channel_id=1, source_target_pairs={{2,0},{3,1},{0,2},{1,3},{6,4},{7,5},{4,6},{5,7},{10,8},{11,9},{8,1... | collective-permute-start | bytes 98312 | tf_op jit(solution)/shard_map/gram/ppermute | solution.py:21
  89.4 4.0 %collective-permute-start.23 = (f32[32,256]{1,0:T(8,128)S(1)}, f32[32,256]{1,0:T(8,128)S(1)}, u32[]{:S(2)}, u32[]{:S(2)}) collective-permute-start(f32[32,256]{1,0:T(8,128)S(1)} %add_add_fusion.1), channel_id=1, source_target_pairs={{24,0},{28,4},{16,8},{20,12},{8,16},{12,20},{0,24},{4,28},{25,1},{... | collective-permute-start | bytes 98312 | tf_op jit(solution)/shard_map/gram/ppermute | solution.py:21
  97.5 3.0 %collective-permute-done.26 = bf16[512,256]{1,0:T(8,128)(2,1)S(1)} collective-permute-done((bf16[512,256]{1,0:T(8,128)(2,1)S(1)}, bf16[512,256]{1,0:T(8,128)(2,1)S(1)}, u32[]{:S(2)}, u32[]{:S(2)}) %collective-permute-start.26) | collective-permute-done | bytes 262176 | tf_op jit(solution)/shard_map/gram/ppermute | solution.py:16
  100.5 3.3 %collective-permute-start.28 = (f32[32,256]{1,0:T(8,128)S(1)}, f32[32,256]{1,0:T(8,128)S(1)}, u32[]{:S(2)}, u32[]{:S(2)}) collective-permute-start(f32[32,256]{1,0:T(8,128)S(1)} %add_add_fusion), channel_id=1, source_target_pairs={{8,0},{12,4},{0,8},{4,12},{24,16},{28,20},{16,24},{20,28},{9,1},{1... | collective-permute-start | bytes 98312 | tf_op jit(solution)/shard_map/gram/ppermute | solution.py:21
  112.4 6.4 %collective-permute-start.32 = (f32[128,256]{1,0:T(8,128)S(1)}, f32[128,256]{1,0:T(8,128)S(1)}, u32[]{:S(2)}, u32[]{:S(2)}) collective-permute-start(f32[128,256]{1,0:T(8,128)S(1)} %constant_dynamic-update-slice_fusion.4), channel_id=1, source_target_pairs={{32,0},{0,32},{33,1},{1,33},{34,2},{2,34},{35,3},{3,35},{36,4},{4,... | collective-permute-start | bytes 393224 | tf_op jit(solution)/shard_map/gram/ppermute | solution.py:16
  120.2 10.0 %factorize.1 = (f32[256,256]{1,0:T(8,128)}, bf16[256,256]{1,0:T(8,128)(2,1)S(1)}, bf16[256,256]{1,0:T(8,128)(2,1)S(1)}) custom-call(f32[256,256]{1,0:T(8,128)S(1)} %constant_dynamic-update-slice_fusion.2.refs_0_), custom_call_target="tpu_custom_call" | custom-call | flops 201326592 | bytes 524288 | tf_op jit(solution)/shard_map/gram/factorize/pallas_call | solution.py:125
  (85 shorter events, 36.7 us)
Async XLA Ops:
  5.8 6.3 %collective-permute-start = (bf16[64,1024]{1,0:T(8,128)(2,1)S(1)}, bf16[64,1024]{1,0:T(8,128)(2,1)S(1)}, u32[]{:S(2)}, u32[]{:S(2)}) collective-permute-start(bf16[64,1024]{1,0:T(8,128)(2,1)S(1)} %get-tuple-element.26), channel_id=1, source_target_pairs={{2,0},{3,1},{0,2},{1,3},{6,4},{7,5},{4,6},{5,7},{10,8},{11,9},{8,1... | collective-permute-start | bytes 393224 | tf_op jit(solution)/shard_map/project/ppermute | solution.py:16
  9.5 7.2 %collective-permute-start.1 = (bf16[64,1024]{1,0:T(8,128)(2,1)S(1)}, bf16[64,1024]{1,0:T(8,128)(2,1)S(1)}, u32[]{:S(2)}, u32[]{:S(2)}) collective-permute-start(bf16[64,1024]{1,0:T(8,128)(2,1)S(1)} %get-tuple-element.27), channel_id=1, source_target_pairs={{3,0},{0,1},{1,2},{2,3},{7,4},{4,5},{5,6},{6,7},{11,8},{8,9},{9,10... | collective-permute-start | bytes 393224 | tf_op jit(solution)/shard_map/project/ppermute | solution.py:16
  9.8 6.9 %collective-permute-start.2 = (bf16[64,1024]{1,0:T(8,128)(2,1)S(1)}, bf16[64,1024]{1,0:T(8,128)(2,1)S(1)}, u32[]{:S(2)}, u32[]{:S(2)}) collective-permute-start(bf16[64,1024]{1,0:T(8,128)(2,1)S(1)} %get-tuple-element.28), channel_id=1, source_target_pairs={{1,0},{2,1},{3,2},{0,3},{5,4},{6,5},{7,6},{4,7},{9,8},{10,9},{11,1... | collective-permute-start | bytes 393224 | tf_op jit(solution)/shard_map/project/ppermute | solution.py:16
  16.7 7.8 %collective-permute-start.3 = (bf16[64,1024]{1,0:T(8,128)(2,1)S(1)}, bf16[64,1024]{1,0:T(8,128)(2,1)S(1)}, u32[]{:S(2)}, u32[]{:S(2)}) collective-permute-start(bf16[64,1024]{1,0:T(8,128)(2,1)S(1)} %get-tuple-element.52), channel_id=1, source_target_pairs={{28,0},{0,4},{4,8},{8,12},{12,16},{16,20},{20,24},{24,28},{29,1},{... | collective-permute-start | bytes 393224 | tf_op jit(solution)/shard_map/project/ppermute | solution.py:16
  17.9 6.6 %collective-permute-start.4 = (bf16[64,1024]{1,0:T(8,128)(2,1)S(1)}, bf16[64,1024]{1,0:T(8,128)(2,1)S(1)}, u32[]{:S(2)}, u32[]{:S(2)}) collective-permute-start(bf16[64,1024]{1,0:T(8,128)(2,1)S(1)} %get-tuple-element.52), channel_id=1, source_target_pairs={{4,0},{8,4},{12,8},{16,12},{20,16},{24,20},{28,24},{0,28},{5,1},{9... | collective-permute-start | bytes 393224 | tf_op jit(solution)/shard_map/project/ppermute | solution.py:16
  24.6 12.1 %collective-permute-start.5 = (bf16[64,1024]{1,0:T(8,128)(2,1)S(1)}, bf16[64,1024]{1,0:T(8,128)(2,1)S(1)}, u32[]{:S(2)}, u32[]{:S(2)}) collective-permute-start(bf16[64,1024]{1,0:T(8,128)(2,1)S(1)} %get-tuple-element.54), channel_id=1, source_target_pairs={{12,0},{16,4},{20,8},{24,12},{28,16},{0,20},{4,24},{8,28},{13,1},{... | collective-permute-start | bytes 393224 | tf_op jit(solution)/shard_map/project/ppermute | solution.py:16
  27.7 9.0 %collective-permute-start.6 = (bf16[64,1024]{1,0:T(8,128)(2,1)S(1)}, bf16[64,1024]{1,0:T(8,128)(2,1)S(1)}, u32[]{:S(2)}, u32[]{:S(2)}) collective-permute-start(bf16[64,1024]{1,0:T(8,128)(2,1)S(1)} %get-tuple-element.55), channel_id=1, source_target_pairs={{24,0},{28,4},{0,8},{4,12},{8,16},{12,20},{16,24},{20,28},{25,1},{... | collective-permute-start | bytes 393224 | tf_op jit(solution)/shard_map/project/ppermute | solution.py:16
  36.9 5.4 %collective-permute-start.7 = (bf16[64,1024]{1,0:T(8,128)(2,1)S(1)}, bf16[64,1024]{1,0:T(8,128)(2,1)S(1)}, u32[]{:S(2)}, u32[]{:S(2)}) collective-permute-start(bf16[64,1024]{1,0:T(8,128)(2,1)S(1)} %get-tuple-element.51), channel_id=1, source_target_pairs={{2,0},{3,1},{0,2},{1,3},{6,4},{7,5},{4,6},{5,7},{10,8},{11,9},{8,1... | collective-permute-start | bytes 393224 | tf_op jit(solution)/shard_map/project/ppermute | solution.py:16
  37.0 6.9 %collective-permute-start.8 = (bf16[64,1024]{1,0:T(8,128)(2,1)S(1)}, bf16[64,1024]{1,0:T(8,128)(2,1)S(1)}, u32[]{:S(2)}, u32[]{:S(2)}) collective-permute-start(bf16[64,1024]{1,0:T(8,128)(2,1)S(1)} %get-tuple-element.51), channel_id=1, source_target_pairs={{1,0},{2,1},{3,2},{0,3},{5,4},{6,5},{7,6},{4,7},{9,8},{10,9},{11,1... | collective-permute-start | bytes 393224 | tf_op jit(solution)/shard_map/project/ppermute | solution.py:16
  42.0 5.1 %collective-permute-start.9 = (bf16[64,1024]{1,0:T(8,128)(2,1)S(1)}, bf16[64,1024]{1,0:T(8,128)(2,1)S(1)}, u32[]{:S(2)}, u32[]{:S(2)}) collective-permute-start(bf16[64,1024]{1,0:T(8,128)(2,1)S(1)} %get-tuple-element.51), channel_id=1, source_target_pairs={{3,0},{0,1},{1,2},{2,3},{7,4},{4,5},{5,6},{6,7},{11,8},{8,9},{9,10... | collective-permute-start | bytes 393224 | tf_op jit(solution)/shard_map/project/ppermute | solution.py:16
  53.0 11.1 %collective-permute-start.11 = (bf16[3,256,512]{2,1,0:T(8,128)(2,1)S(1)}, bf16[3,256,512]{2,1,0:T(8,128)(2,1)S(1)}, u32[]{:S(2)}, u32[]{:S(2)}) collective-permute-start(bf16[3,256,512]{2,1,0:T(8,128)(2,1)S(1)} %cross.5), channel_id=1, source_target_pairs={{32,0},{0,32},{33,1},{1,33},{34,2},{2,34},{35,3},{3,35},{36,4},{4,... | collective-permute-start | bytes 2359304 | tf_op jit(solution)/shard_map/sketch/ppermute | solution.py:21
  57.9 9.1 %collective-permute-start.12 = (bf16[256,512]{1,0:T(8,128)(2,1)S(1)}, bf16[256,512]{1,0:T(8,128)(2,1)S(1)}, u32[]{:S(2)}, u32[]{:S(2)}) collective-permute-start(bf16[256,512]{1,0:T(8,128)(2,1)S(1)} %combine.2), channel_id=1, source_target_pairs={{128,0},{192,64},{0,128},{64,192},{129,1},{193,65},{1,129},{65,193... | collective-permute-start | bytes 786440 | tf_op jit(solution)/shard_map/sketch/ppermute | solution.py:16
  64.1 8.5 %collective-permute-start.13 = (bf16[256,512]{1,0:T(8,128)(2,1)S(1)}, bf16[256,512]{1,0:T(8,128)(2,1)S(1)}, u32[]{:S(2)}, u32[]{:S(2)}) collective-permute-start(bf16[256,512]{1,0:T(8,128)(2,1)S(1)} %get-tuple-element.34), channel_id=1, source_target_pairs={{192,0},{0,64},{64,128},{128,192},{193,1},{1,65},{65,129},{129,193... | collective-permute-start | bytes 786440 | tf_op jit(solution)/shard_map/sketch/ppermute | solution.py:16
  64.6 8.4 %collective-permute-start.14 = (bf16[256,512]{1,0:T(8,128)(2,1)S(1)}, bf16[256,512]{1,0:T(8,128)(2,1)S(1)}, u32[]{:S(2)}, u32[]{:S(2)}) collective-permute-start(bf16[256,512]{1,0:T(8,128)(2,1)S(1)} %get-tuple-element.35), channel_id=1, source_target_pairs={{64,0},{128,64},{192,128},{0,192},{65,1},{129,65},{193,129},{1,193... | collective-permute-start | bytes 786440 | tf_op jit(solution)/shard_map/sketch/ppermute | solution.py:16
  76.0 5.3 %collective-permute-start.16 = (f32[32,256]{1,0:T(8,128)S(1)}, f32[32,256]{1,0:T(8,128)S(1)}, u32[]{:S(2)}, u32[]{:S(2)}) collective-permute-start(f32[32,256]{1,0:T(8,128)S(1)} %get-tuple-element.56), channel_id=1, source_target_pairs={{128,0},{192,64},{0,128},{64,192},{129,1},{193,65},{1,129},{65,193... | collective-permute-start | bytes 98312 | tf_op jit(solution)/shard_map/gram/ppermute | solution.py:16
  82.7 6.6 %collective-permute-start.19 = (f32[32,256]{1,0:T(8,128)S(1)}, f32[32,256]{1,0:T(8,128)S(1)}, u32[]{:S(2)}, u32[]{:S(2)}) collective-permute-start(f32[32,256]{1,0:T(8,128)S(1)} %add_add_fusion.2), channel_id=1, source_target_pairs={{1,0},{0,1},{3,2},{2,3},{5,4},{4,5},{7,6},{6,7},{9,8},{8,9},{11,10... | collective-permute-start | bytes 98312 | tf_op jit(solution)/shard_map/gram/ppermute | solution.py:21
  82.8 6.5 %collective-permute-start.20 = (f32[32,256]{1,0:T(8,128)S(1)}, f32[32,256]{1,0:T(8,128)S(1)}, u32[]{:S(2)}, u32[]{:S(2)}) collective-permute-start(f32[32,256]{1,0:T(8,128)S(1)} %add_add_fusion.2), channel_id=1, source_target_pairs={{2,0},{3,1},{0,2},{1,3},{6,4},{7,5},{4,6},{5,7},{10,8},{11,9},{8,1... | collective-permute-start | bytes 98312 | tf_op jit(solution)/shard_map/gram/ppermute | solution.py:21
  86.6 10.8 %collective-permute-start.25 = (bf16[512,256]{1,0:T(8,128)(2,1)S(1)}, bf16[512,256]{1,0:T(8,128)(2,1)S(1)}, u32[]{:S(2)}, u32[]{:S(2)}) collective-permute-start(bf16[512,256]{1,0:T(8,128)(2,1)S(1)} %get-tuple-element.40), channel_id=1, source_target_pairs={{128,0},{192,64},{0,128},{64,192},{129,1},{193,65},{1,129},{65,193... | collective-permute-start | bytes 786440 | tf_op jit(solution)/shard_map/gram/ppermute | solution.py:16
  88.1 12.3 %collective-permute-start.26 = (bf16[512,256]{1,0:T(8,128)(2,1)S(1)}, bf16[512,256]{1,0:T(8,128)(2,1)S(1)}, u32[]{:S(2)}, u32[]{:S(2)}) collective-permute-start(bf16[512,256]{1,0:T(8,128)(2,1)S(1)} %get-tuple-element.40), channel_id=1, source_target_pairs={{64,0},{128,64},{192,128},{0,192},{65,1},{129,65},{193,129},{1,193... | collective-permute-start | bytes 786440 | tf_op jit(solution)/shard_map/gram/ppermute | solution.py:16
  89.4 5.9 %collective-permute-start.23 = (f32[32,256]{1,0:T(8,128)S(1)}, f32[32,256]{1,0:T(8,128)S(1)}, u32[]{:S(2)}, u32[]{:S(2)}) collective-permute-start(f32[32,256]{1,0:T(8,128)S(1)} %add_add_fusion.1), channel_id=1, source_target_pairs={{24,0},{28,4},{16,8},{20,12},{8,16},{12,20},{0,24},{4,28},{25,1},{... | collective-permute-start | bytes 98312 | tf_op jit(solution)/shard_map/gram/ppermute | solution.py:21
  93.5 6.9 %collective-permute-start.27 = (bf16[512,256]{1,0:T(8,128)(2,1)S(1)}, bf16[512,256]{1,0:T(8,128)(2,1)S(1)}, u32[]{:S(2)}, u32[]{:S(2)}) collective-permute-start(bf16[512,256]{1,0:T(8,128)(2,1)S(1)} %get-tuple-element.40), channel_id=1, source_target_pairs={{192,0},{0,64},{64,128},{128,192},{193,1},{1,65},{65,129},{129,193... | collective-permute-start | bytes 786440 | tf_op jit(solution)/shard_map/gram/ppermute | solution.py:16
  100.5 4.8 %collective-permute-start.28 = (f32[32,256]{1,0:T(8,128)S(1)}, f32[32,256]{1,0:T(8,128)S(1)}, u32[]{:S(2)}, u32[]{:S(2)}) collective-permute-start(f32[32,256]{1,0:T(8,128)S(1)} %add_add_fusion), channel_id=1, source_target_pairs={{8,0},{12,4},{0,8},{4,12},{24,16},{28,20},{16,24},{20,28},{9,1},{1... | collective-permute-start | bytes 98312 | tf_op jit(solution)/shard_map/gram/ppermute | solution.py:21
  112.4 7.4 %collective-permute-start.32 = (f32[128,256]{1,0:T(8,128)S(1)}, f32[128,256]{1,0:T(8,128)S(1)}, u32[]{:S(2)}, u32[]{:S(2)}) collective-permute-start(f32[128,256]{1,0:T(8,128)S(1)} %constant_dynamic-update-slice_fusion.4), channel_id=1, source_target_pairs={{32,0},{0,32},{33,1},{1,33},{34,2},{2,34},{35,3},{3,35},{36,4},{4,... | collective-permute-start | bytes 393224 | tf_op jit(solution)/shard_map/gram/ppermute | solution.py:16
  119.8 10.7 %collective-permute-start.33 = (bf16[2048,256]{1,0:T(8,128)(2,1)S(1)}, bf16[2048,256]{1,0:T(8,128)(2,1)S(1)}, u32[]{:S(2)}, u32[]{:S(2)}) collective-permute-start(bf16[2048,256]{1,0:T(8,128)(2,1)S(1)} %constant_dynamic-update-slice_fusion.8), channel_id=1, source_target_pairs={{32,0},{0,32},{33,1},{1,33},{34,2},{2,34},{35,3},{3,35},{36,4},{4,... | collective-permute-start | bytes 3145736 | tf_op jit(solution)/shard_map/gram/ppermute | solution.py:16
  (11 other events, 68.0 us)

commit v3 on v2

--- a/solution.py
+++ b/solution.py
@@ -375,9 +375,9 @@
         came = swapped(send, "c", 1)
         (send,) = cross(c, y, ring, (1, 3, 0), (), proj, *terms)
         (piece,) = combine(own, came, 1)
+        send, proj, piece = lax.optimization_barrier((send, proj, piece))
         others = [shifted(piece, "y", -2)]
         came = swapped(send, "c", 1)
-        proj, piece = lax.optimization_barrier((proj, piece))
         (own,) = cross(c, y, ring, (), (1, 3, 0), proj, *terms)
         pieces = combine(own, came, 2)
         others += [shifted(pieces[0], "y", -1), shifted(pieces[1], "y", -3)]

time: 133 us -> 131 us (0.985)
  waiting for transfers between devices: 42.2 us -> 40.2 us
    ppermute x10, waiting for transfers between devices: 7.7 us -> 5.7 us  [swapped(): return lax.ppermute(x, axis, [(i ^ mask, i) for i in range(n)])]
  transfers between devices with their start and end apart: 34 -> 34, of which waited for: 20 -> 19; matrix products, arithmetic and copies ran while one was open for 0% -> 0% of each run, Pallas kernels for 10% -> 13%
where the time goes in v3:
time: 131 us
  starting transfers between devices  61.4 us (47%)
  waiting for transfers between devices  40.2 us (31%)
  Pallas kernels  27.2 us (21%)
    ppermute x24, starting transfers between devices, shifted(): return lax.ppermute(x, axis, [((i + by) % n, i) for i in range(n)])  46 us
    ppermute x24, waiting for transfers between devices, shifted(): return lax.ppermute(x, axis, [((i + by) % n, i) for i in range(n)])  34.5 us
    ppermute x10, starting transfers between devices, swapped(): return lax.ppermute(x, axis, [(i ^ mask, i) for i in range(n)])  15.4 us
    pallas_call x1, Pallas kernels, factorize(): pl.pallas_call(lambda *refs: factor_kernel(scale, *refs), out_shape=[jax....  10 us
    pallas_call x3, Pallas kernels, cross(): pl.pallas_call(lambda *refs: cross_kernel(jobs, *refs), in_specs=[pl.Bloc...  8.93 us
    ppermute x10, waiting for transfers between devices, swapped(): return lax.ppermute(x, axis, [(i ^ mask, i) for i in range(n)])  5.7 us
    pallas_call x1, Pallas kernels, project(): pl.pallas_call(lambda *refs: project_kernel(parts, *refs), in_specs=[pl.B...  5.16 us
  transfers between devices with their start and end apart: 34, of which 19 were waited for; matrix products, arithmetic and copies ran while one was open for 0% of the time, Pallas kernels for 13%

profile of v3, /device:TPU:1, one launch (start us, length us, event | category | flops | bytes accessed | tf_op | source)
XLA Modules:
  0.0 131.0 jit_solution(17900089278964598450)
XLA Ops:
  0.6 5.2 %project.1 = (f32[64,1024]{1,0:T(8,128)S(1)}, bf16[64,1024]{1,0:T(8,128)(2,1)S(1)}, bf16[64,1024]{1,0:T(8,128)(2,1)S(1)}, bf16[64,1024]{1,0:T(8,128)(2,1)S(1)}) custom-call(s32[1]{0:T(128)} %bitcast.2.refs_0_, bf16[512,4096]{1,0:T(8,128)(2,1)} %refs_2_.7, bf16[512,4096]{1,0:T(8,128)(2,1)} %refs_3_.7, bf16[4096,256]{1,0:T(8,128)(2,1)} %refs_3_.4, ...), custom_call_target="tpu_custom_call" | custom-call | flops 2147483648 | bytes 8388608 | tf_op jit(solution)/shard_map/project/project/pallas_call | solution.py:195
  5.8 3.7 %collective-permute-start = (bf16[64,1024]{1,0:T(8,128)(2,1)S(1)}, bf16[64,1024]{1,0:T(8,128)(2,1)S(1)}, u32[]{:S(2)}, u32[]{:S(2)}) collective-permute-start(bf16[64,1024]{1,0:T(8,128)(2,1)S(1)} %get-tuple-element.28), channel_id=1, source_target_pairs={{2,0},{3,1},{0,2},{1,3},{6,4},{7,5},{4,6},{5,7},{10,8},{11,9},{8,1... | collective-permute-start | bytes 393224 | tf_op jit(solution)/shard_map/project/ppermute | solution.py:16
  9.8 2.4 %collective-permute-start.2 = (bf16[64,1024]{1,0:T(8,128)(2,1)S(1)}, bf16[64,1024]{1,0:T(8,128)(2,1)S(1)}, u32[]{:S(2)}, u32[]{:S(2)}) collective-permute-start(bf16[64,1024]{1,0:T(8,128)(2,1)S(1)} %get-tuple-element.30), channel_id=1, source_target_pairs={{1,0},{2,1},{3,2},{0,3},{5,4},{6,5},{7,6},{4,7},{9,8},{10,9},{11,1... | collective-permute-start | bytes 393224 | tf_op jit(solution)/shard_map/project/ppermute | solution.py:16
  12.2 4.5 %collective-permute-done.1 = bf16[64,1024]{1,0:T(8,128)(2,1)S(1)} collective-permute-done((bf16[64,1024]{1,0:T(8,128)(2,1)S(1)}, bf16[64,1024]{1,0:T(8,128)(2,1)S(1)}, u32[]{:S(2)}, u32[]{:S(2)}) %collective-permute-start.1) | collective-permute-done | bytes 131104 | tf_op jit(solution)/shard_map/project/ppermute | solution.py:16
  17.9 4.0 %collective-permute-start.4 = (bf16[64,1024]{1,0:T(8,128)(2,1)S(1)}, bf16[64,1024]{1,0:T(8,128)(2,1)S(1)}, u32[]{:S(2)}, u32[]{:S(2)}) collective-permute-start(bf16[64,1024]{1,0:T(8,128)(2,1)S(1)} %get-tuple-element.56), channel_id=1, source_target_pairs={{4,0},{8,4},{12,8},{16,12},{20,16},{24,20},{28,24},{0,28},{5,1},{9... | collective-permute-start | bytes 393224 | tf_op jit(solution)/shard_map/project/ppermute | solution.py:16
  21.9 2.6 %collective-permute-done.3 = bf16[64,1024]{1,0:T(8,128)(2,1)S(1)} collective-permute-done((bf16[64,1024]{1,0:T(8,128)(2,1)S(1)}, bf16[64,1024]{1,0:T(8,128)(2,1)S(1)}, u32[]{:S(2)}, u32[]{:S(2)}) %collective-permute-start.3) | collective-permute-done | bytes 131104 | tf_op jit(solution)/shard_map/project/ppermute | solution.py:16
  24.6 3.1 %collective-permute-start.5 = (bf16[64,1024]{1,0:T(8,128)(2,1)S(1)}, bf16[64,1024]{1,0:T(8,128)(2,1)S(1)}, u32[]{:S(2)}, u32[]{:S(2)}) collective-permute-start(bf16[64,1024]{1,0:T(8,128)(2,1)S(1)} %get-tuple-element.58), channel_id=1, source_target_pairs={{12,0},{16,4},{20,8},{24,12},{28,16},{0,20},{4,24},{8,28},{13,1},{... | collective-permute-start | bytes 393224 | tf_op jit(solution)/shard_map/project/ppermute | solution.py:16
  29.2 7.5 %collective-permute-done.5 = bf16[64,1024]{1,0:T(8,128)(2,1)S(1)} collective-permute-done((bf16[64,1024]{1,0:T(8,128)(2,1)S(1)}, bf16[64,1024]{1,0:T(8,128)(2,1)S(1)}, u32[]{:S(2)}, u32[]{:S(2)}) %collective-permute-start.5) | collective-permute-done | bytes 131104 | tf_op jit(solution)/shard_map/project/ppermute | solution.py:16
  37.0 4.9 %collective-permute-start.8 = (bf16[64,1024]{1,0:T(8,128)(2,1)S(1)}, bf16[64,1024]{1,0:T(8,128)(2,1)S(1)}, u32[]{:S(2)}, u32[]{:S(2)}) collective-permute-start(bf16[64,1024]{1,0:T(8,128)(2,1)S(1)} %get-tuple-element.55), channel_id=1, source_target_pairs={{1,0},{2,1},{3,2},{0,3},{5,4},{6,5},{7,6},{4,7},{9,8},{10,9},{11,1... | collective-permute-start | bytes 393224 | tf_op jit(solution)/shard_map/project/ppermute | solution.py:16
  43.9 3.3 %collective-permute-done.9 = bf16[64,1024]{1,0:T(8,128)(2,1)S(1)} collective-permute-done((bf16[64,1024]{1,0:T(8,128)(2,1)S(1)}, bf16[64,1024]{1,0:T(8,128)(2,1)S(1)}, u32[]{:S(2)}, u32[]{:S(2)}) %collective-permute-start.9) | collective-permute-done | bytes 131104 | tf_op jit(solution)/shard_map/project/ppermute | solution.py:16
  47.2 2.7 %cross.3 = (bf16[1,256,512]{2,1,0:T(8,128)(2,1)S(1)}, f32[1,256,512]{2,1,0:T(8,128)S(1)}) custom-call(s32[2]{0:T(128)S(1)} %pad_add_fusion.refs_0_, bf16[256,1024]{1,0:T(8,128)(2,1)S(1)} %constant_dynamic-update-slice_fusion.12.refs_1_, bf16[512,4096]{1,0:T(8,128)(2,1)} %refs_2_.7, bf16[512,4096]{1,0:T(8,128)(2,1)} %refs_3_.7, f32[1,4096]{1,0:T(1,128)S(1)} %bitcast.5), custom_call_target="tpu_custom_call" | custom-call | flops 536870912 | bytes 2097152 | tf_op jit(solution)/shard_map/sketch/cross/pallas_call | solution.py:255
  49.8 2.6 %collective-permute-start.10 = (bf16[1,256,512]{2,1,0:T(8,128)(2,1)S(1)}, bf16[1,256,512]{2,1,0:T(8,128)(2,1)S(1)}, u32[]{:S(2)}, u32[]{:S(2)}) collective-permute-start(bf16[1,256,512]{2,1,0:T(8,128)(2,1)S(1)} %get-tuple-element.34), channel_id=1, source_target_pairs={{32,0},{0,32},{33,1},{1,33},{34,2},{2,34},{35,3},{3,35},{36,4},{4,... | collective-permute-start | bytes 786440 | tf_op jit(solution)/shard_map/sketch/ppermute | solution.py:21
  52.4 3.1 %cross.4 = bf16[3,256,512]{2,1,0:T(8,128)(2,1)S(1)} custom-call(s32[2]{0:T(128)S(1)} %pad_add_fusion.refs_0_, bf16[256,1024]{1,0:T(8,128)(2,1)S(1)} %constant_dynamic-update-slice_fusion.12.refs_1_, bf16[512,4096]{1,0:T(8,128)(2,1)} %refs_2_.7, bf16[512,4096]{1,0:T(8,128)(2,1)} %refs_3_.7, f32[1,4096]{1,0:T(1,128)S(1)} %bitcast.6), custom_call_target="tpu_custom_call" | custom-call | flops 805306368 | bytes 3145728 | tf_op jit(solution)/shard_map/sketch/cross/pallas_call | solution.py:255
  55.9 3.0 %collective-permute-start.12 = (bf16[256,512]{1,0:T(8,128)(2,1)S(1)}, bf16[256,512]{1,0:T(8,128)(2,1)S(1)}, u32[]{:S(2)}, u32[]{:S(2)}) collective-permute-start(bf16[256,512]{1,0:T(8,128)(2,1)S(1)} %combine.2), channel_id=1, source_target_pairs={{128,0},{192,64},{0,128},{64,192},{129,1},{193,65},{1,129},{65,193... | collective-permute-start | bytes 786440 | tf_op jit(solution)/shard_map/sketch/ppermute | solution.py:16
  58.9 3.1 %cross.5.own_ref = f32[3,256,512]{2,1,0:T(8,128)S(1)} custom-call(s32[2]{0:T(128)S(1)} %pad_add_fusion.refs_0_, bf16[256,1024]{1,0:T(8,128)(2,1)S(1)} %constant_dynamic-update-slice_fusion.12.refs_1_, bf16[512,4096]{1,0:T(8,128)(2,1)} %refs_2_.7, bf16[512,4096]{1,0:T(8,128)(2,1)} %refs_3_.7, f32[1,4096]{1,0:T(1,128)S(1)} %bitcast.7), custom_call_target="tpu_custom_call" | custom-call | flops 805306368 | bytes 3145728 | tf_op jit(solution)/shard_map/sketch/cross/pallas_call | solution.py:255
  62.6 2.3 %collective-permute-start.14 = (bf16[256,512]{1,0:T(8,128)(2,1)S(1)}, bf16[256,512]{1,0:T(8,128)(2,1)S(1)}, u32[]{:S(2)}, u32[]{:S(2)}) collective-permute-start(bf16[256,512]{1,0:T(8,128)(2,1)S(1)} %get-tuple-element.39), channel_id=1, source_target_pairs={{64,0},{128,64},{192,128},{0,192},{65,1},{129,65},{193,129},{1,193... | collective-permute-start | bytes 786440 | tf_op jit(solution)/shard_map/sketch/ppermute | solution.py:16
  64.9 5.6 %collective-permute-done.13.b_ref = bf16[256,512]{1,0:T(8,128)(2,1)S(1)} collective-permute-done((bf16[256,512]{1,0:T(8,128)(2,1)S(1)}, bf16[256,512]{1,0:T(8,128)(2,1)S(1)}, u32[]{:S(2)}, u32[]{:S(2)}) %collective-permute-start.13) | collective-permute-done | bytes 262176 | tf_op jit(solution)/shard_map/sketch/ppermute | solution.py:16
  74.0 2.7 %collective-permute-start.16 = (f32[32,256]{1,0:T(8,128)S(1)}, f32[32,256]{1,0:T(8,128)S(1)}, u32[]{:S(2)}, u32[]{:S(2)}) collective-permute-start(f32[32,256]{1,0:T(8,128)S(1)} %get-tuple-element.60), channel_id=1, source_target_pairs={{128,0},{192,64},{0,128},{64,192},{129,1},{193,65},{1,129},{65,193... | collective-permute-start | bytes 98312 | tf_op jit(solution)/shard_map/gram/ppermute | solution.py:16
  80.8 2.2 %collective-permute-start.20 = (f32[32,256]{1,0:T(8,128)S(1)}, f32[32,256]{1,0:T(8,128)S(1)}, u32[]{:S(2)}, u32[]{:S(2)}) collective-permute-start(f32[32,256]{1,0:T(8,128)S(1)} %add_add_fusion.2), channel_id=1, source_target_pairs={{2,0},{3,1},{0,2},{1,3},{6,4},{7,5},{4,6},{5,7},{10,8},{11,9},{8,1... | collective-permute-start | bytes 98312 | tf_op jit(solution)/shard_map/gram/ppermute | solution.py:21
  87.4 4.0 %collective-permute-start.23 = (f32[32,256]{1,0:T(8,128)S(1)}, f32[32,256]{1,0:T(8,128)S(1)}, u32[]{:S(2)}, u32[]{:S(2)}) collective-permute-start(f32[32,256]{1,0:T(8,128)S(1)} %add_add_fusion.1), channel_id=1, source_target_pairs={{24,0},{28,4},{16,8},{20,12},{8,16},{12,20},{0,24},{4,28},{25,1},{... | collective-permute-start | bytes 98312 | tf_op jit(solution)/shard_map/gram/ppermute | solution.py:21
  95.5 3.0 %collective-permute-done.26 = bf16[512,256]{1,0:T(8,128)(2,1)S(1)} collective-permute-done((bf16[512,256]{1,0:T(8,128)(2,1)S(1)}, bf16[512,256]{1,0:T(8,128)(2,1)S(1)}, u32[]{:S(2)}, u32[]{:S(2)}) %collective-permute-start.26) | collective-permute-done | bytes 262176 | tf_op jit(solution)/shard_map/gram/ppermute | solution.py:16
  98.5 3.3 %collective-permute-start.28 = (f32[32,256]{1,0:T(8,128)S(1)}, f32[32,256]{1,0:T(8,128)S(1)}, u32[]{:S(2)}, u32[]{:S(2)}) collective-permute-start(f32[32,256]{1,0:T(8,128)S(1)} %add_add_fusion), channel_id=1, source_target_pairs={{8,0},{12,4},{0,8},{4,12},{24,16},{28,20},{16,24},{20,28},{9,1},{1... | collective-permute-start | bytes 98312 | tf_op jit(solution)/shard_map/gram/ppermute | solution.py:21
  110.4 6.4 %collective-permute-start.32 = (f32[128,256]{1,0:T(8,128)S(1)}, f32[128,256]{1,0:T(8,128)S(1)}, u32[]{:S(2)}, u32[]{:S(2)}) collective-permute-start(f32[128,256]{1,0:T(8,128)S(1)} %constant_dynamic-update-slice_fusion.4), channel_id=1, source_target_pairs={{32,0},{0,32},{33,1},{1,33},{34,2},{2,34},{35,3},{3,35},{36,4},{4,... | collective-permute-start | bytes 393224 | tf_op jit(solution)/shard_map/gram/ppermute | solution.py:16
  118.2 10.0 %factorize.1 = (f32[256,256]{1,0:T(8,128)}, bf16[256,256]{1,0:T(8,128)(2,1)S(1)}, bf16[256,256]{1,0:T(8,128)(2,1)S(1)}) custom-call(f32[256,256]{1,0:T(8,128)S(1)} %constant_dynamic-update-slice_fusion.2.refs_0_), custom_call_target="tpu_custom_call" | custom-call | flops 201326592 | bytes 524288 | tf_op jit(solution)/shard_map/gram/factorize/pallas_call | solution.py:125
  (85 shorter events, 34.7 us)
Async XLA Ops:
  5.8 6.3 %collective-permute-start = (bf16[64,1024]{1,0:T(8,128)(2,1)S(1)}, bf16[64,1024]{1,0:T(8,128)(2,1)S(1)}, u32[]{:S(2)}, u32[]{:S(2)}) collective-permute-start(bf16[64,1024]{1,0:T(8,128)(2,1)S(1)} %get-tuple-element.28), channel_id=1, source_target_pairs={{2,0},{3,1},{0,2},{1,3},{6,4},{7,5},{4,6},{5,7},{10,8},{11,9},{8,1... | collective-permute-start | bytes 393224 | tf_op jit(solution)/shard_map/project/ppermute | solution.py:16
  9.5 7.2 %collective-permute-start.1 = (bf16[64,1024]{1,0:T(8,128)(2,1)S(1)}, bf16[64,1024]{1,0:T(8,128)(2,1)S(1)}, u32[]{:S(2)}, u32[]{:S(2)}) collective-permute-start(bf16[64,1024]{1,0:T(8,128)(2,1)S(1)} %get-tuple-element.29), channel_id=1, source_target_pairs={{3,0},{0,1},{1,2},{2,3},{7,4},{4,5},{5,6},{6,7},{11,8},{8,9},{9,10... | collective-permute-start | bytes 393224 | tf_op jit(solution)/shard_map/project/ppermute | solution.py:16
  9.8 6.9 %collective-permute-start.2 = (bf16[64,1024]{1,0:T(8,128)(2,1)S(1)}, bf16[64,1024]{1,0:T(8,128)(2,1)S(1)}, u32[]{:S(2)}, u32[]{:S(2)}) collective-permute-start(bf16[64,1024]{1,0:T(8,128)(2,1)S(1)} %get-tuple-element.30), channel_id=1, source_target_pairs={{1,0},{2,1},{3,2},{0,3},{5,4},{6,5},{7,6},{4,7},{9,8},{10,9},{11,1... | collective-permute-start | bytes 393224 | tf_op jit(solution)/shard_map/project/ppermute | solution.py:16
  16.7 7.8 %collective-permute-start.3 = (bf16[64,1024]{1,0:T(8,128)(2,1)S(1)}, bf16[64,1024]{1,0:T(8,128)(2,1)S(1)}, u32[]{:S(2)}, u32[]{:S(2)}) collective-permute-start(bf16[64,1024]{1,0:T(8,128)(2,1)S(1)} %get-tuple-element.56), channel_id=1, source_target_pairs={{28,0},{0,4},{4,8},{8,12},{12,16},{16,20},{20,24},{24,28},{29,1},{... | collective-permute-start | bytes 393224 | tf_op jit(solution)/shard_map/project/ppermute | solution.py:16
  17.9 6.6 %collective-permute-start.4 = (bf16[64,1024]{1,0:T(8,128)(2,1)S(1)}, bf16[64,1024]{1,0:T(8,128)(2,1)S(1)}, u32[]{:S(2)}, u32[]{:S(2)}) collective-permute-start(bf16[64,1024]{1,0:T(8,128)(2,1)S(1)} %get-tuple-element.56), channel_id=1, source_target_pairs={{4,0},{8,4},{12,8},{16,12},{20,16},{24,20},{28,24},{0,28},{5,1},{9... | collective-permute-start | bytes 393224 | tf_op jit(solution)/shard_map/project/ppermute | solution.py:16
  24.6 12.1 %collective-permute-start.5 = (bf16[64,1024]{1,0:T(8,128)(2,1)S(1)}, bf16[64,1024]{1,0:T(8,128)(2,1)S(1)}, u32[]{:S(2)}, u32[]{:S(2)}) collective-permute-start(bf16[64,1024]{1,0:T(8,128)(2,1)S(1)} %get-tuple-element.58), channel_id=1, source_target_pairs={{12,0},{16,4},{20,8},{24,12},{28,16},{0,20},{4,24},{8,28},{13,1},{... | collective-permute-start | bytes 393224 | tf_op jit(solution)/shard_map/project/ppermute | solution.py:16
  27.7 9.0 %collective-permute-start.6 = (bf16[64,1024]{1,0:T(8,128)(2,1)S(1)}, bf16[64,1024]{1,0:T(8,128)(2,1)S(1)}, u32[]{:S(2)}, u32[]{:S(2)}) collective-permute-start(bf16[64,1024]{1,0:T(8,128)(2,1)S(1)} %get-tuple-element.59), channel_id=1, source_target_pairs={{24,0},{28,4},{0,8},{4,12},{8,16},{12,20},{16,24},{20,28},{25,1},{... | collective-permute-start | bytes 393224 | tf_op jit(solution)/shard_map/project/ppermute | solution.py:16
  36.9 5.4 %collective-permute-start.7 = (bf16[64,1024]{1,0:T(8,128)(2,1)S(1)}, bf16[64,1024]{1,0:T(8,128)(2,1)S(1)}, u32[]{:S(2)}, u32[]{:S(2)}) collective-permute-start(bf16[64,1024]{1,0:T(8,128)(2,1)S(1)} %get-tuple-element.55), channel_id=1, source_target_pairs={{2,0},{3,1},{0,2},{1,3},{6,4},{7,5},{4,6},{5,7},{10,8},{11,9},{8,1... | collective-permute-start | bytes 393224 | tf_op jit(solution)/shard_map/project/ppermute | solution.py:16
  37.0 6.9 %collective-permute-start.8 = (bf16[64,1024]{1,0:T(8,128)(2,1)S(1)}, bf16[64,1024]{1,0:T(8,128)(2,1)S(1)}, u32[]{:S(2)}, u32[]{:S(2)}) collective-permute-start(bf16[64,1024]{1,0:T(8,128)(2,1)S(1)} %get-tuple-element.55), channel_id=1, source_target_pairs={{1,0},{2,1},{3,2},{0,3},{5,4},{6,5},{7,6},{4,7},{9,8},{10,9},{11,1... | collective-permute-start | bytes 393224 | tf_op jit(solution)/shard_map/project/ppermute | solution.py:16
  42.0 5.1 %collective-permute-start.9 = (bf16[64,1024]{1,0:T(8,128)(2,1)S(1)}, bf16[64,1024]{1,0:T(8,128)(2,1)S(1)}, u32[]{:S(2)}, u32[]{:S(2)}) collective-permute-start(bf16[64,1024]{1,0:T(8,128)(2,1)S(1)} %get-tuple-element.55), channel_id=1, source_target_pairs={{3,0},{0,1},{1,2},{2,3},{7,4},{4,5},{5,6},{6,7},{11,8},{8,9},{9,10... | collective-permute-start | bytes 393224 | tf_op jit(solution)/shard_map/project/ppermute | solution.py:16
  49.8 5.7 %collective-permute-start.10 = (bf16[1,256,512]{2,1,0:T(8,128)(2,1)S(1)}, bf16[1,256,512]{2,1,0:T(8,128)(2,1)S(1)}, u32[]{:S(2)}, u32[]{:S(2)}) collective-permute-start(bf16[1,256,512]{2,1,0:T(8,128)(2,1)S(1)} %get-tuple-element.34), channel_id=1, source_target_pairs={{32,0},{0,32},{33,1},{1,33},{34,2},{2,34},{35,3},{3,35},{36,4},{4,... | collective-permute-start | bytes 786440 | tf_op jit(solution)/shard_map/sketch/ppermute | solution.py:21
  55.6 6.4 %collective-permute-start.11 = (bf16[3,256,512]{2,1,0:T(8,128)(2,1)S(1)}, bf16[3,256,512]{2,1,0:T(8,128)(2,1)S(1)}, u32[]{:S(2)}, u32[]{:S(2)}) collective-permute-start(bf16[3,256,512]{2,1,0:T(8,128)(2,1)S(1)} %cross.4), channel_id=1, source_target_pairs={{32,0},{0,32},{33,1},{1,33},{34,2},{2,34},{35,3},{3,35},{36,4},{4,... | collective-permute-start | bytes 2359304 | tf_op jit(solution)/shard_map/sketch/ppermute | solution.py:21
  55.9 9.1 %collective-permute-start.12 = (bf16[256,512]{1,0:T(8,128)(2,1)S(1)}, bf16[256,512]{1,0:T(8,128)(2,1)S(1)}, u32[]{:S(2)}, u32[]{:S(2)}) collective-permute-start(bf16[256,512]{1,0:T(8,128)(2,1)S(1)} %combine.2), channel_id=1, source_target_pairs={{128,0},{192,64},{0,128},{64,192},{129,1},{193,65},{1,129},{65,193... | collective-permute-start | bytes 786440 | tf_op jit(solution)/shard_map/sketch/ppermute | solution.py:16
  62.1 8.4 %collective-permute-start.13 = (bf16[256,512]{1,0:T(8,128)(2,1)S(1)}, bf16[256,512]{1,0:T(8,128)(2,1)S(1)}, u32[]{:S(2)}, u32[]{:S(2)}) collective-permute-start(bf16[256,512]{1,0:T(8,128)(2,1)S(1)} %get-tuple-element.38), channel_id=1, source_target_pairs={{192,0},{0,64},{64,128},{128,192},{193,1},{1,65},{65,129},{129,193... | collective-permute-start | bytes 786440 | tf_op jit(solution)/shard_map/sketch/ppermute | solution.py:16
  62.6 8.4 %collective-permute-start.14 = (bf16[256,512]{1,0:T(8,128)(2,1)S(1)}, bf16[256,512]{1,0:T(8,128)(2,1)S(1)}, u32[]{:S(2)}, u32[]{:S(2)}) collective-permute-start(bf16[256,512]{1,0:T(8,128)(2,1)S(1)} %get-tuple-element.39), channel_id=1, source_target_pairs={{64,0},{128,64},{192,128},{0,192},{65,1},{129,65},{193,129},{1,193... | collective-permute-start | bytes 786440 | tf_op jit(solution)/shard_map/sketch/ppermute | solution.py:16
  74.0 5.3 %collective-permute-start.16 = (f32[32,256]{1,0:T(8,128)S(1)}, f32[32,256]{1,0:T(8,128)S(1)}, u32[]{:S(2)}, u32[]{:S(2)}) collective-permute-start(f32[32,256]{1,0:T(8,128)S(1)} %get-tuple-element.60), channel_id=1, source_target_pairs={{128,0},{192,64},{0,128},{64,192},{129,1},{193,65},{1,129},{65,193... | collective-permute-start | bytes 98312 | tf_op jit(solution)/shard_map/gram/ppermute | solution.py:16
  80.7 6.6 %collective-permute-start.19 = (f32[32,256]{1,0:T(8,128)S(1)}, f32[32,256]{1,0:T(8,128)S(1)}, u32[]{:S(2)}, u32[]{:S(2)}) collective-permute-start(f32[32,256]{1,0:T(8,128)S(1)} %add_add_fusion.2), channel_id=1, source_target_pairs={{1,0},{0,1},{3,2},{2,3},{5,4},{4,5},{7,6},{6,7},{9,8},{8,9},{11,10... | collective-permute-start | bytes 98312 | tf_op jit(solution)/shard_map/gram/ppermute | solution.py:21
  80.8 6.5 %collective-permute-start.20 = (f32[32,256]{1,0:T(8,128)S(1)}, f32[32,256]{1,0:T(8,128)S(1)}, u32[]{:S(2)}, u32[]{:S(2)}) collective-permute-start(f32[32,256]{1,0:T(8,128)S(1)} %add_add_fusion.2), channel_id=1, source_target_pairs={{2,0},{3,1},{0,2},{1,3},{6,4},{7,5},{4,6},{5,7},{10,8},{11,9},{8,1... | collective-permute-start | bytes 98312 | tf_op jit(solution)/shard_map/gram/ppermute | solution.py:21
  84.6 10.8 %collective-permute-start.25 = (bf16[512,256]{1,0:T(8,128)(2,1)S(1)}, bf16[512,256]{1,0:T(8,128)(2,1)S(1)}, u32[]{:S(2)}, u32[]{:S(2)}) collective-permute-start(bf16[512,256]{1,0:T(8,128)(2,1)S(1)} %get-tuple-element.44), channel_id=1, source_target_pairs={{128,0},{192,64},{0,128},{64,192},{129,1},{193,65},{1,129},{65,193... | collective-permute-start | bytes 786440 | tf_op jit(solution)/shard_map/gram/ppermute | solution.py:16
  86.1 12.3 %collective-permute-start.26 = (bf16[512,256]{1,0:T(8,128)(2,1)S(1)}, bf16[512,256]{1,0:T(8,128)(2,1)S(1)}, u32[]{:S(2)}, u32[]{:S(2)}) collective-permute-start(bf16[512,256]{1,0:T(8,128)(2,1)S(1)} %get-tuple-element.44), channel_id=1, source_target_pairs={{64,0},{128,64},{192,128},{0,192},{65,1},{129,65},{193,129},{1,193... | collective-permute-start | bytes 786440 | tf_op jit(solution)/shard_map/gram/ppermute | solution.py:16
  87.4 5.9 %collective-permute-start.23 = (f32[32,256]{1,0:T(8,128)S(1)}, f32[32,256]{1,0:T(8,128)S(1)}, u32[]{:S(2)}, u32[]{:S(2)}) collective-permute-start(f32[32,256]{1,0:T(8,128)S(1)} %add_add_fusion.1), channel_id=1, source_target_pairs={{24,0},{28,4},{16,8},{20,12},{8,16},{12,20},{0,24},{4,28},{25,1},{... | collective-permute-start | bytes 98312 | tf_op jit(solution)/shard_map/gram/ppermute | solution.py:21
  91.5 6.9 %collective-permute-start.27 = (bf16[512,256]{1,0:T(8,128)(2,1)S(1)}, bf16[512,256]{1,0:T(8,128)(2,1)S(1)}, u32[]{:S(2)}, u32[]{:S(2)}) collective-permute-start(bf16[512,256]{1,0:T(8,128)(2,1)S(1)} %get-tuple-element.44), channel_id=1, source_target_pairs={{192,0},{0,64},{64,128},{128,192},{193,1},{1,65},{65,129},{129,193... | collective-permute-start | bytes 786440 | tf_op jit(solution)/shard_map/gram/ppermute | solution.py:16
  110.4 7.4 %collective-permute-start.32 = (f32[128,256]{1,0:T(8,128)S(1)}, f32[128,256]{1,0:T(8,128)S(1)}, u32[]{:S(2)}, u32[]{:S(2)}) collective-permute-start(f32[128,256]{1,0:T(8,128)S(1)} %constant_dynamic-update-slice_fusion.4), channel_id=1, source_target_pairs={{32,0},{0,32},{33,1},{1,33},{34,2},{2,34},{35,3},{3,35},{36,4},{4,... | collective-permute-start | bytes 393224 | tf_op jit(solution)/shard_map/gram/ppermute | solution.py:16
  117.8 10.7 %collective-permute-start.33 = (bf16[2048,256]{1,0:T(8,128)(2,1)S(1)}, bf16[2048,256]{1,0:T(8,128)(2,1)S(1)}, u32[]{:S(2)}, u32[]{:S(2)}) collective-permute-start(bf16[2048,256]{1,0:T(8,128)(2,1)S(1)} %constant_dynamic-update-slice_fusion.8), channel_id=1, source_target_pairs={{32,0},{0,32},{33,1},{1,33},{34,2},{2,34},{35,3},{3,35},{36,4},{4,... | collective-permute-start | bytes 3145736 | tf_op jit(solution)/shard_map/gram/ppermute | solution.py:16
  (11 other events, 70.5 us)

commit v4 on v3

--- a/solution.py
+++ b/solution.py
@@ -35,15 +35,20 @@
     return total
 
 
+def placed(pieces, axis):
+    n = len(pieces)
+    me = lax.axis_index(axis)
+    size = pieces[0].shape[0]
+    out = jnp.zeros((n * size, pieces[0].shape[1]), pieces[0].dtype)
+    for k, piece_k in enumerate(pieces):
+        out = lax.dynamic_update_slice_in_dim(out, piece_k, ((me + k) % n) * size, axis=0)
+    return out
+
+
 def gather(x, axis):
     n = lax.axis_size(axis)
-    me = lax.axis_index(axis)
-    size = x.shape[0]
-    out = jnp.zeros((n * size, x.shape[1]), x.dtype)
-    out = lax.dynamic_update_slice_in_dim(out, x, me * size, axis=0)
-    for by in (2, 1, 3) if n == 4 else (1,):
-        out = lax.dynamic_update_slice_in_dim(out, shifted(x, axis, by), ((me + by) % n) * size, axis=0)
-    return out
+    came = {k: shifted(x, axis, k) for k in ((2, 1, 3) if n == 4 else (1,))}
+    return placed([x] + [came[k] for k in range(1, n)], axis)
 
 
 def ring_sum(x, axis):
@@ -57,8 +62,9 @@
     return three + (far + near)
 
 
-def exact_sum(x, axis):
-    return (x + swapped(x, axis, 1)) + (swapped(x, axis, 2) + swapped(x, axis, 3))
+def exact_sum(x, axis, masks):
+    came = [swapped(x, axis, mask) for mask in masks]
+    return x + came[0] if len(came) == 1 else (x + came[0]) + (came[1] + came[2])
 
 
 def factor_block(tile, lead, size):
@@ -384,14 +390,18 @@
 
     with jax.named_scope("gram"):
         keep, send, mine = gram_of(c[None], own, came, others)
-        slab = scatter_sum(keep + swapped(send, "c", 1), "y")
+        slab = keep + swapped(send, "c", 1)
         slab, mine = lax.optimization_barrier((slab, mine))
-        whole = gather(mine, "y")
-        slab = exact_sum(slab, "x")
-        slab = (slab + swapped(slab, "z", 1)) + (swapped(slab, "z", 6) + swapped(slab, "z", 7))
-        slab, whole = lax.optimization_barrier((slab, whole))
-        slab = slab + swapped(slab, "z", 2)
-        gram = gather(gather(slab, "y"), "c")
+        across = shifted(mine, "y", 2)
+        slab = scatter_sum(slab, "x")
+        slab, across = lax.optimization_barrier((slab, across))
+        ahead, behind = shifted(mine, "y", 1), shifted(mine, "y", -1)
+        slab = exact_sum(slab, "z", (1, 6, 7))
+        slab = exact_sum(slab, "z", (2,))
+        slab, ahead, behind = lax.optimization_barrier((slab, ahead, behind))
+        slab = exact_sum(slab, "y", (1, 2, 3))
+        gram = gather(gather(slab, "x"), "c")
+        whole = placed((mine, ahead, across, behind), "y")
         gram, whole = lax.optimization_barrier((gram, whole))
         whole = gather(whole, "c")
         upper, high, low = factorize(gram, feature_total**0.5)

time: 131 us -> 130 us (level)
    ppermute x10, waiting for transfers between devices: 5.7 us -> 4.02 us  [swapped(): return lax.ppermute(x, axis, [(i ^ mask, i) for i in range(n)])]
  transfers between devices with their start and end apart: 34 -> 34, of which waited for: 19 -> 21; matrix products, arithmetic and copies ran while one was open for 0% -> 0% of each run, Pallas kernels for 13% -> 13%
where the time goes in v4:
time: 130 us
  starting transfers between devices  61.1 us (47%)
  waiting for transfers between devices  39.6 us (30%)
  Pallas kernels  27.2 us (21%)
    ppermute x24, starting transfers between devices, shifted(): return lax.ppermute(x, axis, [((i + by) % n, i) for i in range(n)])  44.8 us
    ppermute x24, waiting for transfers between devices, shifted(): return lax.ppermute(x, axis, [((i + by) % n, i) for i in range(n)])  35.6 us
    ppermute x10, starting transfers between devices, swapped(): return lax.ppermute(x, axis, [(i ^ mask, i) for i in range(n)])  16.3 us
    pallas_call x1, Pallas kernels, factorize(): pl.pallas_call(lambda *refs: factor_kernel(scale, *refs), out_shape=[jax....  10 us
    pallas_call x3, Pallas kernels, cross(): pl.pallas_call(lambda *refs: cross_kernel(jobs, *refs), in_specs=[pl.Bloc...  8.93 us
    pallas_call x1, Pallas kernels, project(): pl.pallas_call(lambda *refs: project_kernel(parts, *refs), in_specs=[pl.B...  5.16 us
    ppermute x10, waiting for transfers between devices, swapped(): return lax.ppermute(x, axis, [(i ^ mask, i) for i in range(n)])  4.02 us
  transfers between devices with their start and end apart: 34, of which 21 were waited for; matrix products, arithmetic and copies ran while one was open for 0% of the time, Pallas kernels for 13%

profile of v4, /device:TPU:1, one launch (start us, length us, event | category | flops | bytes accessed | tf_op | source)
XLA Modules:
  0.0 130.0 jit_solution(4615757372195559386)
XLA Ops:
  0.6 5.2 %project.1 = (f32[64,1024]{1,0:T(8,128)S(1)}, bf16[64,1024]{1,0:T(8,128)(2,1)S(1)}, bf16[64,1024]{1,0:T(8,128)(2,1)S(1)}, bf16[64,1024]{1,0:T(8,128)(2,1)S(1)}) custom-call(s32[1]{0:T(128)} %bitcast.2.refs_0_, bf16[512,4096]{1,0:T(8,128)(2,1)} %refs_2_.7, bf16[512,4096]{1,0:T(8,128)(2,1)} %refs_3_.7, bf16[4096,256]{1,0:T(8,128)(2,1)} %refs_3_.4, ...), custom_call_target="tpu_custom_call" | custom-call | flops 2147483648 | bytes 8388608 | tf_op jit(solution)/shard_map/project/project/pallas_call | solution.py:201
  5.8 3.7 %collective-permute-start = (bf16[64,1024]{1,0:T(8,128)(2,1)S(1)}, bf16[64,1024]{1,0:T(8,128)(2,1)S(1)}, u32[]{:S(2)}, u32[]{:S(2)}) collective-permute-start(bf16[64,1024]{1,0:T(8,128)(2,1)S(1)} %get-tuple-element.31), channel_id=1, source_target_pairs={{2,0},{3,1},{0,2},{1,3},{6,4},{7,5},{4,6},{5,7},{10,8},{11,9},{8,1... | collective-permute-start | bytes 393224 | tf_op jit(solution)/shard_map/project/ppermute | solution.py:16
  9.8 2.4 %collective-permute-start.2 = (bf16[64,1024]{1,0:T(8,128)(2,1)S(1)}, bf16[64,1024]{1,0:T(8,128)(2,1)S(1)}, u32[]{:S(2)}, u32[]{:S(2)}) collective-permute-start(bf16[64,1024]{1,0:T(8,128)(2,1)S(1)} %get-tuple-element.33), channel_id=1, source_target_pairs={{1,0},{2,1},{3,2},{0,3},{5,4},{6,5},{7,6},{4,7},{9,8},{10,9},{11,1... | collective-permute-start | bytes 393224 | tf_op jit(solution)/shard_map/project/ppermute | solution.py:16
  12.2 4.5 %collective-permute-done.1 = bf16[64,1024]{1,0:T(8,128)(2,1)S(1)} collective-permute-done((bf16[64,1024]{1,0:T(8,128)(2,1)S(1)}, bf16[64,1024]{1,0:T(8,128)(2,1)S(1)}, u32[]{:S(2)}, u32[]{:S(2)}) %collective-permute-start.1) | collective-permute-done | bytes 131104 | tf_op jit(solution)/shard_map/project/ppermute | solution.py:16
  17.9 4.0 %collective-permute-start.4 = (bf16[64,1024]{1,0:T(8,128)(2,1)S(1)}, bf16[64,1024]{1,0:T(8,128)(2,1)S(1)}, u32[]{:S(2)}, u32[]{:S(2)}) collective-permute-start(bf16[64,1024]{1,0:T(8,128)(2,1)S(1)} %get-tuple-element.62), channel_id=1, source_target_pairs={{4,0},{8,4},{12,8},{16,12},{20,16},{24,20},{28,24},{0,28},{5,1},{9... | collective-permute-start | bytes 393224 | tf_op jit(solution)/shard_map/project/ppermute | solution.py:16
  21.9 2.6 %collective-permute-done.3 = bf16[64,1024]{1,0:T(8,128)(2,1)S(1)} collective-permute-done((bf16[64,1024]{1,0:T(8,128)(2,1)S(1)}, bf16[64,1024]{1,0:T(8,128)(2,1)S(1)}, u32[]{:S(2)}, u32[]{:S(2)}) %collective-permute-start.3) | collective-permute-done | bytes 131104 | tf_op jit(solution)/shard_map/project/ppermute | solution.py:16
  24.6 3.1 %collective-permute-start.5 = (bf16[64,1024]{1,0:T(8,128)(2,1)S(1)}, bf16[64,1024]{1,0:T(8,128)(2,1)S(1)}, u32[]{:S(2)}, u32[]{:S(2)}) collective-permute-start(bf16[64,1024]{1,0:T(8,128)(2,1)S(1)} %get-tuple-element.64), channel_id=1, source_target_pairs={{12,0},{16,4},{20,8},{24,12},{28,16},{0,20},{4,24},{8,28},{13,1},{... | collective-permute-start | bytes 393224 | tf_op jit(solution)/shard_map/project/ppermute | solution.py:16
  29.2 7.5 %collective-permute-done.5 = bf16[64,1024]{1,0:T(8,128)(2,1)S(1)} collective-permute-done((bf16[64,1024]{1,0:T(8,128)(2,1)S(1)}, bf16[64,1024]{1,0:T(8,128)(2,1)S(1)}, u32[]{:S(2)}, u32[]{:S(2)}) %collective-permute-start.5) | collective-permute-done | bytes 131104 | tf_op jit(solution)/shard_map/project/ppermute | solution.py:16
  37.5 3.8 %collective-permute-start.8 = (bf16[64,1024]{1,0:T(8,128)(2,1)S(1)}, bf16[64,1024]{1,0:T(8,128)(2,1)S(1)}, u32[]{:S(2)}, u32[]{:S(2)}) collective-permute-start(bf16[64,1024]{1,0:T(8,128)(2,1)S(1)} %get-tuple-element.61), channel_id=1, source_target_pairs={{2,0},{3,1},{0,2},{1,3},{6,4},{7,5},{4,6},{5,7},{10,8},{11,9},{8,1... | collective-permute-start | bytes 393224 | tf_op jit(solution)/shard_map/project/ppermute | solution.py:16
  43.7 2.7 %collective-permute-done.9 = bf16[64,1024]{1,0:T(8,128)(2,1)S(1)} collective-permute-done((bf16[64,1024]{1,0:T(8,128)(2,1)S(1)}, bf16[64,1024]{1,0:T(8,128)(2,1)S(1)}, u32[]{:S(2)}, u32[]{:S(2)}) %collective-permute-start.9) | collective-permute-done | bytes 131104 | tf_op jit(solution)/shard_map/project/ppermute | solution.py:16
  46.4 2.7 %cross.3 = (bf16[1,256,512]{2,1,0:T(8,128)(2,1)S(1)}, f32[1,256,512]{2,1,0:T(8,128)S(1)}) custom-call(s32[2]{0:T(128)S(1)} %pad_add_fusion.refs_0_, bf16[256,1024]{1,0:T(8,128)(2,1)S(1)} %constant_dynamic-update-slice_fusion.12.refs_1_, bf16[512,4096]{1,0:T(8,128)(2,1)} %refs_2_.7, bf16[512,4096]{1,0:T(8,128)(2,1)} %refs_3_.7, f32[1,4096]{1,0:T(1,128)S(1)} %bitcast.5), custom_call_target="tpu_custom_call" | custom-call | flops 536870912 | bytes 2097152 | tf_op jit(solution)/shard_map/sketch/cross/pallas_call | solution.py:261
  49.1 4.5 %collective-permute-start.10 = (bf16[1,256,512]{2,1,0:T(8,128)(2,1)S(1)}, bf16[1,256,512]{2,1,0:T(8,128)(2,1)S(1)}, u32[]{:S(2)}, u32[]{:S(2)}) collective-permute-start(bf16[1,256,512]{2,1,0:T(8,128)(2,1)S(1)} %get-tuple-element.37), channel_id=1, source_target_pairs={{32,0},{0,32},{33,1},{1,33},{34,2},{2,34},{35,3},{3,35},{36,4},{4,... | collective-permute-start | bytes 786440 | tf_op jit(solution)/shard_map/sketch/ppermute | solution.py:21
  53.6 3.1 %cross.4 = bf16[3,256,512]{2,1,0:T(8,128)(2,1)S(1)} custom-call(s32[2]{0:T(128)S(1)} %pad_add_fusion.refs_0_, bf16[256,1024]{1,0:T(8,128)(2,1)S(1)} %constant_dynamic-update-slice_fusion.12.refs_1_, bf16[512,4096]{1,0:T(8,128)(2,1)} %refs_2_.7, bf16[512,4096]{1,0:T(8,128)(2,1)} %refs_3_.7, f32[1,4096]{1,0:T(1,128)S(1)} %bitcast.6), custom_call_target="tpu_custom_call" | custom-call | flops 805306368 | bytes 3145728 | tf_op jit(solution)/shard_map/sketch/cross/pallas_call | solution.py:261
  57.1 3.0 %collective-permute-start.12 = (bf16[256,512]{1,0:T(8,128)(2,1)S(1)}, bf16[256,512]{1,0:T(8,128)(2,1)S(1)}, u32[]{:S(2)}, u32[]{:S(2)}) collective-permute-start(bf16[256,512]{1,0:T(8,128)(2,1)S(1)} %combine.2), channel_id=1, source_target_pairs={{128,0},{192,64},{0,128},{64,192},{129,1},{193,65},{1,129},{65,193... | collective-permute-start | bytes 786440 | tf_op jit(solution)/shard_map/sketch/ppermute | solution.py:16
  60.1 3.1 %cross.5.own_ref = f32[3,256,512]{2,1,0:T(8,128)S(1)} custom-call(s32[2]{0:T(128)S(1)} %pad_add_fusion.refs_0_, bf16[256,1024]{1,0:T(8,128)(2,1)S(1)} %constant_dynamic-update-slice_fusion.12.refs_1_, bf16[512,4096]{1,0:T(8,128)(2,1)} %refs_2_.7, bf16[512,4096]{1,0:T(8,128)(2,1)} %refs_3_.7, f32[1,4096]{1,0:T(1,128)S(1)} %bitcast.7), custom_call_target="tpu_custom_call" | custom-call | flops 805306368 | bytes 3145728 | tf_op jit(solution)/shard_map/sketch/cross/pallas_call | solution.py:261
  63.8 2.3 %collective-permute-start.14 = (bf16[256,512]{1,0:T(8,128)(2,1)S(1)}, bf16[256,512]{1,0:T(8,128)(2,1)S(1)}, u32[]{:S(2)}, u32[]{:S(2)}) collective-permute-start(bf16[256,512]{1,0:T(8,128)(2,1)S(1)} %get-tuple-element.42), channel_id=1, source_target_pairs={{64,0},{128,64},{192,128},{0,192},{65,1},{129,65},{193,129},{1,193... | collective-permute-start | bytes 786440 | tf_op jit(solution)/shard_map/sketch/ppermute | solution.py:16
  66.2 5.6 %collective-permute-done.13.b_ref = bf16[256,512]{1,0:T(8,128)(2,1)S(1)} collective-permute-done((bf16[256,512]{1,0:T(8,128)(2,1)S(1)}, bf16[256,512]{1,0:T(8,128)(2,1)S(1)}, u32[]{:S(2)}, u32[]{:S(2)}) %collective-permute-start.13) | collective-permute-done | bytes 262176 | tf_op jit(solution)/shard_map/sketch/ppermute | solution.py:16
  75.2 2.7 %collective-permute-start.19 = (bf16[512,256]{1,0:T(8,128)(2,1)S(1)}, bf16[512,256]{1,0:T(8,128)(2,1)S(1)}, u32[]{:S(2)}, u32[]{:S(2)}) collective-permute-start(bf16[512,256]{1,0:T(8,128)(2,1)S(1)} %get-tuple-element.47), channel_id=1, source_target_pairs={{128,0},{192,64},{0,128},{64,192},{129,1},{193,65},{1,129},{65,193... | collective-permute-start | bytes 786440 | tf_op jit(solution)/shard_map/gram/ppermute | solution.py:16
  79.0 2.4 %collective-permute-start.18 = (f32[32,256]{1,0:T(8,128)S(1)}, f32[32,256]{1,0:T(8,128)S(1)}, u32[]{:S(2)}, u32[]{:S(2)}) collective-permute-start(f32[32,256]{1,0:T(8,128)S(1)} %get-tuple-element.67), channel_id=1, source_target_pairs={{1,0},{2,1},{3,2},{0,3},{5,4},{6,5},{7,6},{4,7},{9,8},{10,9},{11,1... | collective-permute-start | bytes 98312 | tf_op jit(solution)/shard_map/gram/ppermute | solution.py:16
  88.2 2.9 %collective-permute-start.24 = (bf16[512,256]{1,0:T(8,128)(2,1)S(1)}, bf16[512,256]{1,0:T(8,128)(2,1)S(1)}, u32[]{:S(2)}, u32[]{:S(2)}) collective-permute-start(bf16[512,256]{1,0:T(8,128)(2,1)S(1)} %get-tuple-element.47), channel_id=1, source_target_pairs={{64,0},{128,64},{192,128},{0,192},{65,1},{129,65},{193,129},{1,193... | collective-permute-start | bytes 786440 | tf_op jit(solution)/shard_map/gram/ppermute | solution.py:16
  91.1 2.6 %collective-permute-start.23 = (f32[32,256]{1,0:T(8,128)S(1)}, f32[32,256]{1,0:T(8,128)S(1)}, u32[]{:S(2)}, u32[]{:S(2)}) collective-permute-start(f32[32,256]{1,0:T(8,128)S(1)} %add_add_fusion.1), channel_id=1, source_target_pairs={{8,0},{12,4},{0,8},{4,12},{24,16},{28,20},{16,24},{20,28},{9,1},{1... | collective-permute-start | bytes 98312 | tf_op jit(solution)/shard_map/gram/ppermute | solution.py:21
  95.0 2.5 %collective-permute-done.25 = bf16[512,256]{1,0:T(8,128)(2,1)S(1)} collective-permute-done((bf16[512,256]{1,0:T(8,128)(2,1)S(1)}, bf16[512,256]{1,0:T(8,128)(2,1)S(1)}, u32[]{:S(2)}, u32[]{:S(2)}) %collective-permute-start.25) | collective-permute-done | bytes 262176 | tf_op jit(solution)/shard_map/gram/ppermute | solution.py:16
  109.1 6.7 %collective-permute-start.32 = (f32[128,256]{1,0:T(8,128)S(1)}, f32[128,256]{1,0:T(8,128)S(1)}, u32[]{:S(2)}, u32[]{:S(2)}) collective-permute-start(f32[128,256]{1,0:T(8,128)S(1)} %constant_dynamic-update-slice_fusion.8), channel_id=1, source_target_pairs={{32,0},{0,32},{33,1},{1,33},{34,2},{2,34},{35,3},{3,35},{36,4},{4,... | collective-permute-start | bytes 393224 | tf_op jit(solution)/shard_map/gram/ppermute | solution.py:16
  117.2 10.0 %factorize.1 = (f32[256,256]{1,0:T(8,128)}, bf16[256,256]{1,0:T(8,128)(2,1)S(1)}, bf16[256,256]{1,0:T(8,128)(2,1)S(1)}) custom-call(f32[256,256]{1,0:T(8,128)S(1)} %constant_dynamic-update-slice_fusion.6.refs_0_), custom_call_target="tpu_custom_call" | custom-call | flops 201326592 | bytes 524288 | tf_op jit(solution)/shard_map/gram/factorize/pallas_call | solution.py:131
  (85 shorter events, 35.3 us)
Async XLA Ops:
  5.8 6.3 %collective-permute-start = (bf16[64,1024]{1,0:T(8,128)(2,1)S(1)}, bf16[64,1024]{1,0:T(8,128)(2,1)S(1)}, u32[]{:S(2)}, u32[]{:S(2)}) collective-permute-start(bf16[64,1024]{1,0:T(8,128)(2,1)S(1)} %get-tuple-element.31), channel_id=1, source_target_pairs={{2,0},{3,1},{0,2},{1,3},{6,4},{7,5},{4,6},{5,7},{10,8},{11,9},{8,1... | collective-permute-start | bytes 393224 | tf_op jit(solution)/shard_map/project/ppermute | solution.py:16
  9.5 7.2 %collective-permute-start.1 = (bf16[64,1024]{1,0:T(8,128)(2,1)S(1)}, bf16[64,1024]{1,0:T(8,128)(2,1)S(1)}, u32[]{:S(2)}, u32[]{:S(2)}) collective-permute-start(bf16[64,1024]{1,0:T(8,128)(2,1)S(1)} %get-tuple-element.32), channel_id=1, source_target_pairs={{3,0},{0,1},{1,2},{2,3},{7,4},{4,5},{5,6},{6,7},{11,8},{8,9},{9,10... | collective-permute-start | bytes 393224 | tf_op jit(solution)/shard_map/project/ppermute | solution.py:16
  9.8 6.9 %collective-permute-start.2 = (bf16[64,1024]{1,0:T(8,128)(2,1)S(1)}, bf16[64,1024]{1,0:T(8,128)(2,1)S(1)}, u32[]{:S(2)}, u32[]{:S(2)}) collective-permute-start(bf16[64,1024]{1,0:T(8,128)(2,1)S(1)} %get-tuple-element.33), channel_id=1, source_target_pairs={{1,0},{2,1},{3,2},{0,3},{5,4},{6,5},{7,6},{4,7},{9,8},{10,9},{11,1... | collective-permute-start | bytes 393224 | tf_op jit(solution)/shard_map/project/ppermute | solution.py:16
  16.7 7.8 %collective-permute-start.3 = (bf16[64,1024]{1,0:T(8,128)(2,1)S(1)}, bf16[64,1024]{1,0:T(8,128)(2,1)S(1)}, u32[]{:S(2)}, u32[]{:S(2)}) collective-permute-start(bf16[64,1024]{1,0:T(8,128)(2,1)S(1)} %get-tuple-element.62), channel_id=1, source_target_pairs={{28,0},{0,4},{4,8},{8,12},{12,16},{16,20},{20,24},{24,28},{29,1},{... | collective-permute-start | bytes 393224 | tf_op jit(solution)/shard_map/project/ppermute | solution.py:16
  17.9 6.6 %collective-permute-start.4 = (bf16[64,1024]{1,0:T(8,128)(2,1)S(1)}, bf16[64,1024]{1,0:T(8,128)(2,1)S(1)}, u32[]{:S(2)}, u32[]{:S(2)}) collective-permute-start(bf16[64,1024]{1,0:T(8,128)(2,1)S(1)} %get-tuple-element.62), channel_id=1, source_target_pairs={{4,0},{8,4},{12,8},{16,12},{20,16},{24,20},{28,24},{0,28},{5,1},{9... | collective-permute-start | bytes 393224 | tf_op jit(solution)/shard_map/project/ppermute | solution.py:16
  24.6 12.1 %collective-permute-start.5 = (bf16[64,1024]{1,0:T(8,128)(2,1)S(1)}, bf16[64,1024]{1,0:T(8,128)(2,1)S(1)}, u32[]{:S(2)}, u32[]{:S(2)}) collective-permute-start(bf16[64,1024]{1,0:T(8,128)(2,1)S(1)} %get-tuple-element.64), channel_id=1, source_target_pairs={{12,0},{16,4},{20,8},{24,12},{28,16},{0,20},{4,24},{8,28},{13,1},{... | collective-permute-start | bytes 393224 | tf_op jit(solution)/shard_map/project/ppermute | solution.py:16
  27.7 9.0 %collective-permute-start.6 = (bf16[64,1024]{1,0:T(8,128)(2,1)S(1)}, bf16[64,1024]{1,0:T(8,128)(2,1)S(1)}, u32[]{:S(2)}, u32[]{:S(2)}) collective-permute-start(bf16[64,1024]{1,0:T(8,128)(2,1)S(1)} %get-tuple-element.65), channel_id=1, source_target_pairs={{24,0},{28,4},{0,8},{4,12},{8,16},{12,20},{16,24},{20,28},{25,1},{... | collective-permute-start | bytes 393224 | tf_op jit(solution)/shard_map/project/ppermute | solution.py:16
  36.9 5.0 %collective-permute-start.7 = (bf16[64,1024]{1,0:T(8,128)(2,1)S(1)}, bf16[64,1024]{1,0:T(8,128)(2,1)S(1)}, u32[]{:S(2)}, u32[]{:S(2)}) collective-permute-start(bf16[64,1024]{1,0:T(8,128)(2,1)S(1)} %get-tuple-element.61), channel_id=1, source_target_pairs={{1,0},{2,1},{3,2},{0,3},{5,4},{6,5},{7,6},{4,7},{9,8},{10,9},{11,1... | collective-permute-start | bytes 393224 | tf_op jit(solution)/shard_map/project/ppermute | solution.py:16
  37.5 6.1 %collective-permute-start.8 = (bf16[64,1024]{1,0:T(8,128)(2,1)S(1)}, bf16[64,1024]{1,0:T(8,128)(2,1)S(1)}, u32[]{:S(2)}, u32[]{:S(2)}) collective-permute-start(bf16[64,1024]{1,0:T(8,128)(2,1)S(1)} %get-tuple-element.61), channel_id=1, source_target_pairs={{2,0},{3,1},{0,2},{1,3},{6,4},{7,5},{4,6},{5,7},{10,8},{11,9},{8,1... | collective-permute-start | bytes 393224 | tf_op jit(solution)/shard_map/project/ppermute | solution.py:16
  41.4 5.0 %collective-permute-start.9 = (bf16[64,1024]{1,0:T(8,128)(2,1)S(1)}, bf16[64,1024]{1,0:T(8,128)(2,1)S(1)}, u32[]{:S(2)}, u32[]{:S(2)}) collective-permute-start(bf16[64,1024]{1,0:T(8,128)(2,1)S(1)} %get-tuple-element.61), channel_id=1, source_target_pairs={{3,0},{0,1},{1,2},{2,3},{7,4},{4,5},{5,6},{6,7},{11,8},{8,9},{9,10... | collective-permute-start | bytes 393224 | tf_op jit(solution)/shard_map/project/ppermute | solution.py:16
  49.1 7.6 %collective-permute-start.10 = (bf16[1,256,512]{2,1,0:T(8,128)(2,1)S(1)}, bf16[1,256,512]{2,1,0:T(8,128)(2,1)S(1)}, u32[]{:S(2)}, u32[]{:S(2)}) collective-permute-start(bf16[1,256,512]{2,1,0:T(8,128)(2,1)S(1)} %get-tuple-element.37), channel_id=1, source_target_pairs={{32,0},{0,32},{33,1},{1,33},{34,2},{2,34},{35,3},{3,35},{36,4},{4,... | collective-permute-start | bytes 786440 | tf_op jit(solution)/shard_map/sketch/ppermute | solution.py:21
  56.8 6.4 %collective-permute-start.11 = (bf16[3,256,512]{2,1,0:T(8,128)(2,1)S(1)}, bf16[3,256,512]{2,1,0:T(8,128)(2,1)S(1)}, u32[]{:S(2)}, u32[]{:S(2)}) collective-permute-start(bf16[3,256,512]{2,1,0:T(8,128)(2,1)S(1)} %cross.4), channel_id=1, source_target_pairs={{32,0},{0,32},{33,1},{1,33},{34,2},{2,34},{35,3},{3,35},{36,4},{4,... | collective-permute-start | bytes 2359304 | tf_op jit(solution)/shard_map/sketch/ppermute | solution.py:21
  57.1 9.1 %collective-permute-start.12 = (bf16[256,512]{1,0:T(8,128)(2,1)S(1)}, bf16[256,512]{1,0:T(8,128)(2,1)S(1)}, u32[]{:S(2)}, u32[]{:S(2)}) collective-permute-start(bf16[256,512]{1,0:T(8,128)(2,1)S(1)} %combine.2), channel_id=1, source_target_pairs={{128,0},{192,64},{0,128},{64,192},{129,1},{193,65},{1,129},{65,193... | collective-permute-start | bytes 786440 | tf_op jit(solution)/shard_map/sketch/ppermute | solution.py:16
  63.3 8.5 %collective-permute-start.13 = (bf16[256,512]{1,0:T(8,128)(2,1)S(1)}, bf16[256,512]{1,0:T(8,128)(2,1)S(1)}, u32[]{:S(2)}, u32[]{:S(2)}) collective-permute-start(bf16[256,512]{1,0:T(8,128)(2,1)S(1)} %get-tuple-element.41), channel_id=1, source_target_pairs={{192,0},{0,64},{64,128},{128,192},{193,1},{1,65},{65,129},{129,193... | collective-permute-start | bytes 786440 | tf_op jit(solution)/shard_map/sketch/ppermute | solution.py:16
  63.8 8.4 %collective-permute-start.14 = (bf16[256,512]{1,0:T(8,128)(2,1)S(1)}, bf16[256,512]{1,0:T(8,128)(2,1)S(1)}, u32[]{:S(2)}, u32[]{:S(2)}) collective-permute-start(bf16[256,512]{1,0:T(8,128)(2,1)S(1)} %get-tuple-element.42), channel_id=1, source_target_pairs={{64,0},{128,64},{192,128},{0,192},{65,1},{129,65},{193,129},{1,193... | collective-permute-start | bytes 786440 | tf_op jit(solution)/shard_map/sketch/ppermute | solution.py:16
  75.2 9.1 %collective-permute-start.19 = (bf16[512,256]{1,0:T(8,128)(2,1)S(1)}, bf16[512,256]{1,0:T(8,128)(2,1)S(1)}, u32[]{:S(2)}, u32[]{:S(2)}) collective-permute-start(bf16[512,256]{1,0:T(8,128)(2,1)S(1)} %get-tuple-element.47), channel_id=1, source_target_pairs={{128,0},{192,64},{0,128},{64,192},{129,1},{193,65},{1,129},{65,193... | collective-permute-start | bytes 786440 | tf_op jit(solution)/shard_map/gram/ppermute | solution.py:16
  77.8 4.6 %collective-permute-start.16 = (f32[32,256]{1,0:T(8,128)S(1)}, f32[32,256]{1,0:T(8,128)S(1)}, u32[]{:S(2)}, u32[]{:S(2)}) collective-permute-start(f32[32,256]{1,0:T(8,128)S(1)} %get-tuple-element.66), channel_id=1, source_target_pairs={{2,0},{3,1},{0,2},{1,3},{6,4},{7,5},{4,6},{5,7},{10,8},{11,9},{8,1... | collective-permute-start | bytes 98312 | tf_op jit(solution)/shard_map/gram/ppermute | solution.py:16
  84.3 6.8 %collective-permute-start.20 = (f32[32,256]{1,0:T(8,128)S(1)}, f32[32,256]{1,0:T(8,128)S(1)}, u32[]{:S(2)}, u32[]{:S(2)}) collective-permute-start(f32[32,256]{1,0:T(8,128)S(1)} %add_add_fusion.2), channel_id=1, source_target_pairs={{4,0},{0,4},{12,8},{8,12},{20,16},{16,20},{28,24},{24,28},{5,1},{1... | collective-permute-start | bytes 98312 | tf_op jit(solution)/shard_map/gram/ppermute | solution.py:21
  84.3 6.8 %collective-permute-start.21 = (f32[32,256]{1,0:T(8,128)S(1)}, f32[32,256]{1,0:T(8,128)S(1)}, u32[]{:S(2)}, u32[]{:S(2)}) collective-permute-start(f32[32,256]{1,0:T(8,128)S(1)} %add_add_fusion.2), channel_id=1, source_target_pairs={{24,0},{28,4},{16,8},{20,12},{8,16},{12,20},{0,24},{4,28},{25,1},{... | collective-permute-start | bytes 98312 | tf_op jit(solution)/shard_map/gram/ppermute | solution.py:21
  86.5 4.6 %collective-permute-start.22 = (f32[32,256]{1,0:T(8,128)S(1)}, f32[32,256]{1,0:T(8,128)S(1)}, u32[]{:S(2)}, u32[]{:S(2)}) collective-permute-start(f32[32,256]{1,0:T(8,128)S(1)} %add_add_fusion.2), channel_id=1, source_target_pairs={{28,0},{24,4},{20,8},{16,12},{12,16},{8,20},{4,24},{0,28},{29,1},{... | collective-permute-start | bytes 98312 | tf_op jit(solution)/shard_map/gram/ppermute | solution.py:21
  88.2 6.8 %collective-permute-start.24 = (bf16[512,256]{1,0:T(8,128)(2,1)S(1)}, bf16[512,256]{1,0:T(8,128)(2,1)S(1)}, u32[]{:S(2)}, u32[]{:S(2)}) collective-permute-start(bf16[512,256]{1,0:T(8,128)(2,1)S(1)} %get-tuple-element.47), channel_id=1, source_target_pairs={{64,0},{128,64},{192,128},{0,192},{65,1},{129,65},{193,129},{1,193... | collective-permute-start | bytes 786440 | tf_op jit(solution)/shard_map/gram/ppermute | solution.py:16
  91.1 6.4 %collective-permute-start.25 = (bf16[512,256]{1,0:T(8,128)(2,1)S(1)}, bf16[512,256]{1,0:T(8,128)(2,1)S(1)}, u32[]{:S(2)}, u32[]{:S(2)}) collective-permute-start(bf16[512,256]{1,0:T(8,128)(2,1)S(1)} %get-tuple-element.47), channel_id=1, source_target_pairs={{192,0},{0,64},{64,128},{128,192},{193,1},{1,65},{65,129},{129,193... | collective-permute-start | bytes 786440 | tf_op jit(solution)/shard_map/gram/ppermute | solution.py:16
  109.1 7.7 %collective-permute-start.32 = (f32[128,256]{1,0:T(8,128)S(1)}, f32[128,256]{1,0:T(8,128)S(1)}, u32[]{:S(2)}, u32[]{:S(2)}) collective-permute-start(f32[128,256]{1,0:T(8,128)S(1)} %constant_dynamic-update-slice_fusion.8), channel_id=1, source_target_pairs={{32,0},{0,32},{33,1},{1,33},{34,2},{2,34},{35,3},{3,35},{36,4},{4,... | collective-permute-start | bytes 393224 | tf_op jit(solution)/shard_map/gram/ppermute | solution.py:16
  116.8 10.7 %collective-permute-start.33 = (bf16[2048,256]{1,0:T(8,128)(2,1)S(1)}, bf16[2048,256]{1,0:T(8,128)(2,1)S(1)}, u32[]{:S(2)}, u32[]{:S(2)}) collective-permute-start(bf16[2048,256]{1,0:T(8,128)(2,1)S(1)} %constant_dynamic-update-slice_fusion.2), channel_id=1, source_target_pairs={{32,0},{0,32},{33,1},{1,33},{34,2},{2,34},{35,3},{3,35},{36,4},{4,... | collective-permute-start | bytes 3145736 | tf_op jit(solution)/shard_map/gram/ppermute | solution.py:16
  (11 other events, 69.4 us)

commit v5 on v3

--- a/solution.py
+++ b/solution.py
@@ -11,39 +11,52 @@
 EXACT = lax.Precision.HIGHEST
 
 
-def shifted(x, axis, by):
+def moved(x, axis, source, core):
     n = lax.axis_size(axis)
-    return lax.ppermute(x, axis, [((i + by) % n, i) for i in range(n)])
-
-
-def swapped(x, axis, mask):
-    n = lax.axis_size(axis)
-    return lax.ppermute(x, axis, [(i ^ mask, i) for i in range(n)])
+    if core is None:
+        return lax.ppermute(x, axis, [(source(i, n), i) for i in range(n)])
+    if axis == "y":
+        return lax.ppermute(x, (axis, "c"), [(2 * source(i, n) + core, 2 * i + core) for i in range(n)])
+    return lax.ppermute(x, ("c", axis), [(core * n + source(i, n), core * n + i) for i in range(n)])
+
+
+def shifted(x, axis, by, core=None):
+    return moved(x, axis, lambda i, n: (i + by) % n, core)
+
+
+def swapped(x, axis, mask, core=None):
+    return moved(x, axis, lambda i, n: i ^ mask, core)
 
 
 def piece(x, index, size):
     return lax.dynamic_slice_in_dim(x, index * size, size, axis=0)
 
 
-def scatter_sum(x, axis):
+def scatter_sum(x, axis, core):
     n = lax.axis_size(axis)
     me = lax.axis_index(axis)
     size = x.shape[0] // n
-    total = piece(x, me, size).astype(F32)
-    for by in (2, 1, 3) if n == 4 else (1,):
-        total = total + shifted(piece(x, (me + by) % n, size), axis, n - by).astype(F32)
+    total = piece(x, me, size)
+    for by in (2, 1, 3):
+        total = total + shifted(piece(x, (me + by) % n, size), axis, n - by, core)
     return total
 
 
-def gather(x, axis):
-    n = lax.axis_size(axis)
+def placed(pieces, axis, dim=0):
+    n = len(pieces)
     me = lax.axis_index(axis)
-    size = x.shape[0]
-    out = jnp.zeros((n * size, x.shape[1]), x.dtype)
-    out = lax.dynamic_update_slice_in_dim(out, x, me * size, axis=0)
-    for by in (2, 1, 3) if n == 4 else (1,):
-        out = lax.dynamic_update_slice_in_dim(out, shifted(x, axis, by), ((me + by) % n) * size, axis=0)
+    shape = list(pieces[0].shape)
+    size = shape[dim]
+    shape[dim] = n * size
+    out = jnp.zeros(shape, pieces[0].dtype)
+    for k, piece_k in enumerate(pieces):
+        out = lax.dynamic_update_slice_in_dim(out, piece_k, ((me + k) % n) * size, axis=dim)
     return out
+
+
+def gather(x, axis, core=None, dim=0):
+    came = {k: shifted(x, axis, k, core) for k in (2, 1, 3)}
+    return placed([x] + [came[k] for k in (1, 2, 3)], axis, dim)
 
 
 def ring_sum(x, axis):
@@ -57,8 +70,9 @@
     return three + (far + near)
 
 
-def exact_sum(x, axis):
-    return (x + swapped(x, axis, 1)) + (swapped(x, axis, 2) + swapped(x, axis, 3))
+def exact_sum(x, axis, masks, core):
+    came = [swapped(x, axis, mask, core) for mask in masks]
+    return x + came[0] if len(came) == 1 else (x + came[0]) + (came[1] + came[2])
 
 
 def factor_block(tile, lead, size):
@@ -289,42 +303,41 @@
     )(own, came)
 
 
-def gram_kernel(core_ref, own_ref, came_ref, a_ref, b_ref, d_ref, keep_ref, send_ref, rows_ref, work):
-    total = own_ref[own_ref.shape[0] - 1] + came_ref[own_ref.shape[0] - 1].astype(F32)
+def gram_kernel(own_ref, came_ref, a_ref, b_ref, d_ref, gram_ref, rows_ref):
+    last = own_ref.shape[0] - 1
+    total = own_ref[last] + came_ref[last].astype(F32)
     total = total + (a_ref[...].astype(F32) + b_ref[...].astype(F32) + d_ref[...].astype(F32))
-    half = keep_ref.shape[0]
-    core = core_ref[0]
-    work[...] = lax.dot_general(
+    gram_ref[...] = lax.dot_general(
         total, total, (((1,), (1,)), ((), ())), precision=EXACT, preferred_element_type=F32
     )
-    keep_ref[...] = work[pl.ds(pl.multiple_of(core * half, half), half), :]
-    send_ref[...] = work[pl.ds(pl.multiple_of((1 - core) * half, half), half), :]
     rows_ref[...] = jnp.transpose(total).astype(BF16)
 
 
-def gram_of(core, own, came, others):
+def gram_of(own, came, others):
     columns, block = own.shape[1:]
     whole = pl.BlockSpec(memory_space=pltpu.VMEM)
-    half = jax.ShapeDtypeStruct((columns // 2, columns), F32)
     return pl.pallas_call(
         gram_kernel,
-        in_specs=[pl.BlockSpec(memory_space=pltpu.SMEM)] + [whole] * 5,
-        out_specs=[whole] * 3,
-        out_shape=[half, half, jax.ShapeDtypeStruct((block, columns), BF16)],
-        scratch_shapes=[pltpu.VMEM((columns, columns), F32)],
+        in_specs=[whole] * 5,
+        out_specs=[whole] * 2,
+        out_shape=[
+            jax.ShapeDtypeStruct((columns, columns), F32),
+            jax.ShapeDtypeStruct((block, columns), BF16),
+        ],
         compiler_params=pltpu.CompilerParams(vmem_limit_bytes=16 * 2**20),
         name="gram",
-    )(core, own, came, *others)
-
-
-def basis_kernel(parts, sketch_ref, high_ref, low_ref, out_hbm, work, sems):
+    )(own, came, *others)
+
+
+def basis_kernel(parts, core_ref, first_ref, second_ref, high_ref, low_ref, out_hbm, work, sems):
     transposed = (((1,), (1,)), ((), ()))
     size = work.shape[0] // parts
     copies = []
     for i in range(parts):
         at = slice(i * size, (i + 1) * size)
-        total = lax.dot_general(sketch_ref[at, :], high_ref[...], transposed, preferred_element_type=F32)
-        total = total + lax.dot_general(sketch_ref[at, :], low_ref[...], transposed, preferred_element_type=F32)
+        sketch = jnp.where(core_ref[0] == 0, first_ref[at, :], second_ref[at, :])
+        total = lax.dot_general(sketch, high_ref[...], transposed, preferred_element_type=F32)
+        total = total + lax.dot_general(sketch, low_ref[...], transposed, preferred_element_type=F32)
         work[at, :] = total.astype(BF16)
         rows = pl.ds(i * size, size)
         copies.append(pltpu.make_async_copy(work.at[rows], out_hbm.at[rows], sems.at[i]))
@@ -333,13 +346,13 @@
         copy.wait()
 
 
-def basis_of(sketch, high, low):
-    rows, columns = sketch.shape
+def basis_of(core, first, second, high, low):
+    rows, columns = first.shape
     parts = 8
     vmem = pl.BlockSpec(memory_space=pltpu.VMEM)
     return pl.pallas_call(
         lambda *refs: basis_kernel(parts, *refs),
-        in_specs=[vmem] * 3,
+        in_specs=[pl.BlockSpec(memory_space=pltpu.SMEM)] + [vmem] * 4,
         out_specs=pl.BlockSpec(memory_space=pl.ANY),
         out_shape=jax.ShapeDtypeStruct((rows, columns), BF16),
         scratch_shapes=[pltpu.VMEM((rows, columns), BF16), pltpu.SemaphoreType.DMA((parts,))],
@@ -348,7 +361,7 @@
             flops=4 * rows * columns * columns, bytes_accessed=4 * rows * columns, transcendentals=0
         ),
         name="basis",
-    )(sketch, high, low)
+    )(core[None], first, second, high, low)
 
 
 def on_device(frames_now, frames_lag, test_matrix, feature_scale):
@@ -383,19 +396,20 @@
         others += [shifted(pieces[0], "y", -1), shifted(pieces[1], "y", -3)]
 
     with jax.named_scope("gram"):
-        keep, send, mine = gram_of(c[None], own, came, others)
-        slab = scatter_sum(keep + swapped(send, "c", 1), "y")
-        slab, mine = lax.optimization_barrier((slab, mine))
-        whole = gather(mine, "y")
-        slab = exact_sum(slab, "x")
-        slab = (slab + swapped(slab, "z", 1)) + (swapped(slab, "z", 6) + swapped(slab, "z", 7))
-        slab, whole = lax.optimization_barrier((slab, whole))
-        slab = slab + swapped(slab, "z", 2)
-        gram = gather(gather(slab, "y"), "c")
+        partial, mine = gram_of(own, came, others)
+        slab = partial + lax.ppermute(partial, "c", [(0, 1)])
+        pair = jnp.stack([mine, lax.ppermute(mine, "c", [(1, 0)])])
+        slab = scatter_sum(slab, "x", 1)
+        slab = exact_sum(slab, "z", (1, 6, 7), 1)
+        slab = exact_sum(slab, "z", (2,), 1)
+        slab = exact_sum(slab, "y", (1, 2, 3), 1)
+        gram = gather(slab, "x", 1)
+        whole = gather(pair, "y", 0, 1).reshape(features, -1)
+        gram = jnp.where(c == 1, gram, lax.ppermute(gram, "c", [(1, 0)]))
         gram, whole = lax.optimization_barrier((gram, whole))
-        whole = gather(whole, "c")
+        copied = lax.ppermute(whole, "c", [(0, 1)])
         upper, high, low = factorize(gram, feature_total**0.5)
-    return (basis_of(whole, high, low), upper)
+    return (basis_of(c, whole, copied, high, low), upper)
 
 
 def solution(mesh):

time: 131 us -> 152 us (1.16)
  starting transfers between devices: 61.4 us -> 74.4 us
  waiting for transfers between devices: 40.2 us -> 46.2 us
    ppermute x34 -> x35, starting transfers between devices: 61.4 us -> 74.4 us  [the longest x15 28.7 us: moved(): return lax.ppermute(x, axis, [(source(i, n), i) for i in range(n)])]
    ppermute x34 -> x35, waiting for transfers between devices: 40.2 us -> 46.2 us  [the longest x15 27.1 us: moved(): return lax.ppermute(x, axis, [(source(i, n), i) for i in range(n)])]
  transfers between devices with their start and end apart: 34 -> 35, of which waited for: 19 -> 19; matrix products, arithmetic and copies ran while one was open for 0% -> 1% of each run, Pallas kernels for 13% -> 11%
where the time goes in v5:
time: 152 us; the launch traced here: 151 us
  starting transfers between devices  74.4 us (49%)
  waiting for transfers between devices  46.2 us (30%)
  Pallas kernels  27.2 us (18%)
    ppermute x15, starting transfers between devices, moved(): return lax.ppermute(x, axis, [(source(i, n), i) for i in range(n)])  28.7 us
    ppermute x10, starting transfers between devices, moved(): lax.ppermute(x, ('c', axis), [(core * n + source(i, n), core * n + i) for...  27.9 us
    ppermute x15, waiting for transfers between devices, moved(): return lax.ppermute(x, axis, [(source(i, n), i) for i in range(n)])  27.1 us
    ppermute x10, waiting for transfers between devices, moved(): lax.ppermute(x, ('c', axis), [(core * n + source(i, n), core * n + i) for...  13.7 us
    ppermute x6, starting transfers between devices, moved(): lax.ppermute(x, (axis, 'c'), [(2 * source(i, n) + core, 2 * i + core) for...  12.4 us
    pallas_call x1, Pallas kernels, factorize(): pl.pallas_call(lambda *refs: factor_kernel(scale, *refs), out_shape=[jax....  10 us
    pallas_call x3, Pallas kernels, cross(): pl.pallas_call(lambda *refs: cross_kernel(jobs, *refs), in_specs=[pl.Bloc...  8.93 us
    pallas_call x1, Pallas kernels, project(): pl.pallas_call(lambda *refs: project_kernel(parts, *refs), in_specs=[pl.B...  5.16 us
  transfers between devices with their start and end apart: 35, of which 19 were waited for; matrix products, arithmetic and copies ran while one was open for 1% of the time, Pallas kernels for 11%

profile of v5, /device:TPU:1, one launch (start us, length us, event | category | flops | bytes accessed | tf_op | source)
XLA Modules:
  0.0 151.0 jit_solution(14744547523665447659)
XLA Ops:
  0.6 5.2 %project.1 = (f32[64,1024]{1,0:T(8,128)S(1)}, bf16[64,1024]{1,0:T(8,128)(2,1)S(1)}, bf16[64,1024]{1,0:T(8,128)(2,1)S(1)}, bf16[64,1024]{1,0:T(8,128)(2,1)S(1)}) custom-call(s32[1]{0:T(128)} %bitcast.2.refs_0_, bf16[512,4096]{1,0:T(8,128)(2,1)} %refs_2_.7, bf16[512,4096]{1,0:T(8,128)(2,1)} %refs_3_.7, bf16[4096,256]{1,0:T(8,128)(2,1)} %refs_3_.4, ...), custom_call_target="tpu_custom_call" | custom-call | flops 2147483648 | bytes 8388608 | tf_op jit(solution)/shard_map/project/project/pallas_call | solution.py:209
  5.8 3.7 %collective-permute-start = (bf16[64,1024]{1,0:T(8,128)(2,1)S(1)}, bf16[64,1024]{1,0:T(8,128)(2,1)S(1)}, u32[]{:S(2)}, u32[]{:S(2)}) collective-permute-start(bf16[64,1024]{1,0:T(8,128)(2,1)S(1)} %get-tuple-element.23), channel_id=1, source_target_pairs={{2,0},{3,1},{0,2},{1,3},{6,4},{7,5},{4,6},{5,7},{10,8},{11,9},{8,1... | collective-permute-start | bytes 393224 | tf_op jit(solution)/shard_map/project/ppermute | solution.py:17
  12.2 4.5 %collective-permute-done.1 = bf16[64,1024]{1,0:T(8,128)(2,1)S(1)} collective-permute-done((bf16[64,1024]{1,0:T(8,128)(2,1)S(1)}, bf16[64,1024]{1,0:T(8,128)(2,1)S(1)}, u32[]{:S(2)}, u32[]{:S(2)}) %collective-permute-start.1) | collective-permute-done | bytes 131104 | tf_op jit(solution)/shard_map/project/ppermute | solution.py:17
  16.8 5.1 %collective-permute-start.4 = (bf16[64,1024]{1,0:T(8,128)(2,1)S(1)}, bf16[64,1024]{1,0:T(8,128)(2,1)S(1)}, u32[]{:S(2)}, u32[]{:S(2)}) collective-permute-start(bf16[64,1024]{1,0:T(8,128)(2,1)S(1)} %get-tuple-element.46), channel_id=1, source_target_pairs={{4,0},{8,4},{12,8},{16,12},{20,16},{24,20},{28,24},{0,28},{5,1},{9... | collective-permute-start | bytes 393224 | tf_op jit(solution)/shard_map/project/ppermute | solution.py:17
  23.8 3.1 %collective-permute-done.3 = bf16[64,1024]{1,0:T(8,128)(2,1)S(1)} collective-permute-done((bf16[64,1024]{1,0:T(8,128)(2,1)S(1)}, bf16[64,1024]{1,0:T(8,128)(2,1)S(1)}, u32[]{:S(2)}, u32[]{:S(2)}) %collective-permute-start.3) | collective-permute-done | bytes 131104 | tf_op jit(solution)/shard_map/project/ppermute | solution.py:17
  29.1 6.0 %collective-permute-done.5 = bf16[64,1024]{1,0:T(8,128)(2,1)S(1)} collective-permute-done((bf16[64,1024]{1,0:T(8,128)(2,1)S(1)}, bf16[64,1024]{1,0:T(8,128)(2,1)S(1)}, u32[]{:S(2)}, u32[]{:S(2)}) %collective-permute-start.5) | collective-permute-done | bytes 131104 | tf_op jit(solution)/shard_map/project/ppermute | solution.py:17
  44.4 2.7 %cross.3 = (bf16[1,256,512]{2,1,0:T(8,128)(2,1)S(1)}, f32[1,256,512]{2,1,0:T(8,128)S(1)}) custom-call(s32[2]{0:T(128)S(1)} %pad_add_fusion.refs_0_, bf16[256,1024]{1,0:T(8,128)(2,1)S(1)} %constant_dynamic-update-slice_fusion.8.refs_1_, bf16[512,4096]{1,0:T(8,128)(2,1)} %refs_2_.7, bf16[512,4096]{1,0:T(8,128)(2,1)} %refs_3_.7, f32[1,4096]{1,0:T(1,128)S(1)} %bitcast.10), custom_call_target="tpu_custom_call" | custom-call | flops 536870912 | bytes 2097152 | tf_op jit(solution)/shard_map/sketch/cross/pallas_call | solution.py:269
  47.1 5.4 %collective-permute-start.10 = (bf16[1,256,512]{2,1,0:T(8,128)(2,1)S(1)}, bf16[1,256,512]{2,1,0:T(8,128)(2,1)S(1)}, u32[]{:S(2)}, u32[]{:S(2)}) collective-permute-start(bf16[1,256,512]{2,1,0:T(8,128)(2,1)S(1)} %get-tuple-element.29), channel_id=1, source_target_pairs={{32,0},{0,32},{33,1},{1,33},{34,2},{2,34},{35,3},{3,35},{36,4},{4,... | collective-permute-start | bytes 786440 | tf_op jit(solution)/shard_map/sketch/ppermute | solution.py:17
  52.5 3.1 %cross.4 = bf16[3,256,512]{2,1,0:T(8,128)(2,1)S(1)} custom-call(s32[2]{0:T(128)S(1)} %pad_add_fusion.refs_0_, bf16[256,1024]{1,0:T(8,128)(2,1)S(1)} %constant_dynamic-update-slice_fusion.8.refs_1_, bf16[512,4096]{1,0:T(8,128)(2,1)} %refs_2_.7, bf16[512,4096]{1,0:T(8,128)(2,1)} %refs_3_.7, f32[1,4096]{1,0:T(1,128)S(1)} %bitcast.11), custom_call_target="tpu_custom_call" | custom-call | flops 805306368 | bytes 3145728 | tf_op jit(solution)/shard_map/sketch/cross/pallas_call | solution.py:269
  56.0 3.0 %collective-permute-start.12 = (bf16[256,512]{1,0:T(8,128)(2,1)S(1)}, bf16[256,512]{1,0:T(8,128)(2,1)S(1)}, u32[]{:S(2)}, u32[]{:S(2)}) collective-permute-start(bf16[256,512]{1,0:T(8,128)(2,1)S(1)} %combine.2), channel_id=1, source_target_pairs={{128,0},{192,64},{0,128},{64,192},{129,1},{193,65},{1,129},{65,193... | collective-permute-start | bytes 786440 | tf_op jit(solution)/shard_map/sketch/ppermute | solution.py:17
  59.0 3.1 %cross.5.own_ref = f32[3,256,512]{2,1,0:T(8,128)S(1)} custom-call(s32[2]{0:T(128)S(1)} %pad_add_fusion.refs_0_, bf16[256,1024]{1,0:T(8,128)(2,1)S(1)} %constant_dynamic-update-slice_fusion.8.refs_1_, bf16[512,4096]{1,0:T(8,128)(2,1)} %refs_2_.7, bf16[512,4096]{1,0:T(8,128)(2,1)} %refs_3_.7, f32[1,4096]{1,0:T(1,128)S(1)} %bitcast.12), custom_call_target="tpu_custom_call" | custom-call | flops 805306368 | bytes 3145728 | tf_op jit(solution)/shard_map/sketch/cross/pallas_call | solution.py:269
  65.1 5.6 %collective-permute-done.13.b_ref = bf16[256,512]{1,0:T(8,128)(2,1)S(1)} collective-permute-done((bf16[256,512]{1,0:T(8,128)(2,1)S(1)}, bf16[256,512]{1,0:T(8,128)(2,1)S(1)}, u32[]{:S(2)}, u32[]{:S(2)}) %collective-permute-start.13) | collective-permute-done | bytes 262176 | tf_op jit(solution)/shard_map/sketch/ppermute | solution.py:17
  75.4 3.2 %collective-permute-start.16 = (f32[64,256]{1,0:T(8,128)S(1)}, f32[64,256]{1,0:T(8,128)S(1)}, u32[]{:S(2)}, u32[]{:S(2)}) collective-permute-start(f32[64,256]{1,0:T(8,128)S(1)} %get-tuple-element.52), channel_id=1, source_target_pairs={{34,32},{35,33},{32,34},{33,35},{38,36},{39,37},{36,38},{37,39},{4... | collective-permute-start | bytes 196616 | tf_op jit(solution)/shard_map/gram/ppermute | solution.py:20
  78.6 2.8 %collective-permute-start.18 = (f32[64,256]{1,0:T(8,128)S(1)}, f32[64,256]{1,0:T(8,128)S(1)}, u32[]{:S(2)}, u32[]{:S(2)}) collective-permute-start(f32[64,256]{1,0:T(8,128)S(1)} %get-tuple-element.53), channel_id=1, source_target_pairs={{33,32},{34,33},{35,34},{32,35},{37,36},{38,37},{39,38},{36,39},{4... | collective-permute-start | bytes 196616 | tf_op jit(solution)/shard_map/gram/ppermute | solution.py:20
  84.0 3.7 %collective-permute-done.17 = f32[64,256]{1,0:T(8,128)S(1)} collective-permute-done((f32[64,256]{1,0:T(8,128)S(1)}, f32[64,256]{1,0:T(8,128)S(1)}, u32[]{:S(2)}, u32[]{:S(2)}) %collective-permute-start.17) | collective-permute-done | bytes 65568 | tf_op jit(solution)/shard_map/gram/ppermute | solution.py:20
  87.7 4.8 %collective-permute-start.21 = (f32[64,256]{1,0:T(8,128)S(1)}, f32[64,256]{1,0:T(8,128)S(1)}, u32[]{:S(2)}, u32[]{:S(2)}) collective-permute-start(f32[64,256]{1,0:T(8,128)S(1)} %add_add_fusion.2), channel_id=1, source_target_pairs={{60,32},{56,36},{52,40},{48,44},{44,48},{40,52},{36,56},{32,60},{6... | collective-permute-start | bytes 196616 | tf_op jit(solution)/shard_map/gram/ppermute | solution.py:20
  92.5 3.4 %collective-permute-start.20 = (f32[64,256]{1,0:T(8,128)S(1)}, f32[64,256]{1,0:T(8,128)S(1)}, u32[]{:S(2)}, u32[]{:S(2)}) collective-permute-start(f32[64,256]{1,0:T(8,128)S(1)} %add_add_fusion.2), channel_id=1, source_target_pairs={{56,32},{60,36},{48,40},{52,44},{40,48},{44,52},{32,56},{36,60},{5... | collective-permute-start | bytes 196616 | tf_op jit(solution)/shard_map/gram/ppermute | solution.py:20
  103.0 4.3 %collective-permute-done.22 = f32[64,256]{1,0:T(8,128)S(1)} collective-permute-done((f32[64,256]{1,0:T(8,128)S(1)}, f32[64,256]{1,0:T(8,128)S(1)}, u32[]{:S(2)}, u32[]{:S(2)}) %collective-permute-start.22) | collective-permute-done | bytes 65568 | tf_op jit(solution)/shard_map/gram/ppermute | solution.py:20
  107.3 5.1 %collective-permute-start.25 = (f32[64,256]{1,0:T(8,128)S(1)}, f32[64,256]{1,0:T(8,128)S(1)}, u32[]{:S(2)}, u32[]{:S(2)}) collective-permute-start(f32[64,256]{1,0:T(8,128)S(1)} %add.170), channel_id=1, source_target_pairs={{224,32},{160,96},{96,160},{32,224},{225,33},{161,97},{97,161},{33... | collective-permute-start | bytes 196616 | tf_op jit(solution)/shard_map/gram/ppermute | solution.py:19
  117.8 3.2 %collective-permute-done.25 = f32[64,256]{1,0:T(8,128)S(1)} collective-permute-done((f32[64,256]{1,0:T(8,128)S(1)}, f32[64,256]{1,0:T(8,128)S(1)}, u32[]{:S(2)}, u32[]{:S(2)}) %collective-permute-start.25) | collective-permute-done | bytes 65568 | tf_op jit(solution)/shard_map/gram/ppermute | solution.py:19
  125.1 2.7 %collective-permute-start.27 = (f32[64,256]{1,0:T(8,128)S(1)}, f32[64,256]{1,0:T(8,128)S(1)}, u32[]{:S(2)}, u32[]{:S(2)}) collective-permute-start(f32[64,256]{1,0:T(8,128)S(1)} %get-tuple-element.43), channel_id=1, source_target_pairs={{34,32},{35,33},{32,34},{33,35},{38,36},{39,37},{36,38},{37,39},{4... | collective-permute-start | bytes 196616 | tf_op jit(solution)/shard_map/gram/ppermute | solution.py:20
  127.9 2.5 %collective-permute-start.28 = (f32[64,256]{1,0:T(8,128)S(1)}, f32[64,256]{1,0:T(8,128)S(1)}, u32[]{:S(2)}, u32[]{:S(2)}) collective-permute-start(f32[64,256]{1,0:T(8,128)S(1)} %get-tuple-element.43), channel_id=1, source_target_pairs={{35,32},{32,33},{33,34},{34,35},{39,36},{36,37},{37,38},{38,39},{4... | collective-permute-start | bytes 196616 | tf_op jit(solution)/shard_map/gram/ppermute | solution.py:20
  131.6 2.8 %collective-permute-done.28 = f32[64,256]{1,0:T(8,128)S(1)} collective-permute-done((f32[64,256]{1,0:T(8,128)S(1)}, f32[64,256]{1,0:T(8,128)S(1)}, u32[]{:S(2)}, u32[]{:S(2)}) %collective-permute-start.28) | collective-permute-done | bytes 65568 | tf_op jit(solution)/shard_map/gram/ppermute | solution.py:20
  138.6 10.0 %factorize.1 = (f32[256,256]{1,0:T(8,128)}, bf16[256,256]{1,0:T(8,128)(2,1)S(1)}, bf16[256,256]{1,0:T(8,128)(2,1)S(1)}) custom-call(f32[256,256]{1,0:T(8,128)S(1)} %broadcast_select_fusion.refs_0_), custom_call_target="tpu_custom_call" | custom-call | flops 201326592 | bytes 524288 | tf_op jit(solution)/shard_map/gram/factorize/pallas_call | solution.py:139
  (82 shorter events, 50.6 us)
Async XLA Ops:
  9.5 7.2 %collective-permute-start.1 = (bf16[64,1024]{1,0:T(8,128)(2,1)S(1)}, bf16[64,1024]{1,0:T(8,128)(2,1)S(1)}, u32[]{:S(2)}, u32[]{:S(2)}) collective-permute-start(bf16[64,1024]{1,0:T(8,128)(2,1)S(1)} %get-tuple-element.24), channel_id=1, source_target_pairs={{3,0},{0,1},{1,2},{2,3},{7,4},{4,5},{5,6},{6,7},{11,8},{8,9},{9,10... | collective-permute-start | bytes 393224 | tf_op jit(solution)/shard_map/project/ppermute | solution.py:17
  9.8 6.9 %collective-permute-start.2 = (bf16[64,1024]{1,0:T(8,128)(2,1)S(1)}, bf16[64,1024]{1,0:T(8,128)(2,1)S(1)}, u32[]{:S(2)}, u32[]{:S(2)}) collective-permute-start(bf16[64,1024]{1,0:T(8,128)(2,1)S(1)} %get-tuple-element.25), channel_id=1, source_target_pairs={{1,0},{2,1},{3,2},{0,3},{5,4},{6,5},{7,6},{4,7},{9,8},{10,9},{11,1... | collective-permute-start | bytes 393224 | tf_op jit(solution)/shard_map/project/ppermute | solution.py:17
  16.8 7.0 %collective-permute-start.4 = (bf16[64,1024]{1,0:T(8,128)(2,1)S(1)}, bf16[64,1024]{1,0:T(8,128)(2,1)S(1)}, u32[]{:S(2)}, u32[]{:S(2)}) collective-permute-start(bf16[64,1024]{1,0:T(8,128)(2,1)S(1)} %get-tuple-element.46), channel_id=1, source_target_pairs={{4,0},{8,4},{12,8},{16,12},{20,16},{24,20},{28,24},{0,28},{5,1},{9... | collective-permute-start | bytes 393224 | tf_op jit(solution)/shard_map/project/ppermute | solution.py:17
  26.9 8.1 %collective-permute-start.5 = (bf16[64,1024]{1,0:T(8,128)(2,1)S(1)}, bf16[64,1024]{1,0:T(8,128)(2,1)S(1)}, u32[]{:S(2)}, u32[]{:S(2)}) collective-permute-start(bf16[64,1024]{1,0:T(8,128)(2,1)S(1)} %get-tuple-element.50), channel_id=1, source_target_pairs={{12,0},{16,4},{20,8},{24,12},{28,16},{0,20},{4,24},{8,28},{13,1},{... | collective-permute-start | bytes 393224 | tf_op jit(solution)/shard_map/project/ppermute | solution.py:17
  27.7 7.4 %collective-permute-start.6 = (bf16[64,1024]{1,0:T(8,128)(2,1)S(1)}, bf16[64,1024]{1,0:T(8,128)(2,1)S(1)}, u32[]{:S(2)}, u32[]{:S(2)}) collective-permute-start(bf16[64,1024]{1,0:T(8,128)(2,1)S(1)} %get-tuple-element.51), channel_id=1, source_target_pairs={{24,0},{28,4},{0,8},{4,12},{8,16},{12,20},{16,24},{20,28},{25,1},{... | collective-permute-start | bytes 393224 | tf_op jit(solution)/shard_map/project/ppermute | solution.py:17
  47.1 8.6 %collective-permute-start.10 = (bf16[1,256,512]{2,1,0:T(8,128)(2,1)S(1)}, bf16[1,256,512]{2,1,0:T(8,128)(2,1)S(1)}, u32[]{:S(2)}, u32[]{:S(2)}) collective-permute-start(bf16[1,256,512]{2,1,0:T(8,128)(2,1)S(1)} %get-tuple-element.29), channel_id=1, source_target_pairs={{32,0},{0,32},{33,1},{1,33},{34,2},{2,34},{35,3},{3,35},{36,4},{4,... | collective-permute-start | bytes 786440 | tf_op jit(solution)/shard_map/sketch/ppermute | solution.py:17
  55.7 6.4 %collective-permute-start.11 = (bf16[3,256,512]{2,1,0:T(8,128)(2,1)S(1)}, bf16[3,256,512]{2,1,0:T(8,128)(2,1)S(1)}, u32[]{:S(2)}, u32[]{:S(2)}) collective-permute-start(bf16[3,256,512]{2,1,0:T(8,128)(2,1)S(1)} %cross.4), channel_id=1, source_target_pairs={{32,0},{0,32},{33,1},{1,33},{34,2},{2,34},{35,3},{3,35},{36,4},{4,... | collective-permute-start | bytes 2359304 | tf_op jit(solution)/shard_map/sketch/ppermute | solution.py:17
  56.0 9.1 %collective-permute-start.12 = (bf16[256,512]{1,0:T(8,128)(2,1)S(1)}, bf16[256,512]{1,0:T(8,128)(2,1)S(1)}, u32[]{:S(2)}, u32[]{:S(2)}) collective-permute-start(bf16[256,512]{1,0:T(8,128)(2,1)S(1)} %combine.2), channel_id=1, source_target_pairs={{128,0},{192,64},{0,128},{64,192},{129,1},{193,65},{1,129},{65,193... | collective-permute-start | bytes 786440 | tf_op jit(solution)/shard_map/sketch/ppermute | solution.py:17
  62.3 8.5 %collective-permute-start.13 = (bf16[256,512]{1,0:T(8,128)(2,1)S(1)}, bf16[256,512]{1,0:T(8,128)(2,1)S(1)}, u32[]{:S(2)}, u32[]{:S(2)}) collective-permute-start(bf16[256,512]{1,0:T(8,128)(2,1)S(1)} %get-tuple-element.33), channel_id=1, source_target_pairs={{192,0},{0,64},{64,128},{128,192},{193,1},{1,65},{65,129},{129,193... | collective-permute-start | bytes 786440 | tf_op jit(solution)/shard_map/sketch/ppermute | solution.py:17
  62.7 8.4 %collective-permute-start.14 = (bf16[256,512]{1,0:T(8,128)(2,1)S(1)}, bf16[256,512]{1,0:T(8,128)(2,1)S(1)}, u32[]{:S(2)}, u32[]{:S(2)}) collective-permute-start(bf16[256,512]{1,0:T(8,128)(2,1)S(1)} %get-tuple-element.34), channel_id=1, source_target_pairs={{64,0},{128,64},{192,128},{0,192},{65,1},{129,65},{193,129},{1,193... | collective-permute-start | bytes 786440 | tf_op jit(solution)/shard_map/sketch/ppermute | solution.py:17
  75.4 8.5 %collective-permute-start.16 = (f32[64,256]{1,0:T(8,128)S(1)}, f32[64,256]{1,0:T(8,128)S(1)}, u32[]{:S(2)}, u32[]{:S(2)}) collective-permute-start(f32[64,256]{1,0:T(8,128)S(1)} %get-tuple-element.52), channel_id=1, source_target_pairs={{34,32},{35,33},{32,34},{33,35},{38,36},{39,37},{36,38},{37,39},{4... | collective-permute-start | bytes 196616 | tf_op jit(solution)/shard_map/gram/ppermute | solution.py:20
  87.7 11.5 %collective-permute-start.21 = (f32[64,256]{1,0:T(8,128)S(1)}, f32[64,256]{1,0:T(8,128)S(1)}, u32[]{:S(2)}, u32[]{:S(2)}) collective-permute-start(f32[64,256]{1,0:T(8,128)S(1)} %add_add_fusion.2), channel_id=1, source_target_pairs={{60,32},{56,36},{52,40},{48,44},{44,48},{40,52},{36,56},{32,60},{6... | collective-permute-start | bytes 196616 | tf_op jit(solution)/shard_map/gram/ppermute | solution.py:20
  92.5 7.1 %collective-permute-start.20 = (f32[64,256]{1,0:T(8,128)S(1)}, f32[64,256]{1,0:T(8,128)S(1)}, u32[]{:S(2)}, u32[]{:S(2)}) collective-permute-start(f32[64,256]{1,0:T(8,128)S(1)} %add_add_fusion.2), channel_id=1, source_target_pairs={{56,32},{60,36},{48,40},{52,44},{40,48},{44,52},{32,56},{36,60},{5... | collective-permute-start | bytes 196616 | tf_op jit(solution)/shard_map/gram/ppermute | solution.py:20
  97.9 19.0 %collective-permute-start.30 = (bf16[512,256]{1,0:T(8,128)(2,1)S(1)}, bf16[512,256]{1,0:T(8,128)(2,1)S(1)}, u32[]{:S(2)}, u32[]{:S(2)}) collective-permute-start(bf16[512,256]{1,0:T(8,128)(2,1)S(1)} %get-tuple-element.36), channel_id=1, source_target_pairs={{32,0},{33,1},{34,2},{35,3},{36,4},{37,5},{38,6},{39,7},{40,8},{41... | collective-permute-start | bytes 786440 | tf_op jit(solution)/shard_map/gram/ppermute | solution.py:401
  107.3 13.6 %collective-permute-start.25 = (f32[64,256]{1,0:T(8,128)S(1)}, f32[64,256]{1,0:T(8,128)S(1)}, u32[]{:S(2)}, u32[]{:S(2)}) collective-permute-start(f32[64,256]{1,0:T(8,128)S(1)} %add.170), channel_id=1, source_target_pairs={{224,32},{160,96},{96,160},{32,224},{225,33},{161,97},{97,161},{33... | collective-permute-start | bytes 196616 | tf_op jit(solution)/shard_map/gram/ppermute | solution.py:19
  112.4 8.5 %collective-permute-start.24 = (f32[64,256]{1,0:T(8,128)S(1)}, f32[64,256]{1,0:T(8,128)S(1)}, u32[]{:S(2)}, u32[]{:S(2)}) collective-permute-start(f32[64,256]{1,0:T(8,128)S(1)} %add.170), channel_id=1, source_target_pairs={{160,32},{224,96},{32,160},{96,224},{161,33},{225,97},{33,161},{97... | collective-permute-start | bytes 196616 | tf_op jit(solution)/shard_map/gram/ppermute | solution.py:19
  114.5 6.4 %collective-permute-start.23 = (f32[64,256]{1,0:T(8,128)S(1)}, f32[64,256]{1,0:T(8,128)S(1)}, u32[]{:S(2)}, u32[]{:S(2)}) collective-permute-start(f32[64,256]{1,0:T(8,128)S(1)} %add.170), channel_id=1, source_target_pairs={{96,32},{32,96},{224,160},{160,224},{97,33},{33,97},{225,161},{161... | collective-permute-start | bytes 196616 | tf_op jit(solution)/shard_map/gram/ppermute | solution.py:19
  117.1 18.7 %collective-permute-start.31 = (bf16[2,512,256]{2,1,0:T(8,128)(2,1)S(1)}, bf16[2,512,256]{2,1,0:T(8,128)(2,1)S(1)}, u32[]{:S(2)}, u32[]{:S(2)}) collective-permute-start(bf16[2,512,256]{2,1,0:T(8,128)(2,1)S(1)} %get-tuple-element.48), channel_id=1, source_target_pairs={{64,0},{128,64},{192,128},{0,192},{65,1},{129,65},{193,129},{1,193... | collective-permute-start | bytes 1572872 | tf_op jit(solution)/shard_map/gram/ppermute | solution.py:19
  121.0 6.8 %collective-permute-start.26 = (f32[64,256]{1,0:T(8,128)S(1)}, f32[64,256]{1,0:T(8,128)S(1)}, u32[]{:S(2)}, u32[]{:S(2)}) collective-permute-start(f32[64,256]{1,0:T(8,128)S(1)} %get-tuple-element.43), channel_id=1, source_target_pairs={{33,32},{34,33},{35,34},{32,35},{37,36},{38,37},{39,38},{36,39},{4... | collective-permute-start | bytes 196616 | tf_op jit(solution)/shard_map/gram/ppermute | solution.py:20
  122.9 12.9 %collective-permute-start.32 = (bf16[2,512,256]{2,1,0:T(8,128)(2,1)S(1)}, bf16[2,512,256]{2,1,0:T(8,128)(2,1)}, u32[]{:S(2)}, u32[]{:S(2)}) collective-permute-start(bf16[2,512,256]{2,1,0:T(8,128)(2,1)S(1)} %get-tuple-element.48), channel_id=1, source_target_pairs={{128,0},{192,64},{0,128},{64,192},{129,1},{193,65},{1,129},{65,193... | collective-permute-start | bytes 1572872 | tf_op jit(solution)/shard_map/gram/ppermute | solution.py:19
  124.4 12.5 %collective-permute-start.33 = (bf16[2,512,256]{2,1,0:T(8,128)(2,1)S(1)}, bf16[2,512,256]{2,1,0:T(8,128)(2,1)S(1)}, u32[]{:S(2)}, u32[]{:S(2)}) collective-permute-start(bf16[2,512,256]{2,1,0:T(8,128)(2,1)S(1)} %get-tuple-element.48), channel_id=1, source_target_pairs={{192,0},{0,64},{64,128},{128,192},{193,1},{1,65},{65,129},{129,193... | collective-permute-start | bytes 1572872 | tf_op jit(solution)/shard_map/gram/ppermute | solution.py:19
  125.1 6.5 %collective-permute-start.27 = (f32[64,256]{1,0:T(8,128)S(1)}, f32[64,256]{1,0:T(8,128)S(1)}, u32[]{:S(2)}, u32[]{:S(2)}) collective-permute-start(f32[64,256]{1,0:T(8,128)S(1)} %get-tuple-element.43), channel_id=1, source_target_pairs={{34,32},{35,33},{32,34},{33,35},{38,36},{39,37},{36,38},{37,39},{4... | collective-permute-start | bytes 196616 | tf_op jit(solution)/shard_map/gram/ppermute | solution.py:20
  127.9 6.6 %collective-permute-start.28 = (f32[64,256]{1,0:T(8,128)S(1)}, f32[64,256]{1,0:T(8,128)S(1)}, u32[]{:S(2)}, u32[]{:S(2)}) collective-permute-start(f32[64,256]{1,0:T(8,128)S(1)} %get-tuple-element.43), channel_id=1, source_target_pairs={{35,32},{32,33},{33,34},{34,35},{39,36},{36,37},{37,38},{38,39},{4... | collective-permute-start | bytes 196616 | tf_op jit(solution)/shard_map/gram/ppermute | solution.py:20
  137.0 11.6 %collective-permute-start.34 = (bf16[4096,256]{1,0:T(8,128)(2,1)S(1)}, bf16[4096,256]{1,0:T(8,128)(2,1)S(1)}, u32[]{:S(2)}, u32[]{:S(2)}) collective-permute-start(bf16[4096,256]{1,0:T(8,128)(2,1)S(1)} %bitcast.8), channel_id=1, source_target_pairs={{0,32},{1,33},{2,34},{3,35},{4,36},{5,37},{6,38},{7,39},{8,40},{9,... | collective-permute-start | bytes 6291464 | tf_op jit(solution)/shard_map/gram/ppermute | solution.py:410
  (12 other events, 88.5 us)

commit v6 on v4

--- a/solution.py
+++ b/solution.py
@@ -11,27 +11,38 @@
 EXACT = lax.Precision.HIGHEST
 
 
-def shifted(x, axis, by):
+def moved(x, axis, source, mixed):
     n = lax.axis_size(axis)
-    return lax.ppermute(x, axis, [((i + by) % n, i) for i in range(n)])
-
-
-def swapped(x, axis, mask):
-    n = lax.axis_size(axis)
-    return lax.ppermute(x, axis, [(i ^ mask, i) for i in range(n)])
+    if not mixed:
+        return lax.ppermute(x, axis, [(source(i, n), i) for i in range(n)])
+    pairs = []
+    for i in range(n):
+        for c in range(2):
+            j = source(i, n)
+            d = c ^ ((i + j) % 2)
+            pairs.append((2 * j + d, 2 * i + c) if axis == "y" else (d * n + j, c * n + i))
+    return lax.ppermute(x, (axis, "c") if axis == "y" else ("c", axis), pairs)
+
+
+def shifted(x, axis, by, mixed=False):
+    return moved(x, axis, lambda i, n: (i + by) % n, mixed)
+
+
+def swapped(x, axis, mask, mixed=False):
+    return moved(x, axis, lambda i, n: i ^ mask, mixed)
 
 
 def piece(x, index, size):
     return lax.dynamic_slice_in_dim(x, index * size, size, axis=0)
 
 
-def scatter_sum(x, axis):
+def scatter_sum(x, axis, mixed):
     n = lax.axis_size(axis)
     me = lax.axis_index(axis)
     size = x.shape[0] // n
-    total = piece(x, me, size).astype(F32)
-    for by in (2, 1, 3) if n == 4 else (1,):
-        total = total + shifted(piece(x, (me + by) % n, size), axis, n - by).astype(F32)
+    total = piece(x, me, size)
+    for by in (2, 1, 3):
+        total = total + shifted(piece(x, (me + by) % n, size), axis, n - by, mixed)
     return total
 
 
@@ -45,10 +56,17 @@
     return out
 
 
-def gather(x, axis):
-    n = lax.axis_size(axis)
-    came = {k: shifted(x, axis, k) for k in ((2, 1, 3) if n == 4 else (1,))}
-    return placed([x] + [came[k] for k in range(1, n)], axis)
+def gather(x, axis, mixed=False):
+    came = {k: shifted(x, axis, k, mixed) for k in (2, 1, 3)}
+    return placed([x] + [came[k] for k in (1, 2, 3)], axis)
+
+
+def gather_cores(x, place):
+    other = swapped(x, "c", 1)
+    size = x.shape[0]
+    out = jnp.zeros((2 * size, x.shape[1]), x.dtype)
+    out = lax.dynamic_update_slice_in_dim(out, x, place * size, axis=0)
+    return lax.dynamic_update_slice_in_dim(out, other, (1 - place) * size, axis=0)
 
 
 def ring_sum(x, axis):
@@ -63,7 +81,7 @@
 
 
 def exact_sum(x, axis, masks):
-    came = [swapped(x, axis, mask) for mask in masks]
+    came = [swapped(x, axis, mask, True) for mask in masks]
     return x + came[0] if len(came) == 1 else (x + came[0]) + (came[1] + came[2])
 
 
@@ -295,20 +313,20 @@
     )(own, came)
 
 
-def gram_kernel(core_ref, own_ref, came_ref, a_ref, b_ref, d_ref, keep_ref, send_ref, rows_ref, work):
+def gram_kernel(side_ref, own_ref, came_ref, a_ref, b_ref, d_ref, keep_ref, send_ref, rows_ref, work):
     total = own_ref[own_ref.shape[0] - 1] + came_ref[own_ref.shape[0] - 1].astype(F32)
     total = total + (a_ref[...].astype(F32) + b_ref[...].astype(F32) + d_ref[...].astype(F32))
     half = keep_ref.shape[0]
-    core = core_ref[0]
+    side = side_ref[0]
     work[...] = lax.dot_general(
         total, total, (((1,), (1,)), ((), ())), precision=EXACT, preferred_element_type=F32
     )
-    keep_ref[...] = work[pl.ds(pl.multiple_of(core * half, half), half), :]
-    send_ref[...] = work[pl.ds(pl.multiple_of((1 - core) * half, half), half), :]
+    keep_ref[...] = work[pl.ds(pl.multiple_of(side * half, half), half), :]
+    send_ref[...] = work[pl.ds(pl.multiple_of((1 - side) * half, half), half), :]
     rows_ref[...] = jnp.transpose(total).astype(BF16)
 
 
-def gram_of(core, own, came, others):
+def gram_of(side, own, came, others):
     columns, block = own.shape[1:]
     whole = pl.BlockSpec(memory_space=pltpu.VMEM)
     half = jax.ShapeDtypeStruct((columns // 2, columns), F32)
@@ -320,7 +338,7 @@
         scratch_shapes=[pltpu.VMEM((columns, columns), F32)],
         compiler_params=pltpu.CompilerParams(vmem_limit_bytes=16 * 2**20),
         name="gram",
-    )(core, own, came, *others)
+    )(side, own, came, *others)
 
 
 def basis_kernel(parts, sketch_ref, high_ref, low_ref, out_hbm, work, sems):
@@ -389,21 +407,22 @@
         others += [shifted(pieces[0], "y", -1), shifted(pieces[1], "y", -3)]
 
     with jax.named_scope("gram"):
-        keep, send, mine = gram_of(c[None], own, came, others)
+        side = (c + lax.axis_index("x") + y + lax.axis_index("z")) % 2
+        keep, send, mine = gram_of(side[None], own, came, others)
         slab = keep + swapped(send, "c", 1)
         slab, mine = lax.optimization_barrier((slab, mine))
         across = shifted(mine, "y", 2)
-        slab = scatter_sum(slab, "x")
+        slab = scatter_sum(slab, "x", True)
         slab, across = lax.optimization_barrier((slab, across))
         ahead, behind = shifted(mine, "y", 1), shifted(mine, "y", -1)
         slab = exact_sum(slab, "z", (1, 6, 7))
         slab = exact_sum(slab, "z", (2,))
         slab, ahead, behind = lax.optimization_barrier((slab, ahead, behind))
         slab = exact_sum(slab, "y", (1, 2, 3))
-        gram = gather(gather(slab, "x"), "c")
+        gram = gather_cores(gather(slab, "x", True), side)
         whole = placed((mine, ahead, across, behind), "y")
         gram, whole = lax.optimization_barrier((gram, whole))
-        whole = gather(whole, "c")
+        whole = gather_cores(whole, c)
         upper, high, low = factorize(gram, feature_total**0.5)
     return (basis_of(whole, high, low), upper)
 

time: 130 us -> 132 us (1.015)
  starting transfers between devices: 61.1 us -> 55.8 us
  waiting for transfers between devices: 39.6 us -> 43.5 us
  local copies, waits for them, and re-layouts: 0.63 us -> 2.29 us
  Pallas kernels: 27.2 us -> 28.6 us
    ppermute x34, starting transfers between devices: 61.1 us -> 55.8 us  [the longest x21 37.9 us: moved(): return lax.ppermute(x, axis, [(source(i, n), i) for i in range(n)])]
    ppermute x34, waiting for transfers between devices: 39.6 us -> 43.5 us  [the longest x21 31.6 us: moved(): return lax.ppermute(x, axis, [(source(i, n), i) for i in range(n)])]
    unnamed x2 -> x6, local copies, waits for them, and re-layouts: 0.01 us -> 1.66 us
  transfers between devices with their start and end apart: 34 -> 34, of which waited for: 21 -> 20; matrix products, arithmetic and copies ran while one was open for 0% -> 0% of each run, Pallas kernels for 13% -> 13%
where the time goes in v6:
time: 132 us
  starting transfers between devices  55.8 us (42%)
  waiting for transfers between devices  43.5 us (33%)
  Pallas kernels  28.6 us (22%)
  local copies, waits for them, and re-layouts  2.29 us (2%)
    ppermute x21, starting transfers between devices, moved(): return lax.ppermute(x, axis, [(source(i, n), i) for i in range(n)])  37.9 us
    ppermute x21, waiting for transfers between devices, moved(): return lax.ppermute(x, axis, [(source(i, n), i) for i in range(n)])  31.6 us
    ppermute x13, starting transfers between devices, moved(): return lax.ppermute(x, (axis, 'c') if axis == 'y' else ('c', axis), pairs)  17.9 us
    ppermute x13, waiting for transfers between devices, moved(): return lax.ppermute(x, (axis, 'c') if axis == 'y' else ('c', axis), pairs)  12 us
    pallas_call x1, Pallas kernels, factorize(): pl.pallas_call(lambda *refs: factor_kernel(scale, *refs), out_shape=[jax....  10 us
    pallas_call x3, Pallas kernels, cross(): pl.pallas_call(lambda *refs: cross_kernel(jobs, *refs), in_specs=[pl.Bloc...  8.93 us
    pallas_call x1, Pallas kernels, project(): pl.pallas_call(lambda *refs: project_kernel(parts, *refs), in_specs=[pl.B...  5.16 us
  transfers between devices with their start and end apart: 34, of which 20 were waited for; matrix products, arithmetic and copies ran while one was open for 0% of the time, Pallas kernels for 13%

profile of v6, /device:TPU:1, one launch (start us, length us, event | category | flops | bytes accessed | tf_op | source)
XLA Modules:
  0.0 131.6 jit_solution(9204712394030731283)
XLA Ops:
  0.6 5.2 %project.1 = (f32[64,1024]{1,0:T(8,128)S(1)}, bf16[64,1024]{1,0:T(8,128)(2,1)S(1)}, bf16[64,1024]{1,0:T(8,128)(2,1)S(1)}, bf16[64,1024]{1,0:T(8,128)(2,1)S(1)}) custom-call(s32[1]{0:T(128)} %bitcast.3.refs_0_, bf16[512,4096]{1,0:T(8,128)(2,1)} %refs_2_.7, bf16[512,4096]{1,0:T(8,128)(2,1)} %refs_3_.7, bf16[4096,256]{1,0:T(8,128)(2,1)} %refs_3_.4, ...), custom_call_target="tpu_custom_call" | custom-call | flops 2147483648 | bytes 8388608 | tf_op jit(solution)/shard_map/project/project/pallas_call | solution.py:219
  5.8 3.7 %collective-permute-start = (bf16[64,1024]{1,0:T(8,128)(2,1)S(1)}, bf16[64,1024]{1,0:T(8,128)(2,1)S(1)}, u32[]{:S(2)}, u32[]{:S(2)}) collective-permute-start(bf16[64,1024]{1,0:T(8,128)(2,1)S(1)} %get-tuple-element.31), channel_id=1, source_target_pairs={{2,0},{3,1},{0,2},{1,3},{6,4},{7,5},{4,6},{5,7},{10,8},{11,9},{8,1... | collective-permute-start | bytes 393224 | tf_op jit(solution)/shard_map/project/ppermute | solution.py:17
  9.8 2.4 %collective-permute-start.2 = (bf16[64,1024]{1,0:T(8,128)(2,1)S(1)}, bf16[64,1024]{1,0:T(8,128)(2,1)S(1)}, u32[]{:S(2)}, u32[]{:S(2)}) collective-permute-start(bf16[64,1024]{1,0:T(8,128)(2,1)S(1)} %get-tuple-element.33), channel_id=1, source_target_pairs={{1,0},{2,1},{3,2},{0,3},{5,4},{6,5},{7,6},{4,7},{9,8},{10,9},{11,1... | collective-permute-start | bytes 393224 | tf_op jit(solution)/shard_map/project/ppermute | solution.py:17
  12.2 4.5 %collective-permute-done.1 = bf16[64,1024]{1,0:T(8,128)(2,1)S(1)} collective-permute-done((bf16[64,1024]{1,0:T(8,128)(2,1)S(1)}, bf16[64,1024]{1,0:T(8,128)(2,1)S(1)}, u32[]{:S(2)}, u32[]{:S(2)}) %collective-permute-start.1) | collective-permute-done | bytes 131104 | tf_op jit(solution)/shard_map/project/ppermute | solution.py:17
  17.9 4.0 %collective-permute-start.4 = (bf16[64,1024]{1,0:T(8,128)(2,1)S(1)}, bf16[64,1024]{1,0:T(8,128)(2,1)S(1)}, u32[]{:S(2)}, u32[]{:S(2)}) collective-permute-start(bf16[64,1024]{1,0:T(8,128)(2,1)S(1)} %get-tuple-element.62), channel_id=1, source_target_pairs={{4,0},{8,4},{12,8},{16,12},{20,16},{24,20},{28,24},{0,28},{5,1},{9... | collective-permute-start | bytes 393224 | tf_op jit(solution)/shard_map/project/ppermute | solution.py:17
  21.9 2.6 %collective-permute-done.3 = bf16[64,1024]{1,0:T(8,128)(2,1)S(1)} collective-permute-done((bf16[64,1024]{1,0:T(8,128)(2,1)S(1)}, bf16[64,1024]{1,0:T(8,128)(2,1)S(1)}, u32[]{:S(2)}, u32[]{:S(2)}) %collective-permute-start.3) | collective-permute-done | bytes 131104 | tf_op jit(solution)/shard_map/project/ppermute | solution.py:17
  24.6 3.1 %collective-permute-start.5 = (bf16[64,1024]{1,0:T(8,128)(2,1)S(1)}, bf16[64,1024]{1,0:T(8,128)(2,1)S(1)}, u32[]{:S(2)}, u32[]{:S(2)}) collective-permute-start(bf16[64,1024]{1,0:T(8,128)(2,1)S(1)} %get-tuple-element.64), channel_id=1, source_target_pairs={{12,0},{16,4},{20,8},{24,12},{28,16},{0,20},{4,24},{8,28},{13,1},{... | collective-permute-start | bytes 393224 | tf_op jit(solution)/shard_map/project/ppermute | solution.py:17
  29.2 7.5 %collective-permute-done.5 = bf16[64,1024]{1,0:T(8,128)(2,1)S(1)} collective-permute-done((bf16[64,1024]{1,0:T(8,128)(2,1)S(1)}, bf16[64,1024]{1,0:T(8,128)(2,1)S(1)}, u32[]{:S(2)}, u32[]{:S(2)}) %collective-permute-start.5) | collective-permute-done | bytes 131104 | tf_op jit(solution)/shard_map/project/ppermute | solution.py:17
  37.5 3.8 %collective-permute-start.8 = (bf16[64,1024]{1,0:T(8,128)(2,1)S(1)}, bf16[64,1024]{1,0:T(8,128)(2,1)S(1)}, u32[]{:S(2)}, u32[]{:S(2)}) collective-permute-start(bf16[64,1024]{1,0:T(8,128)(2,1)S(1)} %get-tuple-element.61), channel_id=1, source_target_pairs={{2,0},{3,1},{0,2},{1,3},{6,4},{7,5},{4,6},{5,7},{10,8},{11,9},{8,1... | collective-permute-start | bytes 393224 | tf_op jit(solution)/shard_map/project/ppermute | solution.py:17
  43.7 2.7 %collective-permute-done.9 = bf16[64,1024]{1,0:T(8,128)(2,1)S(1)} collective-permute-done((bf16[64,1024]{1,0:T(8,128)(2,1)S(1)}, bf16[64,1024]{1,0:T(8,128)(2,1)S(1)}, u32[]{:S(2)}, u32[]{:S(2)}) %collective-permute-start.9) | collective-permute-done | bytes 131104 | tf_op jit(solution)/shard_map/project/ppermute | solution.py:17
  46.4 2.7 %cross.3 = (bf16[1,256,512]{2,1,0:T(8,128)(2,1)S(1)}, f32[1,256,512]{2,1,0:T(8,128)S(1)}) custom-call(s32[2]{0:T(128)S(1)} %pad_add_fusion.refs_0_, bf16[256,1024]{1,0:T(8,128)(2,1)S(1)} %constant_dynamic-update-slice_fusion.12.refs_1_, bf16[512,4096]{1,0:T(8,128)(2,1)} %refs_2_.7, bf16[512,4096]{1,0:T(8,128)(2,1)} %refs_3_.7, f32[1,4096]{1,0:T(1,128)S(1)} %bitcast.6), custom_call_target="tpu_custom_call" | custom-call | flops 536870912 | bytes 2097152 | tf_op jit(solution)/shard_map/sketch/cross/pallas_call | solution.py:279
  49.1 4.5 %collective-permute-start.10 = (bf16[1,256,512]{2,1,0:T(8,128)(2,1)S(1)}, bf16[1,256,512]{2,1,0:T(8,128)(2,1)S(1)}, u32[]{:S(2)}, u32[]{:S(2)}) collective-permute-start(bf16[1,256,512]{2,1,0:T(8,128)(2,1)S(1)} %get-tuple-element.37), channel_id=1, source_target_pairs={{32,0},{0,32},{33,1},{1,33},{34,2},{2,34},{35,3},{3,35},{36,4},{4,... | collective-permute-start | bytes 786440 | tf_op jit(solution)/shard_map/sketch/ppermute | solution.py:17
  53.6 3.1 %cross.4 = bf16[3,256,512]{2,1,0:T(8,128)(2,1)S(1)} custom-call(s32[2]{0:T(128)S(1)} %pad_add_fusion.refs_0_, bf16[256,1024]{1,0:T(8,128)(2,1)S(1)} %constant_dynamic-update-slice_fusion.12.refs_1_, bf16[512,4096]{1,0:T(8,128)(2,1)} %refs_2_.7, bf16[512,4096]{1,0:T(8,128)(2,1)} %refs_3_.7, f32[1,4096]{1,0:T(1,128)S(1)} %bitcast.7), custom_call_target="tpu_custom_call" | custom-call | flops 805306368 | bytes 3145728 | tf_op jit(solution)/shard_map/sketch/cross/pallas_call | solution.py:279
  57.1 3.0 %collective-permute-start.12 = (bf16[256,512]{1,0:T(8,128)(2,1)S(1)}, bf16[256,512]{1,0:T(8,128)(2,1)S(1)}, u32[]{:S(2)}, u32[]{:S(2)}) collective-permute-start(bf16[256,512]{1,0:T(8,128)(2,1)S(1)} %combine.2), channel_id=1, source_target_pairs={{128,0},{192,64},{0,128},{64,192},{129,1},{193,65},{1,129},{65,193... | collective-permute-start | bytes 786440 | tf_op jit(solution)/shard_map/sketch/ppermute | solution.py:17
  60.1 3.1 %cross.5.own_ref = f32[3,256,512]{2,1,0:T(8,128)S(1)} custom-call(s32[2]{0:T(128)S(1)} %pad_add_fusion.refs_0_, bf16[256,1024]{1,0:T(8,128)(2,1)S(1)} %constant_dynamic-update-slice_fusion.12.refs_1_, bf16[512,4096]{1,0:T(8,128)(2,1)} %refs_2_.7, bf16[512,4096]{1,0:T(8,128)(2,1)} %refs_3_.7, f32[1,4096]{1,0:T(1,128)S(1)} %bitcast.8), custom_call_target="tpu_custom_call" | custom-call | flops 805306368 | bytes 3145728 | tf_op jit(solution)/shard_map/sketch/cross/pallas_call | solution.py:279
  64.5 2.3 %collective-permute-start.14 = (bf16[256,512]{1,0:T(8,128)(2,1)}, bf16[256,512]{1,0:T(8,128)(2,1)S(1)}, u32[]{:S(2)}, u32[]{:S(2)}) collective-permute-start(bf16[256,512]{1,0:T(8,128)(2,1)} %get-tuple-element.42), channel_id=1, source_target_pairs={{64,0},{128,64},{192,128},{0,192},{65,1},{129,65},{193,129},{1,193... | collective-permute-start | bytes 786440 | tf_op jit(solution)/shard_map/sketch/ppermute | solution.py:17
  66.8 5.9 %collective-permute-done.13.b_ref = bf16[256,512]{1,0:T(8,128)(2,1)S(1)} collective-permute-done((bf16[256,512]{1,0:T(8,128)(2,1)}, bf16[256,512]{1,0:T(8,128)(2,1)S(1)}, u32[]{:S(2)}, u32[]{:S(2)}) %collective-permute-start.13) | collective-permute-done | bytes 262176 | tf_op jit(solution)/shard_map/sketch/ppermute | solution.py:17
  87.6 3.3 %collective-permute-start.21 = (f32[32,256]{1,0:T(8,128)S(1)}, f32[32,256]{1,0:T(8,128)S(1)}, u32[]{:S(2)}, u32[]{:S(2)}) collective-permute-start(f32[32,256]{1,0:T(8,128)S(1)} %add_add_fusion.2), channel_id=1, source_target_pairs={{24,0},{56,32},{28,4},{60,36},{16,8},{48,40},{20,12},{52,44},{8,16... | collective-permute-start | bytes 98312 | tf_op jit(solution)/shard_map/gram/ppermute | solution.py:24
  92.0 2.7 %collective-permute-start.24 = (bf16[512,256]{1,0:T(8,128)(2,1)S(1)}, bf16[512,256]{1,0:T(8,128)(2,1)S(1)}, u32[]{:S(2)}, u32[]{:S(2)}) collective-permute-start(bf16[512,256]{1,0:T(8,128)(2,1)S(1)} %get-tuple-element.47), channel_id=1, source_target_pairs={{64,0},{128,64},{192,128},{0,192},{65,1},{129,65},{193,129},{1,193... | collective-permute-start | bytes 786440 | tf_op jit(solution)/shard_map/gram/ppermute | solution.py:17
  95.5 2.9 %collective-permute-start.23 = (f32[32,256]{1,0:T(8,128)S(1)}, f32[32,256]{1,0:T(8,128)S(1)}, u32[]{:S(2)}, u32[]{:S(2)}) collective-permute-start(f32[32,256]{1,0:T(8,128)S(1)} %add_add_fusion.1), channel_id=1, source_target_pairs={{8,0},{40,32},{12,4},{44,36},{0,8},{32,40},{4,12},{36,44},{24,16},... | collective-permute-start | bytes 98312 | tf_op jit(solution)/shard_map/gram/ppermute | solution.py:24
  99.6 2.9 %collective-permute-done.25 = bf16[512,256]{1,0:T(8,128)(2,1)S(1)} collective-permute-done((bf16[512,256]{1,0:T(8,128)(2,1)S(1)}, bf16[512,256]{1,0:T(8,128)(2,1)S(1)}, u32[]{:S(2)}, u32[]{:S(2)}) %collective-permute-start.25) | collective-permute-done | bytes 262176 | tf_op jit(solution)/shard_map/gram/ppermute | solution.py:17
  103.3 2.4 %collective-permute-start.27 = (f32[32,256]{1,0:T(8,128)S(1)}, f32[32,256]{1,0:T(8,128)S(1)}, u32[]{:S(2)}, u32[]{:S(2)}) collective-permute-start(f32[32,256]{1,0:T(8,128)S(1)} %add.209), channel_id=1, source_target_pairs={{128,0},{160,32},{192,64},{224,96},{0,128},{32,160},{64,192},{96,2... | collective-permute-start | bytes 98312 | tf_op jit(solution)/shard_map/gram/ppermute | solution.py:24
  107.6 2.7 %collective-permute-done.28 = f32[32,256]{1,0:T(8,128)S(1)} collective-permute-done((f32[32,256]{1,0:T(8,128)S(1)}, f32[32,256]{1,0:T(8,128)S(1)}, u32[]{:S(2)}, u32[]{:S(2)}) %collective-permute-start.28) | collective-permute-done | bytes 32800 | tf_op jit(solution)/shard_map/gram/ppermute | solution.py:24
  118.8 10.0 %factorize.1 = (f32[256,256]{1,0:T(8,128)}, bf16[256,256]{1,0:T(8,128)(2,1)S(1)}, bf16[256,256]{1,0:T(8,128)(2,1)S(1)}) custom-call(f32[256,256]{1,0:T(8,128)S(1)} %constant_dynamic-update-slice_fusion.6.refs_0_), custom_call_target="tpu_custom_call" | custom-call | flops 201326592 | bytes 524288 | tf_op jit(solution)/shard_map/gram/factorize/pallas_call | solution.py:149
  (89 shorter events, 39.7 us)
Async XLA Ops:
  5.8 6.3 %collective-permute-start = (bf16[64,1024]{1,0:T(8,128)(2,1)S(1)}, bf16[64,1024]{1,0:T(8,128)(2,1)S(1)}, u32[]{:S(2)}, u32[]{:S(2)}) collective-permute-start(bf16[64,1024]{1,0:T(8,128)(2,1)S(1)} %get-tuple-element.31), channel_id=1, source_target_pairs={{2,0},{3,1},{0,2},{1,3},{6,4},{7,5},{4,6},{5,7},{10,8},{11,9},{8,1... | collective-permute-start | bytes 393224 | tf_op jit(solution)/shard_map/project/ppermute | solution.py:17
  9.5 7.2 %collective-permute-start.1 = (bf16[64,1024]{1,0:T(8,128)(2,1)S(1)}, bf16[64,1024]{1,0:T(8,128)(2,1)S(1)}, u32[]{:S(2)}, u32[]{:S(2)}) collective-permute-start(bf16[64,1024]{1,0:T(8,128)(2,1)S(1)} %get-tuple-element.32), channel_id=1, source_target_pairs={{3,0},{0,1},{1,2},{2,3},{7,4},{4,5},{5,6},{6,7},{11,8},{8,9},{9,10... | collective-permute-start | bytes 393224 | tf_op jit(solution)/shard_map/project/ppermute | solution.py:17
  9.8 6.9 %collective-permute-start.2 = (bf16[64,1024]{1,0:T(8,128)(2,1)S(1)}, bf16[64,1024]{1,0:T(8,128)(2,1)S(1)}, u32[]{:S(2)}, u32[]{:S(2)}) collective-permute-start(bf16[64,1024]{1,0:T(8,128)(2,1)S(1)} %get-tuple-element.33), channel_id=1, source_target_pairs={{1,0},{2,1},{3,2},{0,3},{5,4},{6,5},{7,6},{4,7},{9,8},{10,9},{11,1... | collective-permute-start | bytes 393224 | tf_op jit(solution)/shard_map/project/ppermute | solution.py:17
  16.7 7.8 %collective-permute-start.3 = (bf16[64,1024]{1,0:T(8,128)(2,1)S(1)}, bf16[64,1024]{1,0:T(8,128)(2,1)S(1)}, u32[]{:S(2)}, u32[]{:S(2)}) collective-permute-start(bf16[64,1024]{1,0:T(8,128)(2,1)S(1)} %get-tuple-element.62), channel_id=1, source_target_pairs={{28,0},{0,4},{4,8},{8,12},{12,16},{16,20},{20,24},{24,28},{29,1},{... | collective-permute-start | bytes 393224 | tf_op jit(solution)/shard_map/project/ppermute | solution.py:17
  17.9 6.6 %collective-permute-start.4 = (bf16[64,1024]{1,0:T(8,128)(2,1)S(1)}, bf16[64,1024]{1,0:T(8,128)(2,1)S(1)}, u32[]{:S(2)}, u32[]{:S(2)}) collective-permute-start(bf16[64,1024]{1,0:T(8,128)(2,1)S(1)} %get-tuple-element.62), channel_id=1, source_target_pairs={{4,0},{8,4},{12,8},{16,12},{20,16},{24,20},{28,24},{0,28},{5,1},{9... | collective-permute-start | bytes 393224 | tf_op jit(solution)/shard_map/project/ppermute | solution.py:17
  24.6 12.1 %collective-permute-start.5 = (bf16[64,1024]{1,0:T(8,128)(2,1)S(1)}, bf16[64,1024]{1,0:T(8,128)(2,1)S(1)}, u32[]{:S(2)}, u32[]{:S(2)}) collective-permute-start(bf16[64,1024]{1,0:T(8,128)(2,1)S(1)} %get-tuple-element.64), channel_id=1, source_target_pairs={{12,0},{16,4},{20,8},{24,12},{28,16},{0,20},{4,24},{8,28},{13,1},{... | collective-permute-start | bytes 393224 | tf_op jit(solution)/shard_map/project/ppermute | solution.py:17
  27.7 9.0 %collective-permute-start.6 = (bf16[64,1024]{1,0:T(8,128)(2,1)S(1)}, bf16[64,1024]{1,0:T(8,128)(2,1)S(1)}, u32[]{:S(2)}, u32[]{:S(2)}) collective-permute-start(bf16[64,1024]{1,0:T(8,128)(2,1)S(1)} %get-tuple-element.65), channel_id=1, source_target_pairs={{24,0},{28,4},{0,8},{4,12},{8,16},{12,20},{16,24},{20,28},{25,1},{... | collective-permute-start | bytes 393224 | tf_op jit(solution)/shard_map/project/ppermute | solution.py:17
  36.9 5.0 %collective-permute-start.7 = (bf16[64,1024]{1,0:T(8,128)(2,1)S(1)}, bf16[64,1024]{1,0:T(8,128)(2,1)S(1)}, u32[]{:S(2)}, u32[]{:S(2)}) collective-permute-start(bf16[64,1024]{1,0:T(8,128)(2,1)S(1)} %get-tuple-element.61), channel_id=1, source_target_pairs={{1,0},{2,1},{3,2},{0,3},{5,4},{6,5},{7,6},{4,7},{9,8},{10,9},{11,1... | collective-permute-start | bytes 393224 | tf_op jit(solution)/shard_map/project/ppermute | solution.py:17
  37.5 6.1 %collective-permute-start.8 = (bf16[64,1024]{1,0:T(8,128)(2,1)S(1)}, bf16[64,1024]{1,0:T(8,128)(2,1)S(1)}, u32[]{:S(2)}, u32[]{:S(2)}) collective-permute-start(bf16[64,1024]{1,0:T(8,128)(2,1)S(1)} %get-tuple-element.61), channel_id=1, source_target_pairs={{2,0},{3,1},{0,2},{1,3},{6,4},{7,5},{4,6},{5,7},{10,8},{11,9},{8,1... | collective-permute-start | bytes 393224 | tf_op jit(solution)/shard_map/project/ppermute | solution.py:17
  41.4 5.0 %collective-permute-start.9 = (bf16[64,1024]{1,0:T(8,128)(2,1)S(1)}, bf16[64,1024]{1,0:T(8,128)(2,1)S(1)}, u32[]{:S(2)}, u32[]{:S(2)}) collective-permute-start(bf16[64,1024]{1,0:T(8,128)(2,1)S(1)} %get-tuple-element.61), channel_id=1, source_target_pairs={{3,0},{0,1},{1,2},{2,3},{7,4},{4,5},{5,6},{6,7},{11,8},{8,9},{9,10... | collective-permute-start | bytes 393224 | tf_op jit(solution)/shard_map/project/ppermute | solution.py:17
  49.1 7.6 %collective-permute-start.10 = (bf16[1,256,512]{2,1,0:T(8,128)(2,1)S(1)}, bf16[1,256,512]{2,1,0:T(8,128)(2,1)S(1)}, u32[]{:S(2)}, u32[]{:S(2)}) collective-permute-start(bf16[1,256,512]{2,1,0:T(8,128)(2,1)S(1)} %get-tuple-element.37), channel_id=1, source_target_pairs={{32,0},{0,32},{33,1},{1,33},{34,2},{2,34},{35,3},{3,35},{36,4},{4,... | collective-permute-start | bytes 786440 | tf_op jit(solution)/shard_map/sketch/ppermute | solution.py:17
  56.8 6.4 %collective-permute-start.11 = (bf16[3,256,512]{2,1,0:T(8,128)(2,1)S(1)}, bf16[3,256,512]{2,1,0:T(8,128)(2,1)S(1)}, u32[]{:S(2)}, u32[]{:S(2)}) collective-permute-start(bf16[3,256,512]{2,1,0:T(8,128)(2,1)S(1)} %cross.4), channel_id=1, source_target_pairs={{32,0},{0,32},{33,1},{1,33},{34,2},{2,34},{35,3},{3,35},{36,4},{4,... | collective-permute-start | bytes 2359304 | tf_op jit(solution)/shard_map/sketch/ppermute | solution.py:17
  57.1 9.7 %collective-permute-start.12 = (bf16[256,512]{1,0:T(8,128)(2,1)S(1)}, bf16[256,512]{1,0:T(8,128)(2,1)S(1)}, u32[]{:S(2)}, u32[]{:S(2)}) collective-permute-start(bf16[256,512]{1,0:T(8,128)(2,1)S(1)} %combine.2), channel_id=1, source_target_pairs={{128,0},{192,64},{0,128},{64,192},{129,1},{193,65},{1,129},{65,193... | collective-permute-start | bytes 786440 | tf_op jit(solution)/shard_map/sketch/ppermute | solution.py:17
  64.1 8.6 %collective-permute-start.13 = (bf16[256,512]{1,0:T(8,128)(2,1)}, bf16[256,512]{1,0:T(8,128)(2,1)S(1)}, u32[]{:S(2)}, u32[]{:S(2)}) collective-permute-start(bf16[256,512]{1,0:T(8,128)(2,1)} %get-tuple-element.41), channel_id=1, source_target_pairs={{192,0},{0,64},{64,128},{128,192},{193,1},{1,65},{65,129},{129,193... | collective-permute-start | bytes 786440 | tf_op jit(solution)/shard_map/sketch/ppermute | solution.py:17
  64.5 8.2 %collective-permute-start.14 = (bf16[256,512]{1,0:T(8,128)(2,1)}, bf16[256,512]{1,0:T(8,128)(2,1)S(1)}, u32[]{:S(2)}, u32[]{:S(2)}) collective-permute-start(bf16[256,512]{1,0:T(8,128)(2,1)} %get-tuple-element.42), channel_id=1, source_target_pairs={{64,0},{128,64},{192,128},{0,192},{65,1},{129,65},{193,129},{1,193... | collective-permute-start | bytes 786440 | tf_op jit(solution)/shard_map/sketch/ppermute | solution.py:17
  78.5 9.1 %collective-permute-start.19 = (bf16[512,256]{1,0:T(8,128)(2,1)S(1)}, bf16[512,256]{1,0:T(8,128)(2,1)S(1)}, u32[]{:S(2)}, u32[]{:S(2)}) collective-permute-start(bf16[512,256]{1,0:T(8,128)(2,1)S(1)} %get-tuple-element.47), channel_id=1, source_target_pairs={{128,0},{192,64},{0,128},{64,192},{129,1},{193,65},{1,129},{65,193... | collective-permute-start | bytes 786440 | tf_op jit(solution)/shard_map/gram/ppermute | solution.py:17
  80.3 4.6 %collective-permute-start.16 = (f32[32,256]{1,0:T(8,128)S(1)}, f32[32,256]{1,0:T(8,128)S(1)}, u32[]{:S(2)}, u32[]{:S(2)}) collective-permute-start(f32[32,256]{1,0:T(8,128)S(1)} %get-tuple-element.66), channel_id=1, source_target_pairs={{2,0},{34,32},{3,1},{35,33},{0,2},{32,34},{1,3},{33,35},{6,4},{38,... | collective-permute-start | bytes 98312 | tf_op jit(solution)/shard_map/gram/ppermute | solution.py:24
  81.1 5.4 %collective-permute-start.17 = (f32[32,256]{1,0:T(8,128)S(1)}, f32[32,256]{1,0:T(8,128)S(1)}, u32[]{:S(2)}, u32[]{:S(2)}) collective-permute-start(f32[32,256]{1,0:T(8,128)S(1)} %get-tuple-element.68), channel_id=1, source_target_pairs={{35,0},{3,32},{32,1},{0,33},{33,2},{1,34},{34,3},{2,35},{39,4},{7,... | collective-permute-start | bytes 98312 | tf_op jit(solution)/shard_map/gram/ppermute | solution.py:24
  87.6 7.1 %collective-permute-start.20 = (f32[32,256]{1,0:T(8,128)S(1)}, f32[32,256]{1,0:T(8,128)S(1)}, u32[]{:S(2)}, u32[]{:S(2)}) collective-permute-start(f32[32,256]{1,0:T(8,128)S(1)} %add_add_fusion.2), channel_id=1, source_target_pairs={{36,0},{4,32},{32,4},{0,36},{44,8},{12,40},{40,12},{8,44},{52,16},... | collective-permute-start | bytes 98312 | tf_op jit(solution)/shard_map/gram/ppermute | solution.py:24
  87.6 7.1 %collective-permute-start.21 = (f32[32,256]{1,0:T(8,128)S(1)}, f32[32,256]{1,0:T(8,128)S(1)}, u32[]{:S(2)}, u32[]{:S(2)}) collective-permute-start(f32[32,256]{1,0:T(8,128)S(1)} %add_add_fusion.2), channel_id=1, source_target_pairs={{24,0},{56,32},{28,4},{60,36},{16,8},{48,40},{20,12},{52,44},{8,16... | collective-permute-start | bytes 98312 | tf_op jit(solution)/shard_map/gram/ppermute | solution.py:24
  92.0 7.6 %collective-permute-start.24 = (bf16[512,256]{1,0:T(8,128)(2,1)S(1)}, bf16[512,256]{1,0:T(8,128)(2,1)S(1)}, u32[]{:S(2)}, u32[]{:S(2)}) collective-permute-start(bf16[512,256]{1,0:T(8,128)(2,1)S(1)} %get-tuple-element.47), channel_id=1, source_target_pairs={{64,0},{128,64},{192,128},{0,192},{65,1},{129,65},{193,129},{1,193... | collective-permute-start | bytes 786440 | tf_op jit(solution)/shard_map/gram/ppermute | solution.py:17
  94.7 7.8 %collective-permute-start.25 = (bf16[512,256]{1,0:T(8,128)(2,1)S(1)}, bf16[512,256]{1,0:T(8,128)(2,1)S(1)}, u32[]{:S(2)}, u32[]{:S(2)}) collective-permute-start(bf16[512,256]{1,0:T(8,128)(2,1)S(1)} %get-tuple-element.47), channel_id=1, source_target_pairs={{192,0},{0,64},{64,128},{128,192},{193,1},{1,65},{65,129},{129,193... | collective-permute-start | bytes 786440 | tf_op jit(solution)/shard_map/gram/ppermute | solution.py:17
  111.6 5.4 %collective-permute-start.31 = (f32[32,256]{1,0:T(8,128)S(1)}, f32[32,256]{1,0:T(8,128)S(1)}, u32[]{:S(2)}, u32[]{:S(2)}) collective-permute-start(f32[32,256]{1,0:T(8,128)S(1)} %get-tuple-element.59), channel_id=1, source_target_pairs={{35,0},{3,32},{32,1},{0,33},{33,2},{1,34},{34,3},{2,35},{39,4},{7,... | collective-permute-start | bytes 98312 | tf_op jit(solution)/shard_map/gram/ppermute | solution.py:24
  118.4 10.7 %collective-permute-start.33 = (bf16[2048,256]{1,0:T(8,128)(2,1)S(1)}, bf16[2048,256]{1,0:T(8,128)(2,1)S(1)}, u32[]{:S(2)}, u32[]{:S(2)}) collective-permute-start(bf16[2048,256]{1,0:T(8,128)(2,1)S(1)} %constant_dynamic-update-slice_fusion.2), channel_id=1, source_target_pairs={{32,0},{0,32},{33,1},{1,33},{34,2},{2,34},{35,3},{3,35},{36,4},{4,... | collective-permute-start | bytes 3145736 | tf_op jit(solution)/shard_map/gram/ppermute | solution.py:17
  (13 other events, 71.8 us)
